TPU v7x, 32 devices: a whole 2x2x4 slice. The times are simulated.
32 devices in a mesh: dp: 4 (over z), expert: 8 (over y, x, core).
Axes of the slice: x: 2, y: 2, z: 4, core: 2. Of those that a mesh axis runs over, the one named last changes fastest.
Arguments:
- tokens_x: bfloat16 [1024, 4096], P('dp', 'expert'), may hold values from -6 to 6
- in_proj: bfloat16 [4096, 1024], P('expert'), may hold values from -0.09375 to 0.09375
- up_weight: bfloat16 [16, 1024, 768], P('expert'), may hold values from -0.1875 to 0.1875
- down_weight: bfloat16 [16, 768, 1024], P('expert'), may hold values from -0.21875 to 0.21875
- expert_ids: int32 [1024, 8], P(('dp', 'expert')), may hold values from 0 to 15, all different within a row; in each aligned block of 32 rows (0 to 31, 32 to 63, ...) at most 24 rows name the same one
- route_probs: float32 [1024, 8], P(('dp', 'expert')), may hold values from 0.05 to 1
- out_grad: bfloat16 [1024, 1024], P(('dp', 'expert')), may hold values from -6 to 6
Outputs:
- combined: bfloat16 [1024, 1024], P(('dp', 'expert'))
- input_grad: bfloat16 [1024, 4096], P('dp', 'expert')
- proj_grad: float32 [4096, 1024], P('expert')
Inputs may be any that keep to these rules, and one draw needn't show every extreme that they name: `expert_ids`: each row names 8 different experts. Within the rows of one device (aligned blocks of 32 rows) no expert is named more than 24 times, a bound that some block reaches.
All inputs are finite; a program needn't handle non-finite values.
Results may differ from a plain program's by a relative error of at most 0.019.
Values may be sent and summed in bfloat16 or wider, within the bound.
No kernel may reach another device: no remote copies, remote signals or barrier semaphores. Data moves between devices by JAX's collectives and lax.ppermute only.
A program may use at most 64 MiB of HBM per device.

v0:
```python
import jax
import jax.numpy as jnp
from jax import lax
from jax.sharding import PartitionSpec as P


def expert_preact(row_slots, up_local):
    return jnp.einsum("secl,elh->sech", row_slots, up_local, preferred_element_type=jnp.float32)


def expert_outputs(preact, down_local):
    positive = jnp.maximum(preact, 0.0)
    act_slots = (positive * positive).astype(jnp.bfloat16)
    return jnp.einsum(
        "sech,ehl->secl", act_slots, down_local, preferred_element_type=jnp.float32
    ).astype(jnp.bfloat16)


def expert_grads(preact, grad_slots, up_local, down_local):
    positive = jnp.maximum(preact, 0.0)
    grad_act = jnp.einsum(
        "secl,ehl->sech", grad_slots, down_local, preferred_element_type=jnp.float32
    )
    grad_pre = (grad_act * 2.0 * positive).astype(jnp.bfloat16)
    return jnp.einsum(
        "sech,elh->secl", grad_pre, up_local, preferred_element_type=jnp.float32
    ).astype(jnp.bfloat16)


def per_device(tokens_x, in_proj, up_weight, down_weight, expert_ids, route_probs, out_grad):
    owners = lax.axis_size("expert")
    tok_count = expert_ids.shape[0]
    top_count = expert_ids.shape[1]
    local_experts = up_weight.shape[0]
    all_experts = local_experts * owners
    capacity = max(2, 3 * tok_count * top_count // (2 * all_experts))
    latent_width = in_proj.shape[1]
    x_rows = tokens_x
    latent = lax.psum_scatter(
        jnp.dot(x_rows, in_proj, preferred_element_type=jnp.float32).astype(jnp.bfloat16),
        "expert",
        scatter_dimension=0,
        tiled=True,
    )
    pair_count = tok_count * top_count
    flat_ids = expert_ids.reshape(pair_count)
    expert_table = (flat_ids[:, None] == jnp.arange(all_experts, dtype=jnp.int32)[None, :]).astype(
        jnp.int32
    )
    earlier = jnp.cumsum(expert_table, axis=0) - expert_table
    position = jnp.sum(earlier * expert_table, axis=1)
    slot_index = flat_ids * capacity + position
    slot_count = all_experts * capacity
    placement = (jnp.arange(slot_count, dtype=jnp.int32)[:, None] == slot_index[None, :]).astype(
        jnp.bfloat16
    )
    token_place = jnp.sum(placement.reshape(slot_count, tok_count, top_count), axis=2)
    slot_shape = (owners, local_experts, capacity, latent_width)
    latent_slots = (
        jnp.dot(token_place, latent, preferred_element_type=jnp.float32)
        .astype(jnp.bfloat16)
        .reshape(slot_shape)
    )
    pair_grad = (route_probs[:, :, None] * out_grad.astype(jnp.float32)[:, None, :]).astype(
        jnp.bfloat16
    )
    pair_grad = pair_grad.reshape(pair_count, latent_width)
    grad_slots = (
        jnp.dot(placement, pair_grad, preferred_element_type=jnp.float32)
        .astype(jnp.bfloat16)
        .reshape(slot_shape)
    )
    row_slots = lax.all_to_all(latent_slots, "expert", split_axis=0, concat_axis=0, tiled=True)
    preact = expert_preact(row_slots, up_weight)
    out_slots = lax.all_to_all(
        expert_outputs(preact, down_weight), "expert", split_axis=0, concat_axis=0, tiled=True
    )
    cot_slots = lax.all_to_all(grad_slots, "expert", split_axis=0, concat_axis=0, tiled=True)
    lat_slots = lax.all_to_all(
        expert_grads(preact, cot_slots, up_weight, down_weight),
        "expert",
        split_axis=0,
        concat_axis=0,
        tiled=True,
    )
    out_flat = out_slots.reshape(slot_count, latent_width)
    lat_flat = lat_slots.reshape(slot_count, latent_width)
    pair_out = jnp.einsum("sp,sl->pl", placement, out_flat, preferred_element_type=jnp.float32)
    pair_out = pair_out.reshape(tok_count, top_count, latent_width)
    combined = jnp.sum(route_probs[:, :, None] * pair_out, axis=1).astype(jnp.bfloat16)
    latent_grad = jnp.einsum(
        "st,sl->tl", token_place, lat_flat, preferred_element_type=jnp.float32
    ).astype(jnp.bfloat16)
    grad_rows = lax.all_gather(latent_grad, "expert", axis=0, tiled=True)
    x_rows = tokens_x
    dx_rows = lax.dot_general(
        grad_rows, in_proj, (((1,), (1,)), ((), ())), preferred_element_type=jnp.float32
    )
    input_acc = dx_rows
    weight_acc = lax.dot_general(
        x_rows, grad_rows, (((0,), (0,)), ((), ())), preferred_element_type=jnp.float32
    )
    input_acc, weight_acc = (input_acc, weight_acc)
    input_grad = input_acc.astype(jnp.bfloat16)
    proj_grad = lax.psum(weight_acc, "dp")
    return (combined, input_grad, proj_grad)


def solution(mesh):
    return jax.shard_map(
        per_device,
        mesh=mesh,
        in_specs=(
            P("dp", "expert"),
            P("expert", None),
            P("expert", None, None),
            P("expert", None, None),
            P(("dp", "expert"), None),
            P(("dp", "expert"), None),
            P(("dp", "expert"), None),
        ),
        out_specs=(P(("dp", "expert"), None), P("dp", "expert"), P("expert", None)),
        check_vma=False,
    )
```

profile of v0, /device:TPU:0, one launch (start us, length us, event | category | flops | bytes accessed | tf_op | source)
XLA Modules:
  0.0 214.3 jit_solution(4948683395460895752)
XLA Ops:
  7.2 0.0 copy-start
  7.2 0.0 copy-start.6
  7.2 0.0 copy-start.7
  7.2 0.0 copy-start.5
  7.2 0.0 reduce-scatter.2.cloned.1.call-start
  7.3 2.7 %convolution_convert_fusion.2 = bf16[256,1024]{1,0:T(8,128)(2,1)} fusion(bf16[256,512]{1,0:T(8,128)(2,1)} %param.7, bf16[512,1024]{1,0:T(8,128)(2,1)} %param.8), kind=kOutput, calls=%fused_computation.18 | convolution fusion | flops 268697600 | bytes 1835008 | tf_op jit(solution)/shard_map/dot_general | solution.py:40
  9.9 0.0 reduce-scatter.2.cloned.1.call-update
  10.0 0.0 copy-done.6
  10.0 0.1 copy.47
  10.1 0.1 reshape.87
  10.1 0.1 eq.62
  10.3 0.6 reduce-window.6
  10.8 0.2 slice_reduce_fusion
  11.1 0.1 fusion.56
  11.2 0.1 reduce_sum.33
  11.3 0.2 fusion.51
  11.5 37.1 %reduce-scatter.2.cloned.1.call-done = bf16[32,1024]{1,0:T(8,128)(2,1)} async-done(((bf16[256,1024]{1,0:T(8,128)(2,1)}), bf16[32,1024]{1,0:T(8,128)(2,1)}) %reduce-scatter.2.cloned.1.call-update) | async-done | bytes 65552 | tf_op jit(solution)/shard_map/reduce_scatter | solution.py:39
  48.5 2.1 convolution_convert_fusion
  50.6 4.2 %all-to-all-start = ((bf16[8,2,24,1024]{3,2,1,0:T(8,128)(2,1)}), bf16[8,2,24,1024]{3,2,1,0:T(8,128)(2,1)}, u32[]{:S(2)}, u32[]{:S(2)}) async-start(bf16[8,2,24,1024]{3,2,1,0:T(8,128)(2,1)} %bitcast.92), calls=%async_computation.1 | async-start | bytes 1572864 | tf_op jit(solution)/shard_map/all_to_all | solution.py:73
  54.9 0.0 copy-done.7
  54.9 0.1 copy.46
  54.9 0.1 mul.67
  55.0 0.0 copy-done.5
  55.1 1.3 convolution_convert_fusion.1
  56.4 11.0 %all-to-all-done = bf16[8,2,24,1024]{3,2,1,0:T(8,128)(2,1)} async-done(((bf16[8,2,24,1024]{3,2,1,0:T(8,128)(2,1)}), bf16[8,2,24,1024]{3,2,1,0:T(8,128)(2,1)}, u32[]{:S(2)}, u32[]{:S(2)}) %all-to-all-start) | async-done | bytes 786464 | tf_op jit(solution)/shard_map/all_to_all | solution.py:73
  67.5 4.2 %all-to-all-start.2 = ((bf16[8,2,24,1024]{3,2,1,0:T(8,128)(2,1)}), bf16[8,2,24,1024]{3,2,1,0:T(8,128)(2,1)}, u32[]{:S(2)}, u32[]{:S(2)}) async-start(bf16[8,2,24,1024]{3,2,1,0:T(8,128)(2,1)} %bitcast.91), calls=%async_computation.3 | async-start | bytes 1572864 | tf_op jit(solution)/shard_map/all_to_all | solution.py:78
  71.7 0.0 all-reduce.2.cloned.1.call-start
  71.7 3.9 %fusion.14 = f32[2,8,24,768]{3,2,1,0:T(8,128)} fusion(bf16[2,1024,768]{2,1,0:T(8,128)(2,1)} %param.9, bf16[8,2,24,1024]{3,2,1,0:T(8,128)(2,1)} %all-to-all-done), kind=kOutput, calls=%fused_computation.11 | convolution fusion | flops 604274688 | bytes 5111808 | tf_op jit(solution)/shard_map/secl,elh->sech/dot_general | solution.py:8
  75.7 8.6 %all-to-all-done.2 = bf16[8,2,24,1024]{3,2,1,0:T(8,128)(2,1)} async-done(((bf16[8,2,24,1024]{3,2,1,0:T(8,128)(2,1)}), bf16[8,2,24,1024]{3,2,1,0:T(8,128)(2,1)}, u32[]{:S(2)}, u32[]{:S(2)}) %all-to-all-start.2) | async-done | bytes 786464 | tf_op jit(solution)/shard_map/all_to_all | solution.py:78
  84.3 0.0 copy-done
  84.3 5.6 %fusion.26 = bf16[8,2,24,1024]{3,2,0,1:T(8,128)(2,1)} fusion(bf16[2,1024,768]{2,1,0:T(8,128)(2,1)} %param.9, f32[2,8,24,768]{3,2,1,0:T(8,128)} %fusion.14, bf16[2,768,1024]{2,1,0:T(8,128)(2,1)S(1)} %copy-done, bf16[8,2,24,1024]{3,2,1,0:T(8,128)(2,1)} %all-to-all-done.2), kind=kOutput, calls=%fused_computation.19 | convolution fusion | flops 1209237504 | bytes 9043968 | tf_op jit(solution)/shard_map/sech,elh->secl/dot_general | solution.py:25
  89.9 0.0 copy-start.4
  89.9 1.2 copy.55
  91.1 15.0 %all_to_all.20 = bf16[8,2,24,1024]{3,2,1,0:T(8,128)(2,1)S(1)} all-to-all(bf16[8,2,24,1024]{3,2,1,0:T(8,128)(2,1)S(1)} %copy.55), channel_id=1, replica_groups=mesh['dp'=4,'expert'=8] {'expert'}, dimensions={0} | all-to-all | bytes 1572864 | tf_op jit(solution)/shard_map/all_to_all | solution.py:79
  106.1 0.2 convolution_convert_fusion.4
  106.3 8.9 %all_gather.3 = bf16[256,1024]{1,0:T(8,128)(2,1)S(1)} all-gather(bf16[32,1024]{1,0:T(8,128)(2,1)S(1)} %convolution_convert_fusion.4), channel_id=1, replica_groups=mesh['dp'=4,'expert'=8] {'expert'}, dimensions={0}, use_global_device_ids=true | all-gather | bytes 589824 | tf_op jit(solution)/shard_map/all_gather | solution.py:94
  115.2 0.0 copy-start.1
  115.2 0.8 copy-done.1
  116.0 0.0 copy-done.4
  116.0 1.8 convolution_bitcast_fusion
  117.8 0.0 all-reduce.2.cloned.1.call-update
  117.9 2.1 fusion.29
  119.9 0.0 copy-start.2
  119.9 0.0 copy-start.3
  119.9 0.1 copy.52
  120.0 15.3 %all_to_all.21 = bf16[8,2,24,1024]{3,2,1,0:T(8,128)(2,1)S(1)} all-to-all(bf16[8,2,24,1024]{3,2,1,0:T(8,128)(2,1)S(1)} %copy.52), channel_id=1, replica_groups=mesh['dp'=4,'expert'=8] {'expert'}, dimensions={0} | all-to-all | bytes 1572864 | tf_op jit(solution)/shard_map/all_to_all | solution.py:75
  135.3 1.2 fusion.35
  136.5 0.0 copy-done.2
  136.5 0.0 copy-done.3
  136.5 1.2 convolution_convert_fusion.3
  137.7 66.9 %all-reduce.2.cloned.1.call-done = f32[512,1024]{0,1:T(8,128)} async-done(((f32[512,1024]{0,1:T(8,128)}), f32[512,1024]{0,1:T(8,128)}) %all-reduce.2.cloned.1.call-update) | async-done | bytes 2097168 | tf_op jit(solution)/shard_map/psum | solution.py:105
  204.6 2.9 %copy.56 = f32[512,1024]{1,0:T(8,128)} copy(f32[512,1024]{0,1:T(8,128)} %all-reduce.2.cloned.1.call-done) | data formatting | bytes 4194304
  (6 shorter events, 0.1 us)
Async XLA Ops:
  7.2 77.1 %copy-start = (bf16[2,768,1024]{2,1,0:T(8,128)(2,1)S(1)}, bf16[2,768,1024]{2,1,0:T(8,128)(2,1)}, u32[]{:S(2)}) copy-start(bf16[2,768,1024]{2,1,0:T(8,128)(2,1)} %param.10) | copy-start | bytes 9437188
  7.2 2.8 %copy-start.6 = (s32[32,8]{0,1:T(8,128)S(1)}, s32[32,8]{0,1:T(8,128)}, u32[]{:S(2)}) copy-start(s32[32,8]{0,1:T(8,128)} %param.11) | copy-start | bytes 3076
  7.2 47.7 %copy-start.7 = (f32[32,8]{0,1:T(8,128)S(1)}, f32[32,8]{0,1:T(8,128)}, u32[]{:S(2)}) copy-start(f32[32,8]{0,1:T(8,128)} %param.12) | copy-start | bytes 3076
  7.2 47.8 %copy-start.5 = (bf16[32,1024]{1,0:T(8,128)(2,1)S(1)}, bf16[32,1024]{1,0:T(8,128)(2,1)}, u32[]{:S(2)}) copy-start(bf16[32,1024]{1,0:T(8,128)(2,1)} %param.13) | copy-start | bytes 196612
  7.2 41.3 %reduce-scatter.2.cloned.1.call-start = ((), (), s32[]{:S(2)}) async-start(), calls=%async_computation.5 | async-start | bytes 589824 | tf_op jit(solution)/shard_map/reduce_scatter | solution.py:39
  50.6 16.8 %all-to-all-start = ((bf16[8,2,24,1024]{3,2,1,0:T(8,128)(2,1)}), bf16[8,2,24,1024]{3,2,1,0:T(8,128)(2,1)}, u32[]{:S(2)}, u32[]{:S(2)}) async-start(bf16[8,2,24,1024]{3,2,1,0:T(8,128)(2,1)} %bitcast.92), calls=%async_computation.1 | async-start | bytes 1572864 | tf_op jit(solution)/shard_map/all_to_all | solution.py:73
  67.5 16.8 %all-to-all-start.2 = ((bf16[8,2,24,1024]{3,2,1,0:T(8,128)(2,1)}), bf16[8,2,24,1024]{3,2,1,0:T(8,128)(2,1)}, u32[]{:S(2)}, u32[]{:S(2)}) async-start(bf16[8,2,24,1024]{3,2,1,0:T(8,128)(2,1)} %bitcast.91), calls=%async_computation.3 | async-start | bytes 1572864 | tf_op jit(solution)/shard_map/all_to_all | solution.py:78
  71.7 132.9 %all-reduce.2.cloned.1.call-start = ((), (), s32[]{:S(2)}) async-start(), calls=%async_computation.6 | async-start | bytes 4194304 | tf_op jit(solution)/shard_map/psum | solution.py:105
  89.9 26.1 %copy-start.4 = (bf16[256,512]{1,0:T(8,128)(2,1)S(1)}, bf16[256,512]{1,0:T(8,128)(2,1)}, u32[]{:S(2)}) copy-start(bf16[256,512]{1,0:T(8,128)(2,1)} %param.7) | copy-start | bytes 786436
  115.2 0.8 copy-start.1
  119.9 16.6 %copy-start.2 = (bf16[256,1024]{1,0:T(8,128)(2,1)S(1)}, bf16[256,1024]{1,0:T(8,128)(2,1)}, u32[]{:S(2)}) copy-start(bf16[256,1024]{1,0:T(8,128)(2,1)} %copy-done.1) | copy-start | bytes 1572868
  119.9 16.6 %copy-start.3 = (bf16[512,1024]{1,0:T(8,128)(2,1)S(1)}, bf16[512,1024]{1,0:T(8,128)(2,1)}, u32[]{:S(2)}) copy-start(bf16[512,1024]{1,0:T(8,128)(2,1)} %param.8) | copy-start | bytes 3145732
Sparse Core Ops, SparseCore 0:
  11.7 36.7 reduce-scatter.1
  118.0 86.5 all-reduce.1
where the time goes:
time: 215 us; the launch traced here: 214 us
  waiting for transfers between devices  124 us (58%)
  blocking collectives  39.1 us (18%)
  matrix products  22.1 us (10%)
  between operations  14.2 us (7%)
  starting transfers between devices  8.51 us (4%)
  local copies, waits for them, and re-layouts  5.68 us (3%)
    psum x1, waiting for transfers between devices, per_device(): proj_grad = lax.psum(weight_acc, 'dp')  66.9 us
    reduce_scatter x1, waiting for transfers between devices, per_device(): lax.psum_scatter(jnp.dot(x_rows, in_proj, preferred_element_type=jnp.floa...  37.1 us
    all_to_all x1, blocking collectives, per_device(): lax.all_to_all(expert_outputs(preact, down_weight), 'expert', split_axis=...  15.3 us
    all_to_all x1, blocking collectives, per_device(): lax.all_to_all(expert_grads(preact, cot_slots, up_weight, down_weight), '...  15 us
    all_to_all x1, waiting for transfers between devices, per_device(): lax.all_to_all(latent_slots, 'expert', split_axis=0, concat_axis=0, tiled...  11 us
    all_gather x1, blocking collectives, per_device(): grad_rows = lax.all_gather(latent_grad, 'expert', axis=0, tiled=True)  8.91 us
    all_to_all x1, waiting for transfers between devices, per_device(): lax.all_to_all(grad_slots, 'expert', split_axis=0, concat_axis=0, tiled=T...  8.63 us
    dot_general x1, matrix products, expert_grads(): jnp.einsum('sech,elh->secl', grad_pre, up_local, preferred_element_type=j...  5.57 us
  transfers between devices with their start and end apart: 4, of which 4 were waited for; matrix products, arithmetic and copies ran while one was open for 5% of the time, Pallas kernels for 0%

commit v1 on v0

v1 whole, which is shorter than its diff:
```python
import jax
import jax.numpy as jnp
from jax import lax
from jax.sharding import PartitionSpec as P


def xor_permute(value, axis, mask):
    size = lax.axis_size(axis)
    return lax.ppermute(value, axis, [(i, i ^ mask) for i in range(size)])


def add_bf16(first, second):
    return (first.astype(jnp.float32) + second.astype(jnp.float32)).astype(jnp.bfloat16)


def dot32(first, second):
    return jnp.dot(first, second, preferred_element_type=jnp.float32)


def dot32_t(first, second):
    return lax.dot_general(
        first, second, (((1,), (1,)), ((), ())), preferred_element_type=jnp.float32
    )


def from_xor_order(pieces, me):
    count = len(pieces)
    rows = pieces[0].shape[0]
    whole = jnp.zeros((count * rows,) + pieces[0].shape[1:], pieces[0].dtype)
    for offset, piece in enumerate(pieces):
        whole = lax.dynamic_update_slice_in_dim(whole, piece, (me ^ offset) * rows, axis=0)
    return whole


def sum_and_gather(summed, gathered, bits):
    for bit in bits:
        sum_rows = summed.shape[0]
        got = xor_permute(jnp.concatenate([summed, gathered], axis=0), "expert", bit)
        summed = add_bf16(summed, got[:sum_rows])
        gathered = jnp.concatenate([gathered, got[sum_rows:]], axis=0)
    return summed, gathered


def order_of(bits):
    masks = [0]
    for bit in bits:
        masks = masks + [mask ^ bit for mask in masks]
    return masks


def scatter_sum(partial, chip, chips):
    rows = partial.shape[0] // chips
    pieces = [
        lax.dynamic_slice_in_dim(partial, (chip ^ k) * rows, rows, axis=0) for k in range(chips)
    ]
    got = [xor_permute(pieces[k], "expert", 2 * k) for k in range(1, chips)]
    total = pieces[0].astype(jnp.float32)
    for piece in got:
        total = total + piece.astype(jnp.float32)
    return total.astype(jnp.bfloat16)


def per_device(tokens_x, in_proj, up_weight, down_weight, expert_ids, route_probs, out_grad):
    owners = lax.axis_size("expert")
    groups = lax.axis_size("dp")
    chips = owners // 2
    me = lax.axis_index("expert")
    core = me % 2
    chip = me // 2
    tok, top = expert_ids.shape
    local_experts = up_weight.shape[0]
    all_experts = local_experts * owners
    features, width = in_proj.shape
    half = chips * tok
    bits = [1 << b for b in range(1, owners.bit_length() - 1)]

    chosen = expert_ids[None, :, :] == jnp.arange(all_experts, dtype=jnp.int32)[:, None, None]
    routing = jnp.sum(jnp.where(chosen, route_probs[None, :, :], 0.0), axis=2).astype(jnp.bfloat16)
    routing = lax.dynamic_update_slice(
        jnp.zeros((all_experts, width), jnp.bfloat16), routing, (0, chip * tok)
    )

    x_cores = tokens_x.reshape(chips, 2, tok, features)
    x_other = lax.dynamic_index_in_dim(x_cores, 1 - core, 1, False).reshape(half, features)
    x_mine = lax.dynamic_index_in_dim(x_cores, core, 1, False).reshape(half, features)
    got = xor_permute(dot32(x_other, in_proj).astype(jnp.bfloat16), "expert", 1)
    summed = add_bf16(dot32(x_mine, in_proj).astype(jnp.bfloat16), got)
    first = jnp.concatenate([summed[: half // 2], routing], axis=0)
    second = summed[half // 2 :]
    first, first_cot = sum_and_gather(first, out_grad[: tok // 2], bits)
    second, second_cot = sum_and_gather(second, out_grad[tok // 2 :], bits[::-1])
    cot = jnp.zeros((chips, 2, tok // 2, width), jnp.bfloat16)
    for position, pieces, order in ((0, first_cot, order_of(bits)), (1, second_cot, order_of(bits[::-1]))):
        pieces = pieces.reshape(chips, 1, 1, tok // 2, width)
        for place, mask in enumerate(order):
            cot = lax.dynamic_update_slice(
                cot, pieces[place], (chip ^ (mask // 2), position, 0, 0)
            )
    mine = jnp.concatenate([first[: half // 2], second, cot.reshape(half, width), first[half // 2 :]], axis=0)
    other = xor_permute(mine, "expert", 1)
    latent = jnp.concatenate([mine[:half], other[:half]], axis=0)
    cot = jnp.concatenate([mine[half : 2 * half], other[half : 2 * half]], axis=0)
    probs = jnp.concatenate([mine[2 * half :, :half], other[2 * half :, :half]], axis=1)
    probs = lax.dynamic_slice_in_dim(probs, me * local_experts, local_experts, axis=0)
    probs = probs.astype(jnp.float32)

    acts, grads = [], []
    for expert in range(local_experts):
        positive = jnp.maximum(dot32(latent, up_weight[expert]), 0.0)
        prob = probs[expert][:, None]
        grad_act = dot32_t(cot, down_weight[expert])
        acts.append((positive * positive * prob).astype(jnp.bfloat16))
        grads.append((grad_act * (2.0 * positive * prob)).astype(jnp.bfloat16))
    lat_part = sum(dot32_t(grads[i], up_weight[i]) for i in range(local_experts)).astype(jnp.bfloat16)
    got = xor_permute(lat_part[half:], "expert", 1)
    latent_grad = scatter_sum(add_bf16(lat_part[:half], got), chip, chips)
    out_part = sum(dot32(acts[i], down_weight[i]) for i in range(local_experts)).astype(jnp.bfloat16)
    got = xor_permute(out_part[half:], "expert", 1)
    combined = scatter_sum(add_bf16(out_part[:half], got), chip, chips)

    gather_groups = groups & (groups - 1) == 0 and groups * owners * tok * width <= 1 << 22
    held = [latent_grad]
    x_held = [tokens_x]
    if gather_groups:
        held += [xor_permute(latent_grad, "dp", m) for m in range(1, groups)]
        x_held += [xor_permute(tokens_x, "dp", m) for m in range(1, groups)]
    count = len(held)
    own = jnp.concatenate(held, axis=0)
    pieces = [own] + [xor_permute(own, "expert", 2 * k) for k in range(1, chips)]
    mine = from_xor_order(pieces, chip).reshape(chips, count, tok, width)
    other = xor_permute(mine, "expert", 1)
    low = jnp.where(core == 0, mine, other)
    high = jnp.where(core == 0, other, mine)
    rows = jnp.stack([low, high], axis=1)
    rows = jnp.transpose(rows, (2, 0, 1, 3, 4)).reshape(count, owners * tok, width)
    input_grad = dot32_t(rows[0], in_proj).astype(jnp.bfloat16)
    proj_grad = lax.dot_general(
        jnp.concatenate(x_held, axis=0),
        rows.reshape(count * owners * tok, width),
        (((0,), (0,)), ((), ())),
        preferred_element_type=jnp.float32,
    )
    if not gather_groups:
        proj_grad = lax.psum(proj_grad, "dp")
    return (combined, input_grad, proj_grad)


def solution(mesh):
    return jax.shard_map(
        per_device,
        mesh=mesh,
        in_specs=(
            P("dp", "expert"),
            P("expert", None),
            P("expert", None, None),
            P("expert", None, None),
            P(("dp", "expert"), None),
            P(("dp", "expert"), None),
            P(("dp", "expert"), None),
        ),
        out_specs=(P(("dp", "expert"), None), P("dp", "expert"), P("expert", None)),
        check_vma=False,
    )
```

time: 215 us -> 103 us (0.48)
  waiting for transfers between devices: 124 us -> 48.2 us
  blocking collectives: 39.1 us -> 0 us
  starting transfers between devices: 8.51 us -> 27.1 us
  between operations: 14.2 us -> 1.19 us
  matrix products: 22.1 us -> 18.6 us
    psum x1 -> x0, waiting for transfers between devices: 66.9 us -> none  [per_device(): proj_grad = lax.psum(weight_acc, 'dp')]
    ppermute x0 -> x24, waiting for transfers between devices: none -> 48.2 us  [xor_permute(): return lax.ppermute(value, axis, [(i, i ^ mask) for i in range(size)])]
    reduce_scatter x1 -> x0, waiting for transfers between devices: 37.1 us -> none  [per_device(): lax.psum_scatter(jnp.dot(x_rows, in_proj, preferred_element_type=jnp.floa...]
    all_to_all x2 -> x0, blocking collectives: 30.2 us -> none  [the longest x1 15.3 us: per_device(): lax.all_to_all(expert_outputs(preact, down_weight), 'expert', split_axis=...]
    ppermute x0 -> x24, starting transfers between devices: none -> 27.1 us  [xor_permute(): return lax.ppermute(value, axis, [(i, i ^ mask) for i in range(size)])]
    all_to_all x2 -> x0, waiting for transfers between devices: 19.7 us -> none  [the longest x1 11 us: per_device(): lax.all_to_all(latent_slots, 'expert', split_axis=0, concat_axis=0, tiled...]
    all_gather x1 -> x0, blocking collectives: 8.91 us -> none  [per_device(): grad_rows = lax.all_gather(latent_grad, 'expert', axis=0, tiled=True)]
    all_to_all x2 -> x0, starting transfers between devices: 8.43 us -> none  [the longest x1 4.21 us: per_device(): lax.all_to_all(grad_slots, 'expert', split_axis=0, concat_axis=0, tiled=T...]
  transfers between devices with their start and end apart: 4 -> 24, of which waited for: 4 -> 19; matrix products, arithmetic and copies ran while one was open for 5% -> 7% of each run, Pallas kernels for 0% -> 0%
where the time goes in v1:
time: 103 us; the launch traced here: 102 us
  waiting for transfers between devices  48.2 us (47%)
  starting transfers between devices  27.1 us (26%)
  matrix products  18.6 us (18%)
  local copies, waits for them, and re-layouts  4.77 us (5%)
  other arithmetic  2.38 us (2%)
  between operations  1.19 us (1%)
    ppermute x24, waiting for transfers between devices, xor_permute(): return lax.ppermute(value, axis, [(i, i ^ mask) for i in range(size)])  48.2 us
    ppermute x24, starting transfers between devices, xor_permute(): return lax.ppermute(value, axis, [(i, i ^ mask) for i in range(size)])  27.1 us
    dot_general x3, matrix products, dot32_t(): lax.dot_general(first, second, (((1,), (1,)), ((), ())), preferred_elemen...  8.96 us
    dot_general x6, matrix products, dot32(): return jnp.dot(first, second, preferred_element_type=jnp.float32)  5.98 us
    dot_general x1, matrix products, per_device(): lax.dot_general(jnp.concatenate(x_held, axis=0), rows.reshape(count * own...  3.62 us
  transfers between devices with their start and end apart: 24, of which 19 were waited for; matrix products, arithmetic and copies ran while one was open for 7% of the time, Pallas kernels for 0%

profile of v1, /device:TPU:0, one launch (start us, length us, event | category | flops | bytes accessed | tf_op | source)
XLA Modules:
  0.0 102.2 jit_solution(10660345319501921214)
XLA Ops:
  0.7 1.1 %constant_dynamic-slice_fusion.6 = (bf16[4,1,32,512]{3,2,1,0:T(8,128)(2,1)S(1)}, bf16[4,1,32,512]{3,2,1,0:T(8,128)(2,1)S(1)}) fusion(bf16[4,2,32,512]{3,2,1,0:T(8,128)(2,1)} %bitcast, s32[]{:T(128)S(6)} %select_n.86, s32[]{:T(128)S(6)} %select_n.85), kind=kLoop, calls=%fused_computation.100 | loop fusion | bytes 524296 | tf_op jit(solution)/shard_map/jit(dynamic_index_in_dim)/dynamic_slice | solution.py:84
  1.8 0.2 copy-done
  2.0 0.3 convolution_convert_fusion.1
  2.3 0.5 collective-permute-start
  2.9 1.1 %collective-permute-done = bf16[128,1024]{1,0:T(8,128)(2,1)S(1)} collective-permute-done((bf16[128,1024]{1,0:T(8,128)(2,1)S(1)}, bf16[128,1024]{1,0:T(8,128)(2,1)S(1)}, u32[]{:S(2)}, u32[]{:S(2)}) %collective-permute-start) | collective-permute-done | bytes 262176 | tf_op jit(solution)/shard_map/ppermute | solution.py:9
  4.0 0.3 add_convert_fusion.2
  4.4 3.0 %collective-permute-start.3 = (bf16[80,1024]{1,0:T(8,128)(2,1)S(1)}, bf16[80,1024]{1,0:T(8,128)(2,1)S(1)}, u32[]{:S(2)}, u32[]{:S(2)}) collective-permute-start(bf16[80,1024]{1,0:T(8,128)(2,1)S(1)} %pad_maximum_fusion.13), channel_id=1, source_target_pairs={{0,4},{1,5},{2,6},{3,7},{4,0},{5,1},{6,2},{7,3},{8,12},{9,13},{10,... | collective-permute-start | bytes 491528 | tf_op jit(solution)/shard_map/ppermute | solution.py:9
  7.4 0.2 dynamic_update_slice.39
  7.6 1.6 %collective-permute-start.1 = (bf16[96,1024]{1,0:T(8,128)(2,1)S(1)}, bf16[96,1024]{1,0:T(8,128)(2,1)S(1)}, u32[]{:S(2)}, u32[]{:S(2)}) collective-permute-start(bf16[96,1024]{1,0:T(8,128)(2,1)S(1)} %pad_maximum_fusion.11), channel_id=1, source_target_pairs={{0,2},{1,3},{2,0},{3,1},{4,6},{5,7},{6,4},{7,5},{8,10},{9,11},{10,... | collective-permute-start | bytes 589832 | tf_op jit(solution)/shard_map/ppermute | solution.py:9
  9.2 2.6 %collective-permute-done.3 = bf16[80,1024]{1,0:T(8,128)(2,1)S(1)} collective-permute-done((bf16[80,1024]{1,0:T(8,128)(2,1)S(1)}, bf16[80,1024]{1,0:T(8,128)(2,1)S(1)}, u32[]{:S(2)}, u32[]{:S(2)}) %collective-permute-start.3) | collective-permute-done | bytes 163872 | tf_op jit(solution)/shard_map/ppermute | solution.py:9
  11.9 1.8 %collective-permute-start.4 = (bf16[96,1024]{1,0:T(8,128)(2,1)S(1)}, bf16[96,1024]{1,0:T(8,128)(2,1)S(1)}, u32[]{:S(2)}, u32[]{:S(2)}) collective-permute-start(bf16[96,1024]{1,0:T(8,128)(2,1)S(1)} %pad_maximum_fusion.12), channel_id=1, source_target_pairs={{0,2},{1,3},{2,0},{3,1},{4,6},{5,7},{6,4},{7,5},{8,10},{9,11},{10,... | collective-permute-start | bytes 589832 | tf_op jit(solution)/shard_map/ppermute | solution.py:9
  13.7 0.8 collective-permute-done.1
  14.5 0.8 collective-permute-start.2
  15.3 3.2 %collective-permute-done.4 = bf16[96,1024]{1,0:T(8,128)(2,1)S(1)} collective-permute-done((bf16[96,1024]{1,0:T(8,128)(2,1)S(1)}, bf16[96,1024]{1,0:T(8,128)(2,1)S(1)}, u32[]{:S(2)}, u32[]{:S(2)}) %collective-permute-start.4) | collective-permute-done | bytes 196640 | tf_op jit(solution)/shard_map/ppermute | solution.py:9
  18.6 2.4 %collective-permute-done.2 = bf16[112,1024]{1,0:T(8,128)(2,1)S(1)} collective-permute-done((bf16[112,1024]{1,0:T(8,128)(2,1)S(1)}, bf16[112,1024]{1,0:T(8,128)(2,1)S(1)}, u32[]{:S(2)}, u32[]{:S(2)}) %collective-permute-start.2) | collective-permute-done | bytes 229408 | tf_op jit(solution)/shard_map/ppermute | solution.py:9
  21.2 0.1 collective-permute-start.5
  21.3 1.9 %collective-permute-done.5 = bf16[272,1024]{1,0:T(8,128)(2,1)S(1)} collective-permute-done((bf16[272,1024]{1,0:T(8,128)(2,1)S(1)}, bf16[272,1024]{1,0:T(8,128)(2,1)S(1)}, u32[]{:S(2)}, u32[]{:S(2)}) %collective-permute-start.5) | collective-permute-done | bytes 557088 | tf_op jit(solution)/shard_map/ppermute | solution.py:9
  23.2 0.8 fusion.86
  24.1 2.1 %fusion.42 = f32[256,768]{1,0:T(8,128)S(1)} fusion(bf16[2,1024,768]{2,1,0:T(8,128)(2,1)} %param.9, bf16[128,1024]{1,0:T(8,128)(2,1)S(1)} %get-tuple-element.6, bf16[64,1024]{1,0:T(8,128)(2,1)S(1)} %add_convert_fusion.5, bf16[64,1024]{1,0:T(8,128)(2,1)S(1)} %slice.158), kind=kOutput, calls=%fused_computation.31 | convolution fusion | flops 404422656 | bytes 2883584 | tf_op jit(solution)/shard_map/dot_general | solution.py:17
  26.2 0.2 copy-done.9
  26.5 0.6 fusion.36
  27.1 0.7 slice.170
  27.8 4.2 %fusion.4 = f32[256,1024]{1,0:T(8,128)} fusion(bf16[2,1024,768]{2,1,0:T(8,128)(2,1)} %param.9, bf16[2,768,1024]{2,1,0:T(8,128)(2,1)} %param.10, f32[256,768]{1,0:T(8,128)S(1)} %fusion.42, f32[256]{0:T(256)S(1)} %broadcast_multiply_fusion, bf16[128,1024]{1,0:T(8,128)(2,1)S(1)} %copy-done.6, bf16[128,1024]{1,0:T(8,128)(2,1)S(1)} %bitcast.95), kind=kOutput, calls=%fused_computation.5 | convolution fusion | flops 806944768 | bytes 5506048 | tf_op jit(solution)/shard_map/dot_general | solution.py:21
  32.0 3.6 %fusion.33 = bf16[256,1024]{1,0:T(8,128)(2,1)S(1)} fusion(f32[256,1024]{1,0:T(8,128)} %fusion.4, bf16[2,1024,768]{2,1,0:T(8,128)(2,1)} %param.9, bf16[2,768,1024]{2,1,0:T(8,128)(2,1)} %param.10, f32[256,768]{1,0:T(8,128)S(1)} %fusion.36, f32[256]{0:T(256)S(1)} %broadcast_multiply_fusion.1, bf16[128,1024]{1,0:T(8,128)(2,1)} %get-tuple-element.5, ...), kind=kOutput, calls=%fused_computation.28 | convolution fusion | flops 807469056 | bytes 6030336 | tf_op jit(solution)/shard_map/dot_general | solution.py:21
  35.6 0.2 collective-permute-start.10
  35.8 1.4 %collective-permute-done.10 = bf16[128,1024]{1,0:T(8,128)(2,1)S(1)} collective-permute-done((bf16[128,1024]{1,0:T(8,128)(2,1)S(1)}, bf16[128,1024]{1,0:T(8,128)(2,1)S(1)}, u32[]{:S(2)}, u32[]{:S(2)}) %collective-permute-start.10) | collective-permute-done | bytes 262176 | tf_op jit(solution)/shard_map/ppermute | solution.py:9
  37.3 1.6 %collective-permute-start.13 = (bf16[32,1024]{1,0:T(8,128)(2,1)S(1)}, bf16[32,1024]{1,0:T(8,128)(2,1)S(1)}, u32[]{:S(2)}, u32[]{:S(2)}) collective-permute-start(bf16[32,1024]{1,0:T(8,128)(2,1)S(1)} %get-tuple-element.10), channel_id=1, source_target_pairs={{0,6},{1,7},{2,4},{3,5},{4,2},{5,3},{6,0},{7,1},{8,14},{9,15},{10,... | collective-permute-start | bytes 196616 | tf_op jit(solution)/shard_map/ppermute | solution.py:9
  38.9 1.5 %collective-permute-start.12 = (bf16[32,1024]{1,0:T(8,128)(2,1)S(1)}, bf16[32,1024]{1,0:T(8,128)(2,1)S(1)}, u32[]{:S(2)}, u32[]{:S(2)}) collective-permute-start(bf16[32,1024]{1,0:T(8,128)(2,1)S(1)} %get-tuple-element.11), channel_id=1, source_target_pairs={{0,4},{1,5},{2,6},{3,7},{4,0},{5,1},{6,2},{7,3},{8,12},{9,13},{10,... | collective-permute-start | bytes 196616 | tf_op jit(solution)/shard_map/ppermute | solution.py:9
  40.5 0.4 collective-permute-start.11
  40.9 1.7 %collective-permute-done.13 = bf16[32,1024]{1,0:T(8,128)(2,1)S(1)} collective-permute-done((bf16[32,1024]{1,0:T(8,128)(2,1)S(1)}, bf16[32,1024]{1,0:T(8,128)(2,1)S(1)}, u32[]{:S(2)}, u32[]{:S(2)}) %collective-permute-start.13) | collective-permute-done | bytes 65568 | tf_op jit(solution)/shard_map/ppermute | solution.py:9
  42.6 1.2 %collective-permute-done.12 = bf16[32,1024]{1,0:T(8,128)(2,1)S(1)} collective-permute-done((bf16[32,1024]{1,0:T(8,128)(2,1)S(1)}, bf16[32,1024]{1,0:T(8,128)(2,1)S(1)}, u32[]{:S(2)}, u32[]{:S(2)}) %collective-permute-start.12) | collective-permute-done | bytes 65568 | tf_op jit(solution)/shard_map/ppermute | solution.py:9
  43.8 0.9 collective-permute-done.11
  44.8 3.7 %collective-permute-start.16 = (bf16[32,1024]{1,0:T(8,128)(2,1)S(1)}, bf16[32,1024]{1,0:T(8,128)(2,1)S(1)}, u32[]{:S(2)}, u32[]{:S(2)}) collective-permute-start(bf16[32,1024]{1,0:T(8,128)(2,1)S(1)} %add_convert_fusion.7), channel_id=1, source_target_pairs={{0,24},{8,16},{16,8},{24,0},{1,25},{9,17},{17,9},{25,1},{2,26},{10... | collective-permute-start | bytes 196616 | tf_op jit(solution)/shard_map/ppermute | solution.py:9
  48.4 0.8 collective-permute-start.14
  49.2 2.0 %collective-permute-done.16 = bf16[32,1024]{1,0:T(8,128)(2,1)S(1)} collective-permute-done((bf16[32,1024]{1,0:T(8,128)(2,1)S(1)}, bf16[32,1024]{1,0:T(8,128)(2,1)S(1)}, u32[]{:S(2)}, u32[]{:S(2)}) %collective-permute-start.16) | collective-permute-done | bytes 65568 | tf_op jit(solution)/shard_map/ppermute | solution.py:9
  51.2 2.6 %collective-permute-done.15 = bf16[32,1024]{1,0:T(8,128)(2,1)S(1)} collective-permute-done((bf16[32,1024]{1,0:T(8,128)(2,1)S(1)}, bf16[32,1024]{1,0:T(8,128)(2,1)S(1)}, u32[]{:S(2)}, u32[]{:S(2)}) %collective-permute-start.15) | collective-permute-done | bytes 65568 | tf_op jit(solution)/shard_map/ppermute | solution.py:9
  53.8 0.1 broadcast_in_dim.28
  54.0 0.5 collective-permute-start.17
  54.5 1.2 %collective-permute-start.18 = (bf16[128,1024]{1,0:T(8,128)(2,1)S(1)}, bf16[128,1024]{1,0:T(8,128)(2,1)S(1)}, u32[]{:S(2)}, u32[]{:S(2)}) collective-permute-start(bf16[128,1024]{1,0:T(8,128)(2,1)S(1)} %get-tuple-element.7), channel_id=1, source_target_pairs={{0,4},{1,5},{2,6},{3,7},{4,0},{5,1},{6,2},{7,3},{8,12},{9,13},{10,... | collective-permute-start | bytes 786440 | tf_op jit(solution)/shard_map/ppermute | solution.py:9
  55.7 1.9 %collective-permute-start.19 = (bf16[128,1024]{1,0:T(8,128)(2,1)S(1)}, bf16[128,1024]{1,0:T(8,128)(2,1)S(1)}, u32[]{:S(2)}, u32[]{:S(2)}) collective-permute-start(bf16[128,1024]{1,0:T(8,128)(2,1)S(1)} %get-tuple-element.7), channel_id=1, source_target_pairs={{0,6},{1,7},{2,4},{3,5},{4,2},{5,3},{6,0},{7,1},{8,14},{9,15},{10,... | collective-permute-start | bytes 786440 | tf_op jit(solution)/shard_map/ppermute | solution.py:9
  57.5 2.0 %fusion.2 = f32[256,1024]{1,0:T(8,128)S(1)} fusion(bf16[2,768,1024]{2,1,0:T(8,128)(2,1)} %param.10, f32[256,768]{1,0:T(8,128)S(1)} %fusion.42, f32[256]{0:T(256)S(1)} %bitcast.100), kind=kOutput, calls=%fused_computation.3 | convolution fusion | flops 403243008 | bytes 3408896 | tf_op jit(solution)/shard_map/dot_general | solution.py:17
  59.6 3.7 %collective-permute-done.17 = bf16[128,1024]{1,0:T(8,128)(2,1)S(1)} collective-permute-done((bf16[128,1024]{1,0:T(8,128)(2,1)S(1)}, bf16[128,1024]{1,0:T(8,128)(2,1)S(1)}, u32[]{:S(2)}, u32[]{:S(2)}) %collective-permute-start.17) | collective-permute-done | bytes 262176 | tf_op jit(solution)/shard_map/ppermute | solution.py:9
  63.3 3.9 %collective-permute-done.18 = bf16[128,1024]{1,0:T(8,128)(2,1)S(1)} collective-permute-done((bf16[128,1024]{1,0:T(8,128)(2,1)S(1)}, bf16[128,1024]{1,0:T(8,128)(2,1)S(1)}, u32[]{:S(2)}, u32[]{:S(2)}) %collective-permute-start.18) | collective-permute-done | bytes 262176 | tf_op jit(solution)/shard_map/ppermute | solution.py:9
  67.3 0.1 collective-permute-start.20
  67.4 0.6 fusion.30
  68.1 0.5 collective-permute-start.6
  68.6 1.8 %collective-permute-done.6 = bf16[128,1024]{1,0:T(8,128)(2,1)S(1)} collective-permute-done((bf16[128,1024]{1,0:T(8,128)(2,1)S(1)}, bf16[128,1024]{1,0:T(8,128)(2,1)S(1)}, u32[]{:S(2)}, u32[]{:S(2)}) %collective-permute-start.6) | collective-permute-done | bytes 262176 | tf_op jit(solution)/shard_map/ppermute | solution.py:9
  70.5 0.7 constant_dynamic-slice_fusion.5
  71.2 1.5 %collective-permute-start.9 = (bf16[32,1024]{1,0:T(8,128)(2,1)}, bf16[32,1024]{1,0:T(8,128)(2,1)S(1)}, u32[]{:S(2)}, u32[]{:S(2)}) collective-permute-start(bf16[32,1024]{1,0:T(8,128)(2,1)} %get-tuple-element.13), channel_id=1, source_target_pairs={{0,6},{1,7},{2,4},{3,5},{4,2},{5,3},{6,0},{7,1},{8,14},{9,15},{10,... | collective-permute-start | bytes 196616 | tf_op jit(solution)/shard_map/ppermute | solution.py:9
  72.7 1.3 %collective-permute-start.8 = (bf16[32,1024]{1,0:T(8,128)(2,1)}, bf16[32,1024]{1,0:T(8,128)(2,1)S(1)}, u32[]{:S(2)}, u32[]{:S(2)}) collective-permute-start(bf16[32,1024]{1,0:T(8,128)(2,1)} %get-tuple-element.14), channel_id=1, source_target_pairs={{0,4},{1,5},{2,6},{3,7},{4,0},{5,1},{6,2},{7,3},{8,12},{9,13},{10,... | collective-permute-start | bytes 196616 | tf_op jit(solution)/shard_map/ppermute | solution.py:9
  74.1 0.6 collective-permute-start.7
  74.7 1.5 %collective-permute-start.23 = (bf16[256,512]{1,0:T(8,128)(2,1)}, bf16[256,512]{1,0:T(8,128)(2,1)}, u32[]{:S(2)}, u32[]{:S(2)}) collective-permute-start(bf16[256,512]{1,0:T(8,128)(2,1)} %param.7), channel_id=1, source_target_pairs={{0,24},{8,16},{16,8},{24,0},{1,25},{9,17},{17,9},{25,1},{2,26},{10... | collective-permute-start | bytes 786440 | tf_op jit(solution)/shard_map/ppermute | solution.py:9
  76.2 0.4 collective-permute-done.9
  76.6 0.7 collective-permute-start.22
  77.3 0.5 collective-permute-done.8
  77.8 1.2 %collective-permute-start.21 = (bf16[256,512]{1,0:T(8,128)(2,1)}, bf16[256,512]{1,0:T(8,128)(2,1)S(1)}, u32[]{:S(2)}, u32[]{:S(2)}) collective-permute-start(bf16[256,512]{1,0:T(8,128)(2,1)} %param.7), channel_id=1, source_target_pairs={{0,8},{8,0},{16,24},{24,16},{1,9},{9,1},{17,25},{25,17},{2,10},{10... | collective-permute-start | bytes 786440 | tf_op jit(solution)/shard_map/ppermute | solution.py:9
  79.1 1.5 %add_convert_fusion.8 = bf16[32,1024]{1,0:T(8,128)(2,1)} fusion(bf16[32,1024]{1,0:T(8,128)(2,1)S(1)} %collective-permute-done.9, bf16[32,1024]{1,0:T(8,128)(2,1)S(1)} %collective-permute-done.8, bf16[32,1024]{1,0:T(8,128)(2,1)} %collective-permute-done.7, bf16[128,1024]{1,0:T(8,128)(2,1)S(1)} %add_convert_fusion.1, s32[]{:T(128)S(6)} %select_n.95), kind=kLoop, calls=%fused_computation.73 | loop fusion | flops 262144 | bytes 327684 | tf_op jit(solution)/shard_map/convert_element_type | solution.py:60
  80.6 0.1 select_bitcast_fusion.1
  80.7 0.2 maximum_bitcast_fusion
  81.0 0.3 copy.20
  81.3 1.2 %convolution_convert_fusion = bf16[256,512]{1,0:T(8,128)(2,1)} fusion(bf16[256,1024]{1,0:T(8,128)(2,1)S(1)} %bitcast.92, bf16[512,1024]{1,0:T(8,128)(2,1)S(1)} %copy-done), kind=kOutput, calls=%fused_computation.35 | convolution fusion | flops 268566528 | bytes 1835008 | tf_op jit(solution)/shard_map/dot_general | solution.py:21
  82.5 3.7 %collective-permute-done.23 = bf16[256,512]{1,0:T(8,128)(2,1)} collective-permute-done((bf16[256,512]{1,0:T(8,128)(2,1)}, bf16[256,512]{1,0:T(8,128)(2,1)}, u32[]{:S(2)}, u32[]{:S(2)}) %collective-permute-start.23) | collective-permute-done | bytes 262176 | tf_op jit(solution)/shard_map/ppermute | solution.py:9
  86.1 12.5 %collective-permute-done.22 = bf16[256,512]{1,0:T(8,128)(2,1)S(1)} collective-permute-done((bf16[256,512]{1,0:T(8,128)(2,1)}, bf16[256,512]{1,0:T(8,128)(2,1)S(1)}, u32[]{:S(2)}, u32[]{:S(2)}) %collective-permute-start.22) | collective-permute-done | bytes 262176 | tf_op jit(solution)/shard_map/ppermute | solution.py:9
  98.6 3.6 %fusion.59 = f32[512,1024]{1,0:T(8,128)} fusion(bf16[1024,1024]{1,0:T(8,128)(2,1)S(1)} %bitcast.93, bf16[256,512]{1,0:T(8,128)(2,1)} %collective-permute-done.23, bf16[256,512]{1,0:T(8,128)(2,1)S(1)} %collective-permute-done.22, bf16[256,512]{1,0:T(8,128)(2,1)S(1)} %collective-permute-done.21, bf16[256,512]{1,0:T(8,128)(2,1)} %param.7), kind=kOutput, calls=%fused_computation.39 | convolution fusion | flops 1077936128 | bytes 5242880 | tf_op jit(solution)/shard_map/dot_general | solution.py:137
  (67 shorter events, 1.0 us)
Async XLA Ops:
  0.6 1.4 %copy-start = (bf16[512,1024]{1,0:T(8,128)(2,1)S(1)}, bf16[512,1024]{1,0:T(8,128)(2,1)}, u32[]{:S(2)}) copy-start(bf16[512,1024]{1,0:T(8,128)(2,1)} %param.8) | copy-start | bytes 3145732
  0.6 2.2 %copy-start.5 = (bf16[32,1024]{1,0:T(8,128)(2,1)S(1)}, bf16[32,1024]{1,0:T(8,128)(2,1)}, u32[]{:S(2)}) copy-start(bf16[32,1024]{1,0:T(8,128)(2,1)} %param.13) | copy-start | bytes 196612
  2.0 5.3 %copy-start.7 = (f32[32,8]{0,1:T(8,128)S(1)}, f32[32,8]{0,1:T(8,128)}, u32[]{:S(2)}) copy-start(f32[32,8]{0,1:T(8,128)} %param.12) | copy-start | bytes 3076
  2.0 5.3 %copy-start.8 = (s32[32,8]{0,1:T(8,128)S(1)}, s32[32,8]{0,1:T(8,128)}, u32[]{:S(2)}) copy-start(s32[32,8]{0,1:T(8,128)} %param.11) | copy-start | bytes 3076
  2.3 1.7 %collective-permute-start = (bf16[128,1024]{1,0:T(8,128)(2,1)S(1)}, bf16[128,1024]{1,0:T(8,128)(2,1)S(1)}, u32[]{:S(2)}, u32[]{:S(2)}) collective-permute-start(bf16[128,1024]{1,0:T(8,128)(2,1)S(1)} %convolution_convert_fusion.1), channel_id=1, source_target_pairs={{0,1},{1,0},{2,3},{3,2},{4,5},{5,4},{6,7},{7,6},{8,9},{9,8},{10,11... | collective-permute-start | bytes 786440 | tf_op jit(solution)/shard_map/ppermute | solution.py:9
  4.4 7.5 %collective-permute-start.3 = (bf16[80,1024]{1,0:T(8,128)(2,1)S(1)}, bf16[80,1024]{1,0:T(8,128)(2,1)S(1)}, u32[]{:S(2)}, u32[]{:S(2)}) collective-permute-start(bf16[80,1024]{1,0:T(8,128)(2,1)S(1)} %pad_maximum_fusion.13), channel_id=1, source_target_pairs={{0,4},{1,5},{2,6},{3,7},{4,0},{5,1},{6,2},{7,3},{8,12},{9,13},{10,... | collective-permute-start | bytes 491528 | tf_op jit(solution)/shard_map/ppermute | solution.py:9
  7.6 6.8 %collective-permute-start.1 = (bf16[96,1024]{1,0:T(8,128)(2,1)S(1)}, bf16[96,1024]{1,0:T(8,128)(2,1)S(1)}, u32[]{:S(2)}, u32[]{:S(2)}) collective-permute-start(bf16[96,1024]{1,0:T(8,128)(2,1)S(1)} %pad_maximum_fusion.11), channel_id=1, source_target_pairs={{0,2},{1,3},{2,0},{3,1},{4,6},{5,7},{6,4},{7,5},{8,10},{9,11},{10,... | collective-permute-start | bytes 589832 | tf_op jit(solution)/shard_map/ppermute | solution.py:9
  11.9 6.7 %collective-permute-start.4 = (bf16[96,1024]{1,0:T(8,128)(2,1)S(1)}, bf16[96,1024]{1,0:T(8,128)(2,1)S(1)}, u32[]{:S(2)}, u32[]{:S(2)}) collective-permute-start(bf16[96,1024]{1,0:T(8,128)(2,1)S(1)} %pad_maximum_fusion.12), channel_id=1, source_target_pairs={{0,2},{1,3},{2,0},{3,1},{4,6},{5,7},{6,4},{7,5},{8,10},{9,11},{10,... | collective-permute-start | bytes 589832 | tf_op jit(solution)/shard_map/ppermute | solution.py:9
  14.5 6.5 %collective-permute-start.2 = (bf16[112,1024]{1,0:T(8,128)(2,1)S(1)}, bf16[112,1024]{1,0:T(8,128)(2,1)S(1)}, u32[]{:S(2)}, u32[]{:S(2)}) collective-permute-start(bf16[112,1024]{1,0:T(8,128)(2,1)S(1)} %pad_maximum_fusion.8), channel_id=1, source_target_pairs={{0,4},{1,5},{2,6},{3,7},{4,0},{5,1},{6,2},{7,3},{8,12},{9,13},{10,... | collective-permute-start | bytes 688136 | tf_op jit(solution)/shard_map/ppermute | solution.py:9
  21.2 2.0 %collective-permute-start.5 = (bf16[272,1024]{1,0:T(8,128)(2,1)S(1)}, bf16[272,1024]{1,0:T(8,128)(2,1)S(1)}, u32[]{:S(2)}, u32[]{:S(2)}) collective-permute-start(bf16[272,1024]{1,0:T(8,128)(2,1)S(1)} %pad_maximum_fusion), channel_id=1, source_target_pairs={{0,1},{1,0},{2,3},{3,2},{4,5},{5,4},{6,7},{7,6},{8,9},{9,8},{10,11... | collective-permute-start | bytes 1671176 | tf_op jit(solution)/shard_map/ppermute | solution.py:9
  23.2 0.9 copy-start.4
  24.1 2.4 %copy-start.9 = (bf16[2,1024,768]{2,1,0:T(8,128)(2,1)S(1)}, bf16[2,1024,768]{2,1,0:T(8,128)(2,1)}, u32[]{:S(2)}) copy-start(bf16[2,1024,768]{2,1,0:T(8,128)(2,1)} %param.9) | copy-start | bytes 9437188
  26.5 1.4 %copy-start.6 = (bf16[128,1024]{1,0:T(8,128)(2,1)S(1)}, bf16[128,1024]{1,0:T(8,128)(2,1)}, u32[]{:S(2)}) copy-start(bf16[128,1024]{1,0:T(8,128)(2,1)} %get-tuple-element.5) | copy-start | bytes 786436
  27.1 5.0 %copy-start.2 = (f32[256,768]{1,0:T(8,128)}, f32[256,768]{1,0:T(8,128)S(1)}, u32[]{:S(2)}) copy-start(f32[256,768]{1,0:T(8,128)S(1)} %fusion.36) | copy-start | bytes 2359300
  35.6 1.6 %collective-permute-start.10 = (bf16[128,1024]{1,0:T(8,128)(2,1)S(1)}, bf16[128,1024]{1,0:T(8,128)(2,1)S(1)}, u32[]{:S(2)}, u32[]{:S(2)}) collective-permute-start(bf16[128,1024]{1,0:T(8,128)(2,1)S(1)} %slice.177), channel_id=1, source_target_pairs={{0,1},{1,0},{2,3},{3,2},{4,5},{5,4},{6,7},{7,6},{8,9},{9,8},{10,11... | collective-permute-start | bytes 786440 | tf_op jit(solution)/shard_map/ppermute | solution.py:9
  37.3 5.3 %collective-permute-start.13 = (bf16[32,1024]{1,0:T(8,128)(2,1)S(1)}, bf16[32,1024]{1,0:T(8,128)(2,1)S(1)}, u32[]{:S(2)}, u32[]{:S(2)}) collective-permute-start(bf16[32,1024]{1,0:T(8,128)(2,1)S(1)} %get-tuple-element.10), channel_id=1, source_target_pairs={{0,6},{1,7},{2,4},{3,5},{4,2},{5,3},{6,0},{7,1},{8,14},{9,15},{10,... | collective-permute-start | bytes 196616 | tf_op jit(solution)/shard_map/ppermute | solution.py:9
  38.9 4.9 %collective-permute-start.12 = (bf16[32,1024]{1,0:T(8,128)(2,1)S(1)}, bf16[32,1024]{1,0:T(8,128)(2,1)S(1)}, u32[]{:S(2)}, u32[]{:S(2)}) collective-permute-start(bf16[32,1024]{1,0:T(8,128)(2,1)S(1)} %get-tuple-element.11), channel_id=1, source_target_pairs={{0,4},{1,5},{2,6},{3,7},{4,0},{5,1},{6,2},{7,3},{8,12},{9,13},{10,... | collective-permute-start | bytes 196616 | tf_op jit(solution)/shard_map/ppermute | solution.py:9
  40.5 4.3 %collective-permute-start.11 = (bf16[32,1024]{1,0:T(8,128)(2,1)S(1)}, bf16[32,1024]{1,0:T(8,128)(2,1)S(1)}, u32[]{:S(2)}, u32[]{:S(2)}) collective-permute-start(bf16[32,1024]{1,0:T(8,128)(2,1)S(1)} %get-tuple-element.9), channel_id=1, source_target_pairs={{0,2},{1,3},{2,0},{3,1},{4,6},{5,7},{6,4},{7,5},{8,10},{9,11},{10,... | collective-permute-start | bytes 196616 | tf_op jit(solution)/shard_map/ppermute | solution.py:9
  44.8 6.4 %collective-permute-start.16 = (bf16[32,1024]{1,0:T(8,128)(2,1)S(1)}, bf16[32,1024]{1,0:T(8,128)(2,1)S(1)}, u32[]{:S(2)}, u32[]{:S(2)}) collective-permute-start(bf16[32,1024]{1,0:T(8,128)(2,1)S(1)} %add_convert_fusion.7), channel_id=1, source_target_pairs={{0,24},{8,16},{16,8},{24,0},{1,25},{9,17},{17,9},{25,1},{2,26},{10... | collective-permute-start | bytes 196616 | tf_op jit(solution)/shard_map/ppermute | solution.py:9
  48.4 5.4 %collective-permute-start.15 = (bf16[32,1024]{1,0:T(8,128)(2,1)S(1)}, bf16[32,1024]{1,0:T(8,128)(2,1)S(1)}, u32[]{:S(2)}, u32[]{:S(2)}) collective-permute-start(bf16[32,1024]{1,0:T(8,128)(2,1)S(1)} %add_convert_fusion.7), channel_id=1, source_target_pairs={{0,16},{8,24},{16,0},{24,8},{1,17},{9,25},{17,1},{25,9},{2,18},{10... | collective-permute-start | bytes 196616 | tf_op jit(solution)/shard_map/ppermute | solution.py:9
  48.4 5.4 %collective-permute-start.14 = (bf16[32,1024]{1,0:T(8,128)(2,1)S(1)}, bf16[32,1024]{1,0:T(8,128)(2,1)S(1)}, u32[]{:S(2)}, u32[]{:S(2)}) collective-permute-start(bf16[32,1024]{1,0:T(8,128)(2,1)S(1)} %add_convert_fusion.7), channel_id=1, source_target_pairs={{0,8},{8,0},{16,24},{24,16},{1,9},{9,1},{17,25},{25,17},{2,10},{10... | collective-permute-start | bytes 196616 | tf_op jit(solution)/shard_map/ppermute | solution.py:9
  54.0 13.4 %copy-start.1 = (bf16[2,768,1024]{2,1,0:T(8,128)(2,1)S(1)}, bf16[2,768,1024]{2,1,0:T(8,128)(2,1)}, u32[]{:S(2)}) copy-start(bf16[2,768,1024]{2,1,0:T(8,128)(2,1)} %param.10) | copy-start | bytes 9437188
  54.0 13.4 %copy-start.3 = (f32[256,768]{1,0:T(8,128)S(1)}, f32[256,768]{1,0:T(8,128)}, u32[]{:S(2)}) copy-start(f32[256,768]{1,0:T(8,128)} %copy-done.2) | copy-start | bytes 2359300
  54.0 9.3 %collective-permute-start.17 = (bf16[128,1024]{1,0:T(8,128)(2,1)S(1)}, bf16[128,1024]{1,0:T(8,128)(2,1)S(1)}, u32[]{:S(2)}, u32[]{:S(2)}) collective-permute-start(bf16[128,1024]{1,0:T(8,128)(2,1)S(1)} %get-tuple-element.7), channel_id=1, source_target_pairs={{0,2},{1,3},{2,0},{3,1},{4,6},{5,7},{6,4},{7,5},{8,10},{9,11},{10,... | collective-permute-start | bytes 786440 | tf_op jit(solution)/shard_map/ppermute | solution.py:9
  54.5 12.8 %collective-permute-start.18 = (bf16[128,1024]{1,0:T(8,128)(2,1)S(1)}, bf16[128,1024]{1,0:T(8,128)(2,1)S(1)}, u32[]{:S(2)}, u32[]{:S(2)}) collective-permute-start(bf16[128,1024]{1,0:T(8,128)(2,1)S(1)} %get-tuple-element.7), channel_id=1, source_target_pairs={{0,4},{1,5},{2,6},{3,7},{4,0},{5,1},{6,2},{7,3},{8,12},{9,13},{10,... | collective-permute-start | bytes 786440 | tf_op jit(solution)/shard_map/ppermute | solution.py:9
  55.7 11.6 %collective-permute-start.19 = (bf16[128,1024]{1,0:T(8,128)(2,1)S(1)}, bf16[128,1024]{1,0:T(8,128)(2,1)S(1)}, u32[]{:S(2)}, u32[]{:S(2)}) collective-permute-start(bf16[128,1024]{1,0:T(8,128)(2,1)S(1)} %get-tuple-element.7), channel_id=1, source_target_pairs={{0,6},{1,7},{2,4},{3,5},{4,2},{5,3},{6,0},{7,1},{8,14},{9,15},{10,... | collective-permute-start | bytes 786440 | tf_op jit(solution)/shard_map/ppermute | solution.py:9
  67.3 13.3 %collective-permute-start.20 = (bf16[4,4,32,1024]{3,2,1,0:T(8,128)(2,1)S(1)}, bf16[4,4,32,1024]{3,2,1,0:T(8,128)(2,1)S(1)}, u32[]{:S(2)}, u32[]{:S(2)}) collective-permute-start(bf16[4,4,32,1024]{3,2,1,0:T(8,128)(2,1)S(1)} %bitcast.90), channel_id=1, source_target_pairs={{0,1},{1,0},{2,3},{3,2},{4,5},{5,4},{6,7},{7,6},{8,9},{9,8},{10,11... | collective-permute-start | bytes 3145736 | tf_op jit(solution)/shard_map/ppermute | solution.py:9
  68.1 2.3 %collective-permute-start.6 = (bf16[128,1024]{1,0:T(8,128)(2,1)S(1)}, bf16[128,1024]{1,0:T(8,128)(2,1)S(1)}, u32[]{:S(2)}, u32[]{:S(2)}) collective-permute-start(bf16[128,1024]{1,0:T(8,128)(2,1)S(1)} %slice.174), channel_id=1, source_target_pairs={{0,1},{1,0},{2,3},{3,2},{4,5},{5,4},{6,7},{7,6},{8,9},{9,8},{10,11... | collective-permute-start | bytes 786440 | tf_op jit(solution)/shard_map/ppermute | solution.py:9
  71.2 5.4 %collective-permute-start.9 = (bf16[32,1024]{1,0:T(8,128)(2,1)}, bf16[32,1024]{1,0:T(8,128)(2,1)S(1)}, u32[]{:S(2)}, u32[]{:S(2)}) collective-permute-start(bf16[32,1024]{1,0:T(8,128)(2,1)} %get-tuple-element.13), channel_id=1, source_target_pairs={{0,6},{1,7},{2,4},{3,5},{4,2},{5,3},{6,0},{7,1},{8,14},{9,15},{10,... | collective-permute-start | bytes 196616 | tf_op jit(solution)/shard_map/ppermute | solution.py:9
  72.7 5.1 %collective-permute-start.8 = (bf16[32,1024]{1,0:T(8,128)(2,1)}, bf16[32,1024]{1,0:T(8,128)(2,1)S(1)}, u32[]{:S(2)}, u32[]{:S(2)}) collective-permute-start(bf16[32,1024]{1,0:T(8,128)(2,1)} %get-tuple-element.14), channel_id=1, source_target_pairs={{0,4},{1,5},{2,6},{3,7},{4,0},{5,1},{6,2},{7,3},{8,12},{9,13},{10,... | collective-permute-start | bytes 196616 | tf_op jit(solution)/shard_map/ppermute | solution.py:9
  74.1 5.0 %collective-permute-start.7 = (bf16[32,1024]{1,0:T(8,128)(2,1)}, bf16[32,1024]{1,0:T(8,128)(2,1)}, u32[]{:S(2)}, u32[]{:S(2)}) collective-permute-start(bf16[32,1024]{1,0:T(8,128)(2,1)} %get-tuple-element.12), channel_id=1, source_target_pairs={{0,2},{1,3},{2,0},{3,1},{4,6},{5,7},{6,4},{7,5},{8,10},{9,11},{10,... | collective-permute-start | bytes 196616 | tf_op jit(solution)/shard_map/ppermute | solution.py:9
  74.7 11.5 %collective-permute-start.23 = (bf16[256,512]{1,0:T(8,128)(2,1)}, bf16[256,512]{1,0:T(8,128)(2,1)}, u32[]{:S(2)}, u32[]{:S(2)}) collective-permute-start(bf16[256,512]{1,0:T(8,128)(2,1)} %param.7), channel_id=1, source_target_pairs={{0,24},{8,16},{16,8},{24,0},{1,25},{9,17},{17,9},{25,1},{2,26},{10... | collective-permute-start | bytes 786440 | tf_op jit(solution)/shard_map/ppermute | solution.py:9
  76.6 22.0 %collective-permute-start.22 = (bf16[256,512]{1,0:T(8,128)(2,1)}, bf16[256,512]{1,0:T(8,128)(2,1)S(1)}, u32[]{:S(2)}, u32[]{:S(2)}) collective-permute-start(bf16[256,512]{1,0:T(8,128)(2,1)} %param.7), channel_id=1, source_target_pairs={{0,16},{8,24},{16,0},{24,8},{1,17},{9,25},{17,1},{25,9},{2,18},{10... | collective-permute-start | bytes 786440 | tf_op jit(solution)/shard_map/ppermute | solution.py:9
  77.8 20.8 %collective-permute-start.21 = (bf16[256,512]{1,0:T(8,128)(2,1)}, bf16[256,512]{1,0:T(8,128)(2,1)S(1)}, u32[]{:S(2)}, u32[]{:S(2)}) collective-permute-start(bf16[256,512]{1,0:T(8,128)(2,1)} %param.7), channel_id=1, source_target_pairs={{0,8},{8,0},{16,24},{24,16},{1,9},{9,1},{17,25},{25,17},{2,10},{10... | collective-permute-start | bytes 786440 | tf_op jit(solution)/shard_map/ppermute | solution.py:9

commit v2 on v1

v2 whole, which is shorter than its diff:
```python
import jax
import jax.numpy as jnp
from jax import lax
from jax.experimental import pallas as pl
from jax.experimental.pallas import tpu as pltpu
from jax.sharding import PartitionSpec as P

VMEM = pl.BlockSpec(memory_space=pltpu.VMEM)
ANY = pl.BlockSpec(memory_space=pl.ANY)
BF16 = jnp.bfloat16
F32 = jnp.float32
NN = (((1,), (0,)), ((), ()))
NT = (((1,), (1,)), ((), ()))
TN = (((0,), (0,)), ((), ()))
MIB = 1 << 20


def mxu(first, second, dims=NN):
    return lax.dot_general(first, second, dims, preferred_element_type=F32)


def shape(rows, columns, dtype=BF16):
    return jax.ShapeDtypeStruct((rows, columns), dtype)


def add_bf16(first, second):
    return (first.astype(F32) + second.astype(F32)).astype(BF16)


def local(body, outs, args, name, scratch=(), limit=8, flops=0, ties=()):
    def kernel(*refs):
        body(*refs[: len(args)], *refs[len(args) + len(ties) :])

    single = not isinstance(outs, tuple)
    return pl.pallas_call(
        kernel,
        out_shape=outs,
        in_specs=[VMEM] * len(args) + [ANY] * len(ties),
        out_specs=VMEM if single else tuple(VMEM for _ in outs),
        scratch_shapes=list(scratch),
        compiler_params=pltpu.CompilerParams(vmem_limit_bytes=limit * MIB),
        cost_estimate=pl.CostEstimate(flops=flops, bytes_accessed=MIB, transcendentals=0),
        name=name,
    )(*args, *ties)


def xor_permute(value, axis, mask):
    size = lax.axis_size(axis)
    return lax.ppermute(value, axis, [(i, i ^ mask) for i in range(size)])


def line_gather(value, axis):
    inner, outer = [(1, 2), (2, 1)], [(1, 0), (2, 3)]
    near = xor_permute(value, axis, 1)
    middle = lax.ppermute(value, axis, inner)
    middle_far = lax.ppermute(near, axis, inner)
    edge = lax.ppermute(middle, axis, outer)
    edge_far = lax.ppermute(middle_far, axis, outer)
    return [(near, middle), (middle_far, edge), (edge_far,)]


def hop(hops, index):
    return hops[index] if index < len(hops) else ()


def order_of(bits):
    masks = [0]
    for bit in bits:
        masks = masks + [mask ^ bit for mask in masks]
    return masks


def block(index, rows):
    return pl.ds(pl.multiple_of(index * rows, rows), rows)


def project(x, in_proj, tok):
    rows, features = x.shape
    width = in_proj.shape[1]
    owners = rows // tok
    half = rows // 2

    def body(x_ref, proj_ref, other_ref, mine_ref, rows_ref):
        me = lax.axis_index("expert")
        core = me % 2
        for chip in range(owners // 2):
            place = pl.ds(chip * tok, tok)
            rows_ref[place, :] = x_ref[block(2 * chip + 1 - core, tok), :]
            rows_ref[pl.ds(half + chip * tok, tok), :] = x_ref[block(2 * chip + core, tok), :]
        other_ref[...] = mxu(rows_ref[:half, :], proj_ref[...]).astype(BF16)
        mine_ref[...] = mxu(rows_ref[half:, :], proj_ref[...]).astype(BF16)

    return local(
        body,
        (shape(half, width), shape(half, width)),
        (x, in_proj),
        "project",
        scratch=[pltpu.VMEM((rows, features), BF16)],
        flops=2 * rows * features * width,
    )


def streams(part, got, out_grad, routing):
    half, width = part.shape
    tok = out_grad.shape[0]
    experts = routing.shape[0]

    def body(part_ref, got_ref, grad_ref, routing_ref, first_ref, second_ref):
        mid, rows = half // 2, tok // 2
        first_ref[:mid, :] = add_bf16(part_ref[:mid, :], got_ref[:mid, :])
        first_ref[mid : mid + experts, :] = routing_ref[...]
        first_ref[mid + experts :, :] = grad_ref[:rows, :]
        second_ref[:mid, :] = add_bf16(part_ref[mid:, :], got_ref[mid:, :])
        second_ref[mid:, :] = grad_ref[rows:, :]

    return local(
        body,
        (shape(half // 2 + experts + tok // 2, width), shape(half // 2 + tok // 2, width)),
        (part, got, out_grad, routing),
        "streams",
    )


def merge(sent, got, sums, flops=0, ties=()):
    width = sent[0].shape[1]
    rows = [value.shape[0] for value in sent]

    def body(*refs):
        count = len(sums)
        for i in range(count):
            sent_ref, got_ref, out_ref = refs[i], refs[count + i], refs[2 * count + i]
            out_ref[: sums[i], :] = add_bf16(sent_ref[: sums[i], :], got_ref[: sums[i], :])
            out_ref[sums[i] : rows[i], :] = sent_ref[sums[i] :, :]
            out_ref[rows[i] :, :] = got_ref[sums[i] :, :]

    return local(
        body,
        tuple(shape(2 * r - s, width) for r, s in zip(rows, sums)),
        tuple(sent) + tuple(got),
        "merge",
        flops=flops,
        ties=ties,
    )


def settle(sent, got, orders, tok, experts, ties=()):
    width = sent[0].shape[1]
    chips = len(orders[0])
    half = chips * tok
    mid, rows = half // 2, tok // 2

    def body(first_ref, second_ref, first_got, second_got, out_ref):
        chip = lax.axis_index("expert") // 2
        out_ref[:mid, :] = add_bf16(first_ref[:mid, :], first_got[:mid, :])
        out_ref[mid:half, :] = add_bf16(second_ref[:mid, :], second_got[:mid, :])
        table = pl.ds(mid, experts)
        out_ref[pl.ds(2 * half, experts), :] = add_bf16(first_ref[table, :], first_got[table, :])
        refs = ((first_ref, first_got, mid + experts), (second_ref, second_got, mid))
        for side, (own, partner, start) in enumerate(refs):
            for place, mask in enumerate(orders[side]):
                src = own if place < chips // 2 else partner
                offset = start + (place % (chips // 2)) * rows
                to = half + pl.multiple_of((chip ^ (mask // 2)) * tok, tok) + side * rows
                out_ref[pl.ds(pl.multiple_of(to, rows), rows), :] = src[pl.ds(offset, rows), :]

    return local(body, shape(2 * half + experts, width), tuple(sent) + tuple(got), "settle", ties=ties)


def experts(mine, other, up_weight, down_weight, half, ties=()):
    local_experts, width, hidden = up_weight.shape
    rows = 2 * half

    def body(mine_ref, other_ref, up, down, act_ref, lat_mine_ref, lat_other_ref, cot):
        me = lax.axis_index("expert")
        all_experts = mine_ref.shape[0] - rows
        ids = lax.broadcasted_iota(jnp.int32, (all_experts, 128), 0)
        slots = lax.broadcasted_iota(jnp.int32, (all_experts, 128), 1)
        pick = jnp.where(ids == slots + me * local_experts, 1.0, 0.0).astype(BF16)
        sources = ((mine_ref, 0), (other_ref, half))
        probs = []
        for src, place in sources:
            cot[pl.ds(place, half), :] = src[half:rows, :]
            probs.append(mxu(src[rows:, :half], pick, TN))
        probs = jnp.concatenate(probs, axis=0)
        total = None
        for i in range(local_experts):
            columns = pl.ds(i * hidden, hidden)
            pre = [mxu(src[:half, :], up[i]) for src, _ in sources]
            positive = jnp.maximum(jnp.concatenate(pre, axis=0), 0.0)
            weighted = positive * probs[:, i : i + 1]
            act_ref[:, columns] = (positive * weighted).astype(BF16)
            grad_act = mxu(cot[...], down[i], NT)
            grad_pre = (grad_act * (2.0 * weighted)).astype(BF16)
            term = mxu(grad_pre, up[i], NT)
            total = term if total is None else total + term
        lat_mine_ref[...] = total[:half].astype(BF16)
        lat_other_ref[...] = total[half:].astype(BF16)

    return local(
        body,
        (shape(rows, local_experts * hidden), shape(half, width), shape(half, width)),
        (mine, other, up_weight, down_weight),
        "experts",
        ties=ties,
        scratch=[pltpu.VMEM((rows, width), BF16)],
        limit=24,
        flops=2 * 3 * rows * width * hidden * local_experts,
    )


def outputs(act, down_weight, half):
    local_experts, hidden, width = down_weight.shape

    def body(act_ref, down, mine_ref, other_ref):
        total = None
        for i in range(local_experts):
            term = mxu(act_ref[:, pl.ds(i * hidden, hidden)], down[i])
            total = term if total is None else total + term
        mine_ref[...] = total[:half].astype(BF16)
        other_ref[...] = total[half:].astype(BF16)

    return local(
        body,
        (shape(half, width), shape(half, width)),
        (act, down_weight),
        "outputs",
        limit=16,
        flops=4 * half * local_experts * hidden * width,
    )


def pieces_of(first, second, chips, ties=()):
    rows, width = first.shape
    tok = rows // chips

    def body(first_ref, second_ref, *out_refs):
        chip = lax.axis_index("expert") // 2
        for mask in range(chips):
            rows = block(chip ^ mask, tok)
            out_refs[mask][...] = add_bf16(first_ref[rows, :], second_ref[rows, :])

    return local(body, tuple(shape(tok, width) for _ in range(chips)), (first, second), "pieces", ties=ties)


def scatter_sum(pieces):
    got = [xor_permute(pieces[k], "expert", 2 * k) for k in range(1, len(pieces))]
    total = pieces[0].astype(F32)
    for piece in got:
        total = total + piece.astype(F32)
    return total.astype(BF16)


def input_grads(pieces, in_proj, tok):
    features, width = in_proj.shape
    rows = len(pieces) * tok

    def body(*refs):
        piece_refs, (proj_ref, out_ref, rows_ref) = refs[: len(pieces)], refs[len(pieces) :]
        me = lax.axis_index("expert")
        for mask, piece_ref in enumerate(piece_refs):
            rows_ref[block(me ^ mask, tok), :] = piece_ref[:tok, :]
        out_ref[...] = mxu(rows_ref[...], proj_ref[...], NT).astype(BF16)

    return local(
        body,
        shape(rows, features),
        tuple(pieces) + (in_proj,),
        "input_grads",
        scratch=[pltpu.VMEM((rows, width), BF16)],
        limit=16,
        flops=2 * rows * features * width,
    )


def arrange(value, hops, chips, tok, tie):
    rows, features = value.shape
    count = 4 if hops else 1
    sources = (value,) + tuple(x for step in hops for x in step)

    def body(*refs):
        x_refs, out_refs = refs[: len(sources)], refs[len(sources) :]
        me = lax.axis_index("expert")

        def place(x_ref, mask):
            for k in range(chips):
                for twin in range(2):
                    out_refs[k][pl.ds((twin * count + mask) * tok, tok), :] = x_ref[
                        block(me ^ (2 * k + twin), tok), :
                    ]

        place(x_refs[0], 0)
        if hops:
            near, middle, middle_far, edge, edge_far = x_refs[1:]
            group = lax.axis_index("dp")
            at_edge = jnp.logical_or(group == 0, group == 3)
            place(near, 1)

            @pl.when(at_edge)
            def _():
                place(edge, 2)
                place(edge_far, 3)

            @pl.when(jnp.logical_not(at_edge))
            def _():
                place(middle_far, 2)
                place(middle, 3)

    out = tuple(shape(2 * count * tok, features) for _ in range(chips))
    return local(body, out, sources, "arrange", ties=(tie,))


def per_device(tokens_x, in_proj, up_weight, down_weight, expert_ids, route_probs, out_grad):
    owners = lax.axis_size("expert")
    groups = lax.axis_size("dp")
    chips = owners // 2
    chip = lax.axis_index("expert") // 2
    tok, top = expert_ids.shape
    all_experts = up_weight.shape[0] * owners
    features, width = in_proj.shape
    half = chips * tok
    bits = [1 << b for b in range(1, owners.bit_length() - 1)]
    gather_groups = groups == 4 and groups * owners * tok * width <= 1 << 22

    chosen = expert_ids[None, :, :] == jnp.arange(all_experts, dtype=jnp.int32)[:, None, None]
    routing = jnp.sum(jnp.where(chosen, route_probs[None, :, :], 0.0), axis=2).astype(BF16)
    routing = lax.dynamic_update_slice(
        jnp.zeros((all_experts, width), BF16), routing, (0, chip * tok)
    )

    part_other, part_mine = project(tokens_x, in_proj, tok)
    got = xor_permute(part_other, "expert", 1)
    sent = streams(part_mine, got, out_grad, routing)
    sums = (half // 2 + all_experts, half // 2)
    hops = line_gather(tokens_x, "dp") if gather_groups else []
    for step, stream_bits in enumerate(zip(bits, bits[::-1])):
        got = [xor_permute(value, "expert", bit) for value, bit in zip(sent, stream_bits)]
        if step + 1 < len(bits):
            sent = merge(sent, got, sums, ties=hop(hops, 0))
    mine = settle(sent, got, (order_of(bits), order_of(bits[::-1])), tok, all_experts, ties=hop(hops, 1))
    other = xor_permute(mine, "expert", 1)
    act, lat_mine, lat_other = experts(mine, other, up_weight, down_weight, half)
    latent_grad = scatter_sum(pieces_of(lat_mine, xor_permute(lat_other, "expert", 1), chips, hop(hops, 2)))
    out_mine, out_other = outputs(act, down_weight, half)
    combined = scatter_sum(pieces_of(out_mine, xor_permute(out_other, "expert", 1), chips))

    held = [latent_grad]
    if gather_groups:
        held += [xor_permute(latent_grad, "dp", m) for m in range(1, groups)]
    own = jnp.concatenate(held, axis=0)
    x_all = arrange(tokens_x, hops, chips, tok, own)
    all_pieces = []
    proj_grad = None
    for k in range(chips):
        piece = own if k == 0 else xor_permute(own, "expert", 2 * k)
        twin = xor_permute(piece, "expert", 1)
        all_pieces += [piece, twin]
        term = mxu(x_all[k], jnp.concatenate([piece, twin], axis=0), TN)
        proj_grad = term if proj_grad is None else proj_grad + term
    input_grad = input_grads(all_pieces, in_proj, tok)
    if not gather_groups:
        proj_grad = lax.psum(proj_grad, "dp")
    return (combined, input_grad, proj_grad)


def solution(mesh):
    return jax.shard_map(
        per_device,
        mesh=mesh,
        in_specs=(
            P("dp", "expert"),
            P("expert", None),
            P("expert", None, None),
            P("expert", None, None),
            P(("dp", "expert"), None),
            P(("dp", "expert"), None),
            P(("dp", "expert"), None),
        ),
        out_specs=(P(("dp", "expert"), None), P("dp", "expert"), P("expert", None)),
        check_vma=False,
    )
```

time: 103 us -> 73.1 us (0.71)
  waiting for transfers between devices: 48.2 us -> 21.5 us
  matrix products: 18.6 us -> 3.16 us
  Pallas kernels: 0 us -> 9.94 us
  starting transfers between devices: 27.1 us -> 29.7 us
  local copies, waits for them, and re-layouts: 4.77 us -> 6.03 us
    ppermute x24 -> x25, waiting for transfers between devices: 48.2 us -> 14 us  [xor_permute(): return lax.ppermute(value, axis, [(i, i ^ mask) for i in range(size)])]
    dot_general x10 -> x4, matrix products: 18.6 us -> 3.16 us  [mxu(): return lax.dot_general(first, second, dims, preferred_element_type=F32)]
    pallas_call x0 -> x10, Pallas kernels: none -> 9.94 us  [local(): pl.pallas_call(kernel, out_shape=outs, in_specs=[VMEM] * len(args) + [ANY...]
    ppermute x0 -> x4, waiting for transfers between devices: none -> 7.52 us  [the longest x1 5.82 us: line_gather(): edge = lax.ppermute(middle, axis, outer)]
    unnamed x20 -> x17, local copies, waits for them, and re-layouts: 0.55 us -> 5.83 us
    ppermute x0 -> x4, starting transfers between devices: none -> 4.6 us  [the longest x1 1.35 us: line_gather(): middle = lax.ppermute(value, axis, inner)]
    ppermute x24 -> x25, starting transfers between devices: 27.1 us -> 25.1 us  [xor_permute(): return lax.ppermute(value, axis, [(i, i ^ mask) for i in range(size)])]
    dynamic_slice x3 -> x0, local copies, waits for them, and re-layouts: 1.79 us -> none  [the longest x1 1.08 us: per_device(): lax.dynamic_index_in_dim(x_cores, 1 - core, 1, False)]
  transfers between devices with their start and end apart: 24 -> 29, of which waited for: 19 -> 9; matrix products, arithmetic and copies ran while one was open for 7% -> 4% of each run, Pallas kernels for 0% -> 9%
where the time goes in v2:
time: 73.1 us; the launch traced here: 72.6 us
  starting transfers between devices  29.7 us (41%)
  waiting for transfers between devices  21.5 us (29%)
  Pallas kernels  9.94 us (14%)
  local copies, waits for them, and re-layouts  6.03 us (8%)
  matrix products  3.16 us (4%)
  other arithmetic  1.46 us (2%)
  between operations  0.85 us (1%)
    ppermute x25, starting transfers between devices, xor_permute(): return lax.ppermute(value, axis, [(i, i ^ mask) for i in range(size)])  25.1 us
    ppermute x25, waiting for transfers between devices, xor_permute(): return lax.ppermute(value, axis, [(i, i ^ mask) for i in range(size)])  14 us
    pallas_call x10, Pallas kernels, local(): pl.pallas_call(kernel, out_shape=outs, in_specs=[VMEM] * len(args) + [ANY...  9.94 us
    unnamed x17, local copies, waits for them, and re-layouts  5.83 us
    ppermute x1, waiting for transfers between devices, line_gather(): edge = lax.ppermute(middle, axis, outer)  5.82 us
    dot_general x4, matrix products, mxu(): return lax.dot_general(first, second, dims, preferred_element_type=F32)  3.16 us
    ppermute x1, waiting for transfers between devices, line_gather(): edge_far = lax.ppermute(middle_far, axis, outer)  1.69 us
  transfers between devices with their start and end apart: 29, of which 9 were waited for; matrix products, arithmetic and copies ran while one was open for 4% of the time, Pallas kernels for 9%

profile of v2, /device:TPU:0, one launch (start us, length us, event | category | flops | bytes accessed | tf_op | source)
XLA Modules:
  0.0 72.6 jit_solution(9022777642439294336)
XLA Ops:
  0.6 0.0 copy-start
  0.6 1.2 %copy-done = bf16[512,1024]{1,0:T(8,128)(2,1)S(1)} copy-done((bf16[512,1024]{1,0:T(8,128)(2,1)S(1)}, bf16[512,1024]{1,0:T(8,128)(2,1)}, u32[]{:S(2)}) %copy-start) | copy-done | bytes 1048600
  1.9 2.0 %project.1 = (bf16[128,1024]{1,0:T(8,128)(2,1)}, bf16[128,1024]{1,0:T(8,128)(2,1)S(1)}) custom-call(bf16[256,512]{1,0:T(8,128)(2,1)} %refs_0_.3, bf16[512,1024]{1,0:T(8,128)(2,1)S(1)} %copy-done), custom_call_target="tpu_custom_call" | custom-call | flops 268435456 | bytes 1048576 | tf_op jit(solution)/shard_map/project/pallas_call | solution.py:35
  3.8 0.7 copy-done.3
  4.5 0.5 collective-permute-start
  5.0 2.6 %collective-permute-start.3 = (bf16[256,512]{1,0:T(8,128)(2,1)}, bf16[256,512]{1,0:T(8,128)(2,1)S(1)}, u32[]{:S(2)}, u32[]{:S(2)}) collective-permute-start(bf16[256,512]{1,0:T(8,128)(2,1)} %refs_0_.3), channel_id=1, source_target_pairs={{0,8},{8,0},{16,24},{24,16},{1,9},{9,1},{17,25},{25,17},{2,10},{10... | collective-permute-start | bytes 786440 | tf_op jit(solution)/shard_map/ppermute | solution.py:49
  7.6 1.4 %collective-permute-start.4 = (bf16[256,512]{1,0:T(8,128)(2,1)}, bf16[256,512]{1,0:T(8,128)(2,1)}, u32[]{:S(2)}, u32[]{:S(2)}) collective-permute-start(bf16[256,512]{1,0:T(8,128)(2,1)} %refs_0_.3), channel_id=1, source_target_pairs={{8,16},{16,8},{9,17},{17,9},{10,18},{18,10},{11,19},{19,11},{12,20... | collective-permute-start | bytes 786440 | tf_op jit(solution)/shard_map/ppermute | solution.py:55
  8.9 0.7 %select_reduce_fusion = bf16[16,32]{1,0:T(8,128)(2,1)S(1)} fusion(f32[32,8]{0,1:T(8,128)} %param.12, s32[32,8]{0,1:T(8,128)} %param.11), kind=kLoop, calls=%fused_computation.16 | loop fusion | flops 11776 | bytes 3072 | tf_op jit(solution)/shard_map/reduce_sum | solution.py:325
  9.7 0.2 dynamic_update_slice.3.refs_3_
  9.8 0.0 collective-permute-done.refs_1_
  9.9 0.0 copy-start.4
  9.9 0.9 %copy-done.4 = bf16[128,1024]{1,0:T(8,128)(2,1)S(1)} copy-done((bf16[128,1024]{1,0:T(8,128)(2,1)S(1)}, bf16[128,1024]{1,0:T(8,128)(2,1)}, u32[]{:S(2)}) %copy-start.4) | copy-done | bytes 262168
  10.8 0.8 %copy-done.5 = bf16[32,1024]{1,0:T(8,128)(2,1)S(1)} copy-done((bf16[32,1024]{1,0:T(8,128)(2,1)S(1)}, bf16[32,1024]{1,0:T(8,128)(2,1)}, u32[]{:S(2)}) %copy-start.5) | copy-done | bytes 65560
  11.6 1.0 %streams.1 = (bf16[96,1024]{1,0:T(8,128)(2,1)S(1)}, bf16[80,1024]{1,0:T(8,128)(2,1)S(1)}) custom-call(bf16[128,1024]{1,0:T(8,128)(2,1)S(1)} %copy-done.4, bf16[128,1024]{1,0:T(8,128)(2,1)} %collective-permute-done.refs_1_, bf16[32,1024]{1,0:T(8,128)(2,1)S(1)} %copy-done.5, bf16[16,1024]{1,0:T(8,128)(2,1)S(1)} %dynamic_update_slice.3.refs_3_), custom_call_target="tpu_custom_call" | custom-call | bytes 1048576 | tf_op jit(solution)/shard_map/streams/pallas_call | solution.py:35
  12.7 1.6 %collective-permute-start.1 = (bf16[96,1024]{1,0:T(8,128)(2,1)S(1)}, bf16[96,1024]{1,0:T(8,128)(2,1)S(1)}, u32[]{:S(2)}, u32[]{:S(2)}) collective-permute-start(bf16[96,1024]{1,0:T(8,128)(2,1)S(1)} %get-tuple-element.28.refs_0_), channel_id=1, source_target_pairs={{0,2},{1,3},{2,0},{3,1},{4,6},{5,7},{6,4},{7,5},{8,10},{9,11},{10,... | collective-permute-start | bytes 589832 | tf_op jit(solution)/shard_map/ppermute | solution.py:49
  14.3 1.5 %collective-permute-start.2 = (bf16[80,1024]{1,0:T(8,128)(2,1)S(1)}, bf16[80,1024]{1,0:T(8,128)(2,1)S(1)}, u32[]{:S(2)}, u32[]{:S(2)}) collective-permute-start(bf16[80,1024]{1,0:T(8,128)(2,1)S(1)} %get-tuple-element.29.refs_1_), channel_id=1, source_target_pairs={{0,4},{1,5},{2,6},{3,7},{4,0},{5,1},{6,2},{7,3},{8,12},{9,13},{10,... | collective-permute-start | bytes 491528 | tf_op jit(solution)/shard_map/ppermute | solution.py:49
  15.8 0.7 collective-permute-start.7
  16.5 0.0 collective-permute-done.4.refs_5_.refs_2_
  16.5 1.3 %collective-permute-start.8 = (bf16[256,512]{1,0:T(8,128)(2,1)}, bf16[256,512]{1,0:T(8,128)(2,1)S(1)}, u32[]{:S(2)}, u32[]{:S(2)}) collective-permute-start(bf16[256,512]{1,0:T(8,128)(2,1)} %collective-permute-done.4.refs_5_.refs_2_), channel_id=1, source_target_pairs={{8,0},{16,24},{9,1},{17,25},{10,2},{18,26},{11,3},{19,27},{12,4},{... | collective-permute-start | bytes 786440 | tf_op jit(solution)/shard_map/ppermute | solution.py:57
  17.8 2.5 %collective-permute-done.2.refs_3_ = bf16[80,1024]{1,0:T(8,128)(2,1)S(1)} collective-permute-done((bf16[80,1024]{1,0:T(8,128)(2,1)S(1)}, bf16[80,1024]{1,0:T(8,128)(2,1)S(1)}, u32[]{:S(2)}, u32[]{:S(2)}) %collective-permute-start.2) | collective-permute-done | bytes 163872 | tf_op jit(solution)/shard_map/ppermute | solution.py:49
  20.4 0.0 collective-permute-done.1.refs_2_
  20.4 0.1 merge.1
  20.4 1.6 %collective-permute-start.5 = (bf16[112,1024]{1,0:T(8,128)(2,1)S(1)}, bf16[112,1024]{1,0:T(8,128)(2,1)S(1)}, u32[]{:S(2)}, u32[]{:S(2)}) collective-permute-start(bf16[112,1024]{1,0:T(8,128)(2,1)S(1)} %get-tuple-element.30.refs_0_), channel_id=1, source_target_pairs={{0,4},{1,5},{2,6},{3,7},{4,0},{5,1},{6,2},{7,3},{8,12},{9,13},{10,... | collective-permute-start | bytes 688136 | tf_op jit(solution)/shard_map/ppermute | solution.py:49
  22.0 1.0 %collective-permute-start.6 = (bf16[96,1024]{1,0:T(8,128)(2,1)S(1)}, bf16[96,1024]{1,0:T(8,128)(2,1)S(1)}, u32[]{:S(2)}, u32[]{:S(2)}) collective-permute-start(bf16[96,1024]{1,0:T(8,128)(2,1)S(1)} %get-tuple-element.31.refs_1_), channel_id=1, source_target_pairs={{0,2},{1,3},{2,0},{3,1},{4,6},{5,7},{6,4},{7,5},{8,10},{9,11},{10,... | collective-permute-start | bytes 589832 | tf_op jit(solution)/shard_map/ppermute | solution.py:49
  23.0 5.8 %collective-permute-done.8.refs_5_.refs_4_ = bf16[256,512]{1,0:T(8,128)(2,1)S(1)} collective-permute-done((bf16[256,512]{1,0:T(8,128)(2,1)}, bf16[256,512]{1,0:T(8,128)(2,1)S(1)}, u32[]{:S(2)}, u32[]{:S(2)}) %collective-permute-start.8) | collective-permute-done | bytes 262176 | tf_op jit(solution)/shard_map/ppermute | solution.py:57
  28.8 0.1 settle.1.refs_0_
  28.9 0.1 collective-permute-start.9
  29.0 1.3 %collective-permute-start.15 = (bf16[256,512]{1,0:T(8,128)(2,1)S(1)}, bf16[256,512]{1,0:T(8,128)(2,1)S(1)}, u32[]{:S(2)}, u32[]{:S(2)}) collective-permute-start(bf16[256,512]{1,0:T(8,128)(2,1)S(1)} %collective-permute-done.7.refs_4_.refs_3_), channel_id=1, source_target_pairs={{8,0},{16,24},{9,1},{17,25},{10,2},{18,26},{11,3},{19,27},{12,4},{... | collective-permute-start | bytes 786440 | tf_op jit(solution)/shard_map/ppermute | solution.py:58
  30.3 0.6 collective-permute-done.9.refs_1_
  30.9 1.9 %copy-done.6 = bf16[2,1024,768]{2,1,0:T(8,128)(2,1)S(1)} copy-done((bf16[2,1024,768]{2,1,0:T(8,128)(2,1)S(1)}, bf16[2,1024,768]{2,1,0:T(8,128)(2,1)}, u32[]{:S(2)}) %copy-start.6) | copy-done | bytes 3145752
  32.8 3.4 %experts.1 = (bf16[256,1536]{1,0:T(8,128)(2,1)S(1)}, bf16[128,1024]{1,0:T(8,128)(2,1)S(1)}, bf16[128,1024]{1,0:T(8,128)(2,1)S(1)}) custom-call(bf16[272,1024]{1,0:T(8,128)(2,1)S(1)} %settle.1.refs_0_, bf16[272,1024]{1,0:T(8,128)(2,1)S(1)} %collective-permute-done.9.refs_1_, bf16[2,1024,768]{2,1,0:T(8,128)(2,1)S(1)} %copy-done.6, ...), custom_call_target="tpu_custom_call" | custom-call | flops 2415919104 | bytes 1048576 | tf_op jit(solution)/shard_map/experts/pallas_call | solution.py:35
  36.3 0.2 collective-permute-start.14
  36.5 1.0 %outputs.1 = (bf16[128,1024]{1,0:T(8,128)(2,1)S(1)}, bf16[128,1024]{1,0:T(8,128)(2,1)S(1)}) custom-call(bf16[256,1536]{1,0:T(8,128)(2,1)S(1)} %get-tuple-element.32.refs_0_, bf16[2,768,1024]{2,1,0:T(8,128)(2,1)S(1)} %copy-done.2), custom_call_target="tpu_custom_call" | custom-call | flops 805306368 | bytes 1048576 | tf_op jit(solution)/shard_map/outputs/pallas_call | solution.py:35
  37.5 0.4 collective-permute-start.10
  37.9 1.7 %collective-permute-done.15.refs_2_.refs_5_ = bf16[256,512]{1,0:T(8,128)(2,1)S(1)} collective-permute-done((bf16[256,512]{1,0:T(8,128)(2,1)S(1)}, bf16[256,512]{1,0:T(8,128)(2,1)S(1)}, u32[]{:S(2)}, u32[]{:S(2)}) %collective-permute-start.15) | collective-permute-done | bytes 262176 | tf_op jit(solution)/shard_map/ppermute | solution.py:58
  39.6 0.1 pieces.3
  39.7 1.0 %collective-permute-start.16 = (bf16[32,1024]{1,0:T(8,128)(2,1)S(1)}, bf16[32,1024]{1,0:T(8,128)(2,1)S(1)}, u32[]{:S(2)}, u32[]{:S(2)}) collective-permute-start(bf16[32,1024]{1,0:T(8,128)(2,1)S(1)} %get-tuple-element.42), channel_id=1, source_target_pairs={{0,2},{1,3},{2,0},{3,1},{4,6},{5,7},{6,4},{7,5},{8,10},{9,11},{10,... | collective-permute-start | bytes 196616 | tf_op jit(solution)/shard_map/ppermute | solution.py:49
  40.6 0.9 %collective-permute-start.17 = (bf16[32,1024]{1,0:T(8,128)(2,1)S(1)}, bf16[32,1024]{1,0:T(8,128)(2,1)S(1)}, u32[]{:S(2)}, u32[]{:S(2)}) collective-permute-start(bf16[32,1024]{1,0:T(8,128)(2,1)S(1)} %get-tuple-element.43), channel_id=1, source_target_pairs={{0,4},{1,5},{2,6},{3,7},{4,0},{5,1},{6,2},{7,3},{8,12},{9,13},{10,... | collective-permute-start | bytes 196616 | tf_op jit(solution)/shard_map/ppermute | solution.py:49
  41.6 1.6 %collective-permute-start.18 = (bf16[32,1024]{1,0:T(8,128)(2,1)S(1)}, bf16[32,1024]{1,0:T(8,128)(2,1)S(1)}, u32[]{:S(2)}, u32[]{:S(2)}) collective-permute-start(bf16[32,1024]{1,0:T(8,128)(2,1)S(1)} %get-tuple-element.44), channel_id=1, source_target_pairs={{0,6},{1,7},{2,4},{3,5},{4,2},{5,3},{6,0},{7,1},{8,14},{9,15},{10,... | collective-permute-start | bytes 196616 | tf_op jit(solution)/shard_map/ppermute | solution.py:49
  43.2 0.1 pieces.2
  43.3 1.0 %collective-permute-start.11 = (bf16[32,1024]{1,0:T(8,128)(2,1)S(1)}, bf16[32,1024]{1,0:T(8,128)(2,1)S(1)}, u32[]{:S(2)}, u32[]{:S(2)}) collective-permute-start(bf16[32,1024]{1,0:T(8,128)(2,1)S(1)} %get-tuple-element.36), channel_id=1, source_target_pairs={{0,2},{1,3},{2,0},{3,1},{4,6},{5,7},{6,4},{7,5},{8,10},{9,11},{10,... | collective-permute-start | bytes 196616 | tf_op jit(solution)/shard_map/ppermute | solution.py:49
  44.3 0.9 %collective-permute-start.12 = (bf16[32,1024]{1,0:T(8,128)(2,1)S(1)}, bf16[32,1024]{1,0:T(8,128)(2,1)S(1)}, u32[]{:S(2)}, u32[]{:S(2)}) collective-permute-start(bf16[32,1024]{1,0:T(8,128)(2,1)S(1)} %get-tuple-element.37), channel_id=1, source_target_pairs={{0,4},{1,5},{2,6},{3,7},{4,0},{5,1},{6,2},{7,3},{8,12},{9,13},{10,... | collective-permute-start | bytes 196616 | tf_op jit(solution)/shard_map/ppermute | solution.py:49
  45.2 1.6 %collective-permute-start.13 = (bf16[32,1024]{1,0:T(8,128)(2,1)S(1)}, bf16[32,1024]{1,0:T(8,128)(2,1)S(1)}, u32[]{:S(2)}, u32[]{:S(2)}) collective-permute-start(bf16[32,1024]{1,0:T(8,128)(2,1)S(1)} %get-tuple-element.38), channel_id=1, source_target_pairs={{0,6},{1,7},{2,4},{3,5},{4,2},{5,3},{6,0},{7,1},{8,14},{9,15},{10,... | collective-permute-start | bytes 196616 | tf_op jit(solution)/shard_map/ppermute | solution.py:49
  46.9 2.7 %collective-permute-start.21 = (bf16[32,1024]{1,0:T(8,128)(2,1)S(1)}, bf16[32,1024]{1,0:T(8,128)(2,1)S(1)}, u32[]{:S(2)}, u32[]{:S(2)}) collective-permute-start(bf16[32,1024]{1,0:T(8,128)(2,1)S(1)} %get-tuple-element.50), channel_id=1, source_target_pairs={{0,24},{8,16},{16,8},{24,0},{1,25},{9,17},{17,9},{25,1},{2,26},{10... | collective-permute-start | bytes 196616 | tf_op jit(solution)/shard_map/ppermute | solution.py:49
  49.6 1.8 %collective-permute-start.19 = (bf16[32,1024]{1,0:T(8,128)(2,1)S(1)}, bf16[32,1024]{1,0:T(8,128)(2,1)S(1)}, u32[]{:S(2)}, u32[]{:S(2)}) collective-permute-start(bf16[32,1024]{1,0:T(8,128)(2,1)S(1)} %get-tuple-element.50), channel_id=1, source_target_pairs={{0,8},{8,0},{16,24},{24,16},{1,9},{9,1},{17,25},{25,17},{2,10},{10... | collective-permute-start | bytes 196616 | tf_op jit(solution)/shard_map/ppermute | solution.py:49
  51.4 0.7 add_convert_fusion.1
  52.0 1.4 %collective-permute-done.21 = bf16[32,1024]{1,0:T(8,128)(2,1)S(1)} collective-permute-done((bf16[32,1024]{1,0:T(8,128)(2,1)S(1)}, bf16[32,1024]{1,0:T(8,128)(2,1)S(1)}, u32[]{:S(2)}, u32[]{:S(2)}) %collective-permute-start.21) | collective-permute-done | bytes 65568 | tf_op jit(solution)/shard_map/ppermute | solution.py:49
  53.4 1.4 %collective-permute-done.20 = bf16[32,1024]{1,0:T(8,128)(2,1)S(1)} collective-permute-done((bf16[32,1024]{1,0:T(8,128)(2,1)S(1)}, bf16[32,1024]{1,0:T(8,128)(2,1)S(1)}, u32[]{:S(2)}, u32[]{:S(2)}) %collective-permute-start.20) | collective-permute-done | bytes 65568 | tf_op jit(solution)/shard_map/ppermute | solution.py:49
  54.8 1.7 %collective-permute-start.27 = (bf16[128,1024]{1,0:T(8,128)(2,1)S(1)}, bf16[128,1024]{1,0:T(8,128)(2,1)S(1)}, u32[]{:S(2)}, u32[]{:S(2)}) collective-permute-start(bf16[128,1024]{1,0:T(8,128)(2,1)S(1)} %pad_maximum_fusion.refs_0_.refs_6_), channel_id=1, source_target_pairs={{0,6},{1,7},{2,4},{3,5},{4,2},{5,3},{6,0},{7,1},{8,14},{9,15},{10,... | collective-permute-start | bytes 786440 | tf_op jit(solution)/shard_map/ppermute | solution.py:49
  56.5 0.5 collective-permute-start.25
  57.0 1.4 %collective-permute-start.23 = (bf16[128,1024]{1,0:T(8,128)(2,1)S(1)}, bf16[128,1024]{1,0:T(8,128)(2,1)S(1)}, u32[]{:S(2)}, u32[]{:S(2)}) collective-permute-start(bf16[128,1024]{1,0:T(8,128)(2,1)S(1)} %pad_maximum_fusion.refs_0_.refs_6_), channel_id=1, source_target_pairs={{0,2},{1,3},{2,0},{3,1},{4,6},{5,7},{6,4},{7,5},{8,10},{9,11},{10,... | collective-permute-start | bytes 786440 | tf_op jit(solution)/shard_map/ppermute | solution.py:49
  58.4 1.1 %arrange.1 = (bf16[256,512]{1,0:T(8,128)(2,1)S(1)}, bf16[256,512]{1,0:T(8,128)(2,1)S(1)}, bf16[256,512]{1,0:T(8,128)(2,1)S(1)}, bf16[256,512]{1,0:T(8,128)(2,1)S(1)}) custom-call(bf16[256,512]{1,0:T(8,128)(2,1)} %refs_0_.3, bf16[256,512]{1,0:T(8,128)(2,1)S(1)} %collective-permute-done.3.refs_4_.refs_1_, ...), custom_call_target="tpu_custom_call" | custom-call | bytes 1048576 | tf_op jit(solution)/shard_map/arrange/pallas_call | solution.py:35
  59.5 4.7 %collective-permute-done.27.refs_6_ = bf16[128,1024]{1,0:T(8,128)(2,1)S(1)} collective-permute-done((bf16[128,1024]{1,0:T(8,128)(2,1)S(1)}, bf16[128,1024]{1,0:T(8,128)(2,1)S(1)}, u32[]{:S(2)}, u32[]{:S(2)}) %collective-permute-start.27) | collective-permute-done | bytes 262176 | tf_op jit(solution)/shard_map/ppermute | solution.py:49
  64.3 2.7 %collective-permute-done.25.refs_4_ = bf16[128,1024]{1,0:T(8,128)(2,1)S(1)} collective-permute-done((bf16[128,1024]{1,0:T(8,128)(2,1)S(1)}, bf16[128,1024]{1,0:T(8,128)(2,1)S(1)}, u32[]{:S(2)}, u32[]{:S(2)}) %collective-permute-start.25) | collective-permute-done | bytes 262176 | tf_op jit(solution)/shard_map/ppermute | solution.py:49
  66.9 0.0 collective-permute-done.23.refs_2_
  67.0 0.5 collective-permute-start.24
  67.5 0.5 fusion.17
  67.9 0.0 copy-start.1
  68.0 0.5 collective-permute-done.26.refs_5_
  68.5 0.5 fusion.4
  69.0 0.2 copy-done.1
  69.2 1.2 %input_grads.1 = bf16[256,512]{1,0:T(8,128)(2,1)} custom-call(bf16[128,1024]{1,0:T(8,128)(2,1)S(1)} %pad_maximum_fusion.refs_0_.refs_6_, bf16[128,1024]{1,0:T(8,128)(2,1)S(1)} %collective-permute-done.22.refs_1_, bf16[128,1024]{1,0:T(8,128)(2,1)S(1)} %collective-permute-done.23.refs_2_, bf16[128,1024]{1,0:T(8,128)(2,1)S(1)} %collective-permute-done.24.refs_3_, ...), custom_call_target="tpu_custom_call" | custom-call | flops 268435456 | bytes 1048576 | tf_op jit(solution)/shard_map/input_grads/pallas_call | solution.py:35
  70.4 0.5 fusion
  70.8 1.8 %add_add_fusion = f32[512,1024]{1,0:T(8,128)} fusion(f32[512,1024]{1,0:T(8,128)S(1)} %fusion.4, f32[512,1024]{1,0:T(8,128)S(1)} %fusion.17, f32[512,1024]{1,0:T(8,128)S(1)} %fusion, bf16[256,512]{1,0:T(8,128)(2,1)S(1)} %get-tuple-element.48, bf16[128,1024]{1,0:T(8,128)(2,1)S(1)} %collective-permute-done.28.refs_7_, ...), kind=kOutput, calls=%fused_computation | convolution fusion | flops 271056896 | bytes 9175040 | tf_op jit(solution)/shard_map/dot_general | solution.py:19
  (32 shorter events, 0.2 us)
Async XLA Ops:
  0.6 1.2 %copy-start = (bf16[512,1024]{1,0:T(8,128)(2,1)S(1)}, bf16[512,1024]{1,0:T(8,128)(2,1)}, u32[]{:S(2)}) copy-start(bf16[512,1024]{1,0:T(8,128)(2,1)} %refs_8_.1) | copy-start | bytes 3145732
  3.8 0.7 copy-start.3
  4.5 26.4 %copy-start.2 = (bf16[2,768,1024]{2,1,0:T(8,128)(2,1)S(1)}, bf16[2,768,1024]{2,1,0:T(8,128)(2,1)}, u32[]{:S(2)}) copy-start(bf16[2,768,1024]{2,1,0:T(8,128)(2,1)} %refs_1_.3) | copy-start | bytes 9437188
  4.5 5.3 %collective-permute-start = (bf16[128,1024]{1,0:T(8,128)(2,1)}, bf16[128,1024]{1,0:T(8,128)(2,1)}, u32[]{:S(2)}, u32[]{:S(2)}) collective-permute-start(bf16[128,1024]{1,0:T(8,128)(2,1)} %get-tuple-element.27), channel_id=1, source_target_pairs={{0,1},{1,0},{2,3},{3,2},{4,5},{5,4},{6,7},{7,6},{8,9},{9,8},{10,11... | collective-permute-start | bytes 786440 | tf_op jit(solution)/shard_map/ppermute | solution.py:49
  5.0 10.8 %collective-permute-start.3 = (bf16[256,512]{1,0:T(8,128)(2,1)}, bf16[256,512]{1,0:T(8,128)(2,1)S(1)}, u32[]{:S(2)}, u32[]{:S(2)}) collective-permute-start(bf16[256,512]{1,0:T(8,128)(2,1)} %refs_0_.3), channel_id=1, source_target_pairs={{0,8},{8,0},{16,24},{24,16},{1,9},{9,1},{17,25},{25,17},{2,10},{10... | collective-permute-start | bytes 786440 | tf_op jit(solution)/shard_map/ppermute | solution.py:49
  7.6 8.9 %collective-permute-start.4 = (bf16[256,512]{1,0:T(8,128)(2,1)}, bf16[256,512]{1,0:T(8,128)(2,1)}, u32[]{:S(2)}, u32[]{:S(2)}) collective-permute-start(bf16[256,512]{1,0:T(8,128)(2,1)} %refs_0_.3), channel_id=1, source_target_pairs={{8,16},{16,8},{9,17},{17,9},{10,18},{18,10},{11,19},{19,11},{12,20... | collective-permute-start | bytes 786440 | tf_op jit(solution)/shard_map/ppermute | solution.py:55
  9.9 1.0 %copy-start.4 = (bf16[128,1024]{1,0:T(8,128)(2,1)S(1)}, bf16[128,1024]{1,0:T(8,128)(2,1)}, u32[]{:S(2)}) copy-start(bf16[128,1024]{1,0:T(8,128)(2,1)} %copy-done.3) | copy-start | bytes 786436
  10.8 0.8 %copy-start.5 = (bf16[32,1024]{1,0:T(8,128)(2,1)S(1)}, bf16[32,1024]{1,0:T(8,128)(2,1)}, u32[]{:S(2)}) copy-start(bf16[32,1024]{1,0:T(8,128)(2,1)} %refs_2_.2) | copy-start | bytes 196612
  12.7 7.7 %collective-permute-start.1 = (bf16[96,1024]{1,0:T(8,128)(2,1)S(1)}, bf16[96,1024]{1,0:T(8,128)(2,1)S(1)}, u32[]{:S(2)}, u32[]{:S(2)}) collective-permute-start(bf16[96,1024]{1,0:T(8,128)(2,1)S(1)} %get-tuple-element.28.refs_0_), channel_id=1, source_target_pairs={{0,2},{1,3},{2,0},{3,1},{4,6},{5,7},{6,4},{7,5},{8,10},{9,11},{10,... | collective-permute-start | bytes 589832 | tf_op jit(solution)/shard_map/ppermute | solution.py:49
  14.3 6.1 %collective-permute-start.2 = (bf16[80,1024]{1,0:T(8,128)(2,1)S(1)}, bf16[80,1024]{1,0:T(8,128)(2,1)S(1)}, u32[]{:S(2)}, u32[]{:S(2)}) collective-permute-start(bf16[80,1024]{1,0:T(8,128)(2,1)S(1)} %get-tuple-element.29.refs_1_), channel_id=1, source_target_pairs={{0,4},{1,5},{2,6},{3,7},{4,0},{5,1},{6,2},{7,3},{8,12},{9,13},{10,... | collective-permute-start | bytes 491528 | tf_op jit(solution)/shard_map/ppermute | solution.py:49
  15.8 7.2 %collective-permute-start.7 = (bf16[256,512]{1,0:T(8,128)(2,1)S(1)}, bf16[256,512]{1,0:T(8,128)(2,1)S(1)}, u32[]{:S(2)}, u32[]{:S(2)}) collective-permute-start(bf16[256,512]{1,0:T(8,128)(2,1)S(1)} %collective-permute-done.3.refs_4_.refs_1_), channel_id=1, source_target_pairs={{8,16},{16,8},{9,17},{17,9},{10,18},{18,10},{11,19},{19,11},{12,20... | collective-permute-start | bytes 786440 | tf_op jit(solution)/shard_map/ppermute | solution.py:56
  16.5 12.3 %collective-permute-start.8 = (bf16[256,512]{1,0:T(8,128)(2,1)}, bf16[256,512]{1,0:T(8,128)(2,1)S(1)}, u32[]{:S(2)}, u32[]{:S(2)}) collective-permute-start(bf16[256,512]{1,0:T(8,128)(2,1)} %collective-permute-done.4.refs_5_.refs_2_), channel_id=1, source_target_pairs={{8,0},{16,24},{9,1},{17,25},{10,2},{18,26},{11,3},{19,27},{12,4},{... | collective-permute-start | bytes 786440 | tf_op jit(solution)/shard_map/ppermute | solution.py:57
  20.4 8.4 %collective-permute-start.5 = (bf16[112,1024]{1,0:T(8,128)(2,1)S(1)}, bf16[112,1024]{1,0:T(8,128)(2,1)S(1)}, u32[]{:S(2)}, u32[]{:S(2)}) collective-permute-start(bf16[112,1024]{1,0:T(8,128)(2,1)S(1)} %get-tuple-element.30.refs_0_), channel_id=1, source_target_pairs={{0,4},{1,5},{2,6},{3,7},{4,0},{5,1},{6,2},{7,3},{8,12},{9,13},{10,... | collective-permute-start | bytes 688136 | tf_op jit(solution)/shard_map/ppermute | solution.py:49
  22.0 6.8 %collective-permute-start.6 = (bf16[96,1024]{1,0:T(8,128)(2,1)S(1)}, bf16[96,1024]{1,0:T(8,128)(2,1)S(1)}, u32[]{:S(2)}, u32[]{:S(2)}) collective-permute-start(bf16[96,1024]{1,0:T(8,128)(2,1)S(1)} %get-tuple-element.31.refs_1_), channel_id=1, source_target_pairs={{0,2},{1,3},{2,0},{3,1},{4,6},{5,7},{6,4},{7,5},{8,10},{9,11},{10,... | collective-permute-start | bytes 589832 | tf_op jit(solution)/shard_map/ppermute | solution.py:49
  28.9 2.0 %collective-permute-start.9 = (bf16[272,1024]{1,0:T(8,128)(2,1)S(1)}, bf16[272,1024]{1,0:T(8,128)(2,1)S(1)}, u32[]{:S(2)}, u32[]{:S(2)}) collective-permute-start(bf16[272,1024]{1,0:T(8,128)(2,1)S(1)} %settle.1.refs_0_), channel_id=1, source_target_pairs={{0,1},{1,0},{2,3},{3,2},{4,5},{5,4},{6,7},{7,6},{8,9},{9,8},{10,11... | collective-permute-start | bytes 1671176 | tf_op jit(solution)/shard_map/ppermute | solution.py:49
  29.0 10.6 %collective-permute-start.15 = (bf16[256,512]{1,0:T(8,128)(2,1)S(1)}, bf16[256,512]{1,0:T(8,128)(2,1)S(1)}, u32[]{:S(2)}, u32[]{:S(2)}) collective-permute-start(bf16[256,512]{1,0:T(8,128)(2,1)S(1)} %collective-permute-done.7.refs_4_.refs_3_), channel_id=1, source_target_pairs={{8,0},{16,24},{9,1},{17,25},{10,2},{18,26},{11,3},{19,27},{12,4},{... | collective-permute-start | bytes 786440 | tf_op jit(solution)/shard_map/ppermute | solution.py:58
  30.9 1.9 %copy-start.6 = (bf16[2,1024,768]{2,1,0:T(8,128)(2,1)S(1)}, bf16[2,1024,768]{2,1,0:T(8,128)(2,1)}, u32[]{:S(2)}) copy-start(bf16[2,1024,768]{2,1,0:T(8,128)(2,1)} %refs_2_.3) | copy-start | bytes 9437188
  36.3 3.3 %collective-permute-start.14 = (bf16[128,1024]{1,0:T(8,128)(2,1)S(1)}, bf16[128,1024]{1,0:T(8,128)(2,1)S(1)}, u32[]{:S(2)}, u32[]{:S(2)}) collective-permute-start(bf16[128,1024]{1,0:T(8,128)(2,1)S(1)} %get-tuple-element.40), channel_id=1, source_target_pairs={{0,1},{1,0},{2,3},{3,2},{4,5},{5,4},{6,7},{7,6},{8,9},{9,8},{10,11... | collective-permute-start | bytes 786440 | tf_op jit(solution)/shard_map/ppermute | solution.py:49
  37.5 5.8 %collective-permute-start.10 = (bf16[128,1024]{1,0:T(8,128)(2,1)S(1)}, bf16[128,1024]{1,0:T(8,128)(2,1)S(1)}, u32[]{:S(2)}, u32[]{:S(2)}) collective-permute-start(bf16[128,1024]{1,0:T(8,128)(2,1)S(1)} %get-tuple-element.34), channel_id=1, source_target_pairs={{0,1},{1,0},{2,3},{3,2},{4,5},{5,4},{6,7},{7,6},{8,9},{9,8},{10,11... | collective-permute-start | bytes 786440 | tf_op jit(solution)/shard_map/ppermute | solution.py:49
  39.7 5.5 %collective-permute-start.16 = (bf16[32,1024]{1,0:T(8,128)(2,1)S(1)}, bf16[32,1024]{1,0:T(8,128)(2,1)S(1)}, u32[]{:S(2)}, u32[]{:S(2)}) collective-permute-start(bf16[32,1024]{1,0:T(8,128)(2,1)S(1)} %get-tuple-element.42), channel_id=1, source_target_pairs={{0,2},{1,3},{2,0},{3,1},{4,6},{5,7},{6,4},{7,5},{8,10},{9,11},{10,... | collective-permute-start | bytes 196616 | tf_op jit(solution)/shard_map/ppermute | solution.py:49
  40.6 6.2 %collective-permute-start.17 = (bf16[32,1024]{1,0:T(8,128)(2,1)S(1)}, bf16[32,1024]{1,0:T(8,128)(2,1)S(1)}, u32[]{:S(2)}, u32[]{:S(2)}) collective-permute-start(bf16[32,1024]{1,0:T(8,128)(2,1)S(1)} %get-tuple-element.43), channel_id=1, source_target_pairs={{0,4},{1,5},{2,6},{3,7},{4,0},{5,1},{6,2},{7,3},{8,12},{9,13},{10,... | collective-permute-start | bytes 196616 | tf_op jit(solution)/shard_map/ppermute | solution.py:49
  41.6 5.3 %collective-permute-start.18 = (bf16[32,1024]{1,0:T(8,128)(2,1)S(1)}, bf16[32,1024]{1,0:T(8,128)(2,1)S(1)}, u32[]{:S(2)}, u32[]{:S(2)}) collective-permute-start(bf16[32,1024]{1,0:T(8,128)(2,1)S(1)} %get-tuple-element.44), channel_id=1, source_target_pairs={{0,6},{1,7},{2,4},{3,5},{4,2},{5,3},{6,0},{7,1},{8,14},{9,15},{10,... | collective-permute-start | bytes 196616 | tf_op jit(solution)/shard_map/ppermute | solution.py:49
  43.3 6.3 %collective-permute-start.11 = (bf16[32,1024]{1,0:T(8,128)(2,1)S(1)}, bf16[32,1024]{1,0:T(8,128)(2,1)S(1)}, u32[]{:S(2)}, u32[]{:S(2)}) collective-permute-start(bf16[32,1024]{1,0:T(8,128)(2,1)S(1)} %get-tuple-element.36), channel_id=1, source_target_pairs={{0,2},{1,3},{2,0},{3,1},{4,6},{5,7},{6,4},{7,5},{8,10},{9,11},{10,... | collective-permute-start | bytes 196616 | tf_op jit(solution)/shard_map/ppermute | solution.py:49
  44.3 7.1 %collective-permute-start.12 = (bf16[32,1024]{1,0:T(8,128)(2,1)S(1)}, bf16[32,1024]{1,0:T(8,128)(2,1)S(1)}, u32[]{:S(2)}, u32[]{:S(2)}) collective-permute-start(bf16[32,1024]{1,0:T(8,128)(2,1)S(1)} %get-tuple-element.37), channel_id=1, source_target_pairs={{0,4},{1,5},{2,6},{3,7},{4,0},{5,1},{6,2},{7,3},{8,12},{9,13},{10,... | collective-permute-start | bytes 196616 | tf_op jit(solution)/shard_map/ppermute | solution.py:49
  45.2 6.2 %collective-permute-start.13 = (bf16[32,1024]{1,0:T(8,128)(2,1)S(1)}, bf16[32,1024]{1,0:T(8,128)(2,1)S(1)}, u32[]{:S(2)}, u32[]{:S(2)}) collective-permute-start(bf16[32,1024]{1,0:T(8,128)(2,1)S(1)} %get-tuple-element.38), channel_id=1, source_target_pairs={{0,6},{1,7},{2,4},{3,5},{4,2},{5,3},{6,0},{7,1},{8,14},{9,15},{10,... | collective-permute-start | bytes 196616 | tf_op jit(solution)/shard_map/ppermute | solution.py:49
  46.9 6.5 %collective-permute-start.21 = (bf16[32,1024]{1,0:T(8,128)(2,1)S(1)}, bf16[32,1024]{1,0:T(8,128)(2,1)S(1)}, u32[]{:S(2)}, u32[]{:S(2)}) collective-permute-start(bf16[32,1024]{1,0:T(8,128)(2,1)S(1)} %get-tuple-element.50), channel_id=1, source_target_pairs={{0,24},{8,16},{16,8},{24,0},{1,25},{9,17},{17,9},{25,1},{2,26},{10... | collective-permute-start | bytes 196616 | tf_op jit(solution)/shard_map/ppermute | solution.py:49
  49.6 5.2 %collective-permute-start.20 = (bf16[32,1024]{1,0:T(8,128)(2,1)S(1)}, bf16[32,1024]{1,0:T(8,128)(2,1)S(1)}, u32[]{:S(2)}, u32[]{:S(2)}) collective-permute-start(bf16[32,1024]{1,0:T(8,128)(2,1)S(1)} %get-tuple-element.50), channel_id=1, source_target_pairs={{0,16},{8,24},{16,0},{24,8},{1,17},{9,25},{17,1},{25,9},{2,18},{10... | collective-permute-start | bytes 196616 | tf_op jit(solution)/shard_map/ppermute | solution.py:49
  49.6 5.2 %collective-permute-start.19 = (bf16[32,1024]{1,0:T(8,128)(2,1)S(1)}, bf16[32,1024]{1,0:T(8,128)(2,1)S(1)}, u32[]{:S(2)}, u32[]{:S(2)}) collective-permute-start(bf16[32,1024]{1,0:T(8,128)(2,1)S(1)} %get-tuple-element.50), channel_id=1, source_target_pairs={{0,8},{8,0},{16,24},{24,16},{1,9},{9,1},{17,25},{25,17},{2,10},{10... | collective-permute-start | bytes 196616 | tf_op jit(solution)/shard_map/ppermute | solution.py:49
  54.8 9.4 %collective-permute-start.27 = (bf16[128,1024]{1,0:T(8,128)(2,1)S(1)}, bf16[128,1024]{1,0:T(8,128)(2,1)S(1)}, u32[]{:S(2)}, u32[]{:S(2)}) collective-permute-start(bf16[128,1024]{1,0:T(8,128)(2,1)S(1)} %pad_maximum_fusion.refs_0_.refs_6_), channel_id=1, source_target_pairs={{0,6},{1,7},{2,4},{3,5},{4,2},{5,3},{6,0},{7,1},{8,14},{9,15},{10,... | collective-permute-start | bytes 786440 | tf_op jit(solution)/shard_map/ppermute | solution.py:49
  56.5 10.4 %collective-permute-start.25 = (bf16[128,1024]{1,0:T(8,128)(2,1)S(1)}, bf16[128,1024]{1,0:T(8,128)(2,1)S(1)}, u32[]{:S(2)}, u32[]{:S(2)}) collective-permute-start(bf16[128,1024]{1,0:T(8,128)(2,1)S(1)} %pad_maximum_fusion.refs_0_.refs_6_), channel_id=1, source_target_pairs={{0,4},{1,5},{2,6},{3,7},{4,0},{5,1},{6,2},{7,3},{8,12},{9,13},{10,... | collective-permute-start | bytes 786440 | tf_op jit(solution)/shard_map/ppermute | solution.py:49
  57.0 10.0 %collective-permute-start.23 = (bf16[128,1024]{1,0:T(8,128)(2,1)S(1)}, bf16[128,1024]{1,0:T(8,128)(2,1)S(1)}, u32[]{:S(2)}, u32[]{:S(2)}) collective-permute-start(bf16[128,1024]{1,0:T(8,128)(2,1)S(1)} %pad_maximum_fusion.refs_0_.refs_6_), channel_id=1, source_target_pairs={{0,2},{1,3},{2,0},{3,1},{4,6},{5,7},{6,4},{7,5},{8,10},{9,11},{10,... | collective-permute-start | bytes 786440 | tf_op jit(solution)/shard_map/ppermute | solution.py:49
  58.4 9.1 %collective-permute-start.22 = (bf16[128,1024]{1,0:T(8,128)(2,1)S(1)}, bf16[128,1024]{1,0:T(8,128)(2,1)S(1)}, u32[]{:S(2)}, u32[]{:S(2)}) collective-permute-start(bf16[128,1024]{1,0:T(8,128)(2,1)S(1)} %pad_maximum_fusion.refs_0_.refs_6_), channel_id=1, source_target_pairs={{0,1},{1,0},{2,3},{3,2},{4,5},{5,4},{6,7},{7,6},{8,9},{9,8},{10,11... | collective-permute-start | bytes 786440 | tf_op jit(solution)/shard_map/ppermute | solution.py:49
  64.3 4.7 %collective-permute-start.28 = (bf16[128,1024]{1,0:T(8,128)(2,1)S(1)}, bf16[128,1024]{1,0:T(8,128)(2,1)S(1)}, u32[]{:S(2)}, u32[]{:S(2)}) collective-permute-start(bf16[128,1024]{1,0:T(8,128)(2,1)S(1)} %collective-permute-done.27.refs_6_), channel_id=1, source_target_pairs={{0,1},{1,0},{2,3},{3,2},{4,5},{5,4},{6,7},{7,6},{8,9},{9,8},{10,11... | collective-permute-start | bytes 786440 | tf_op jit(solution)/shard_map/ppermute | solution.py:49
  66.9 1.5 %collective-permute-start.26 = (bf16[128,1024]{1,0:T(8,128)(2,1)S(1)}, bf16[128,1024]{1,0:T(8,128)(2,1)S(1)}, u32[]{:S(2)}, u32[]{:S(2)}) collective-permute-start(bf16[128,1024]{1,0:T(8,128)(2,1)S(1)} %collective-permute-done.25.refs_4_), channel_id=1, source_target_pairs={{0,1},{1,0},{2,3},{3,2},{4,5},{5,4},{6,7},{7,6},{8,9},{9,8},{10,11... | collective-permute-start | bytes 786440 | tf_op jit(solution)/shard_map/ppermute | solution.py:49
  67.0 2.0 %collective-permute-start.24 = (bf16[128,1024]{1,0:T(8,128)(2,1)S(1)}, bf16[128,1024]{1,0:T(8,128)(2,1)S(1)}, u32[]{:S(2)}, u32[]{:S(2)}) collective-permute-start(bf16[128,1024]{1,0:T(8,128)(2,1)S(1)} %collective-permute-done.23.refs_2_), channel_id=1, source_target_pairs={{0,1},{1,0},{2,3},{3,2},{4,5},{5,4},{6,7},{7,6},{8,9},{9,8},{10,11... | collective-permute-start | bytes 786440 | tf_op jit(solution)/shard_map/ppermute | solution.py:49
  67.9 1.2 %copy-start.1 = (bf16[512,1024]{1,0:T(8,128)(2,1)S(1)}, bf16[512,1024]{1,0:T(8,128)(2,1)}, u32[]{:S(2)}) copy-start(bf16[512,1024]{1,0:T(8,128)(2,1)} %refs_8_.1) | copy-start | bytes 3145732

commit v3 on v2

--- a/solution.py
+++ b/solution.py
@@ -27,15 +27,19 @@
     return (first.astype(F32) + second.astype(F32)).astype(BF16)
 
 
-def local(body, outs, args, name, scratch=(), limit=8, flops=0, ties=()):
+def local(body, outs, args, name, scratch=(), limit=8, flops=0, ties=(), pin=None):
+    single = not isinstance(outs, tuple)
+    spec = VMEM if pin is None else pl.BlockSpec(memory_space=pin)
+
     def kernel(*refs):
         body(*refs[: len(args)], *refs[len(args) + len(ties) :])
 
-    single = not isinstance(outs, tuple)
+    if pin is not None:
+        args = [pltpu.with_memory_space_constraint(value, pin) for value in args]
     return pl.pallas_call(
         kernel,
         out_shape=outs,
-        in_specs=[VMEM] * len(args) + [ANY] * len(ties),
+        in_specs=[spec] * len(args) + [ANY] * len(ties),
         out_specs=VMEM if single else tuple(VMEM for _ in outs),
         scratch_shapes=list(scratch),
         compiler_params=pltpu.CompilerParams(vmem_limit_bytes=limit * MIB),
@@ -44,19 +48,40 @@
     )(*args, *ties)
 
 
+def load(value):
+    def body(src, dst, sems):
+        copies = [
+            pltpu.make_async_copy(src.at[i], dst.at[i], sems.at[i]) for i in range(value.shape[0])
+        ]
+        for copy in copies:
+            copy.start()
+        for copy in copies:
+            copy.wait()
+
+    return local(
+        body,
+        pltpu.VMEM(value.shape, value.dtype),
+        (value,),
+        "load",
+        scratch=[pltpu.SemaphoreType.DMA((value.shape[0],))],
+        pin=pltpu.HBM,
+    )
+
+
 def xor_permute(value, axis, mask):
     size = lax.axis_size(axis)
     return lax.ppermute(value, axis, [(i, i ^ mask) for i in range(size)])
 
 
+INNER, OUTER = [(1, 2), (2, 1)], [(1, 0), (2, 3)]
+
+
 def line_gather(value, axis):
-    inner, outer = [(1, 2), (2, 1)], [(1, 0), (2, 3)]
     near = xor_permute(value, axis, 1)
-    middle = lax.ppermute(value, axis, inner)
-    middle_far = lax.ppermute(near, axis, inner)
-    edge = lax.ppermute(middle, axis, outer)
-    edge_far = lax.ppermute(middle_far, axis, outer)
-    return [(near, middle), (middle_far, edge), (edge_far,)]
+    middle = lax.ppermute(value, axis, INNER)
+    middle_far = lax.ppermute(near, axis, INNER)
+    edge = lax.ppermute(middle, axis, OUTER)
+    return [(near, middle), (middle_far, edge)]
 
 
 def hop(hops, index):
@@ -74,54 +99,72 @@
     return pl.ds(pl.multiple_of(index * rows, rows), rows)
 
 
-def project(x, in_proj, tok):
+def project(x, in_proj, out_grad, expert_ids, route_probs, all_experts):
     rows, features = x.shape
     width = in_proj.shape[1]
-    owners = rows // tok
-    half = rows // 2
-
-    def body(x_ref, proj_ref, other_ref, mine_ref, rows_ref):
+    tok, top = out_grad.shape[0], expert_ids.shape[1]
+    chips = rows // tok // 2
+    half, mid, cot = rows // 2, rows // 4, tok // 2
+
+    args = (x, in_proj, out_grad, expert_ids.T, route_probs.T)
+
+    def body(*refs):
+        other_ref, first_ref, second_ref, rows_ref = refs[5:9]
+        x_ref, proj_ref, grad_ref, ids_ref, probs_ref = refs[9:14]
+        copies = [
+            pltpu.make_async_copy(refs[i], refs[9 + i], refs[14].at[i]) for i in range(len(args))
+        ]
+        for copy in copies:
+            copy.start()
+        copies[0].wait()
         me = lax.axis_index("expert")
         core = me % 2
-        for chip in range(owners // 2):
-            place = pl.ds(chip * tok, tok)
-            rows_ref[place, :] = x_ref[block(2 * chip + 1 - core, tok), :]
+        for chip in range(chips):
+            rows_ref[pl.ds(chip * tok, tok), :] = x_ref[block(2 * chip + 1 - core, tok), :]
             rows_ref[pl.ds(half + chip * tok, tok), :] = x_ref[block(2 * chip + core, tok), :]
+        copies[1].wait()
         other_ref[...] = mxu(rows_ref[:half, :], proj_ref[...]).astype(BF16)
-        mine_ref[...] = mxu(rows_ref[half:, :], proj_ref[...]).astype(BF16)
+        mine = mxu(rows_ref[half:, :], proj_ref[...]).astype(BF16)
+        first_ref[:mid, :] = mine[:mid]
+        second_ref[:mid, :] = mine[mid:]
+        for copy in copies[2:]:
+            copy.wait()
+        names = lax.broadcasted_iota(jnp.int32, (all_experts, tok), 0)
+        table = jnp.zeros((all_experts, tok), F32)
+        for k in range(top):
+            table += jnp.where(names == ids_ref[k : k + 1, :], probs_ref[k : k + 1, :], 0.0)
+        token = lax.broadcasted_iota(jnp.int32, (tok, width), 0)
+        column = lax.broadcasted_iota(jnp.int32, (tok, width), 1)
+        place = jnp.where(column == token + (me // 2) * tok, 1.0, 0.0).astype(BF16)
+        first_ref[mid : mid + all_experts, :] = mxu(table.astype(BF16), place).astype(BF16)
+        first_ref[mid + all_experts :, :] = grad_ref[:cot, :]
+        second_ref[mid:, :] = grad_ref[cot:, :]
 
     return local(
         body,
-        (shape(half, width), shape(half, width)),
-        (x, in_proj),
+        (shape(half, width), shape(mid + all_experts + cot, width), shape(mid + cot, width)),
+        args,
         "project",
-        scratch=[pltpu.VMEM((rows, features), BF16)],
+        scratch=[pltpu.VMEM((rows, features), BF16)]
+        + [pltpu.VMEM(value.shape, value.dtype) for value in args]
+        + [pltpu.SemaphoreType.DMA((len(args),))],
+        pin=pltpu.HBM,
         flops=2 * rows * features * width,
     )
 
 
-def streams(part, got, out_grad, routing):
-    half, width = part.shape
-    tok = out_grad.shape[0]
-    experts = routing.shape[0]
-
-    def body(part_ref, got_ref, grad_ref, routing_ref, first_ref, second_ref):
-        mid, rows = half // 2, tok // 2
-        first_ref[:mid, :] = add_bf16(part_ref[:mid, :], got_ref[:mid, :])
-        first_ref[mid : mid + experts, :] = routing_ref[...]
-        first_ref[mid + experts :, :] = grad_ref[:rows, :]
-        second_ref[:mid, :] = add_bf16(part_ref[mid:, :], got_ref[mid:, :])
-        second_ref[mid:, :] = grad_ref[rows:, :]
-
-    return local(
-        body,
-        (shape(half // 2 + experts + tok // 2, width), shape(half // 2 + tok // 2, width)),
-        (part, got, out_grad, routing),
-        "streams",
-    )
-
-
-def merge(sent, got, sums, flops=0, ties=()):
+def streams(sent, got, ties=()):
+    mid = got.shape[0] // 2
+
+    def body(first_ref, second_ref, got_ref, first_out, second_out):
+        for i, (src, dst) in enumerate(((first_ref, first_out), (second_ref, second_out))):
+            dst[:mid, :] = add_bf16(src[:mid, :], got_ref[i * mid : (i + 1) * mid, :])
+            dst[mid:, :] = src[mid:, :]
+
+    return local(body, tuple(shape(*v.shape) for v in sent), tuple(sent) + (got,), "streams", ties=ties)
+
+
+def merge(sent, got, sums, ties=()):
     width = sent[0].shape[1]
     rows = [value.shape[0] for value in sent]
 
@@ -138,7 +181,6 @@
         tuple(shape(2 * r - s, width) for r, s in zip(rows, sums)),
         tuple(sent) + tuple(got),
         "merge",
-        flops=flops,
         ties=ties,
     )
 
@@ -242,29 +284,60 @@
     return local(body, tuple(shape(tok, width) for _ in range(chips)), (first, second), "pieces", ties=ties)
 
 
-def scatter_sum(pieces):
-    got = [xor_permute(pieces[k], "expert", 2 * k) for k in range(1, len(pieces))]
-    total = pieces[0].astype(F32)
-    for piece in got:
-        total = total + piece.astype(F32)
-    return total.astype(BF16)
-
-
-def input_grads(pieces, in_proj, tok):
+def scatter(pieces):
+    return [xor_permute(pieces[k], "expert", 2 * k) for k in range(1, len(pieces))]
+
+
+def add_pieces(pieces, start=0, ties=()):
+    rows, width = pieces[0].shape
+
+    def body(*refs):
+        total = refs[0][...].astype(F32)
+        for ref in refs[1:-1]:
+            total = total + ref[pl.ds(start, rows), :].astype(F32)
+        refs[-1][...] = total.astype(BF16)
+
+    return local(body, shape(rows, width), tuple(pieces), "add_pieces", ties=ties)
+
+
+def head(value, tails, ties=()):
+    rows, width = value.shape
+    count = len(tails)
+
+    def body(*refs):
+        for tail, out in zip(refs[1 : 1 + count], refs[1 + count :]):
+            out[pl.ds(0, rows), :] = refs[0][...]
+            out[pl.ds(rows, tail.shape[0]), :] = tail[...]
+
+    outs = tuple(shape(rows + tail.shape[0], width) for tail in tails)
+    return local(body, outs, (value, *tails), "head", ties=ties)
+
+
+def stack(values, rows, ties=(), flops=0):
+    width = values[0].shape[1]
+
+    def body(*refs):
+        for i, ref in enumerate(refs[:-1]):
+            refs[-1][pl.ds(i * rows, rows), :] = ref[pl.ds(0, rows), :]
+
+    return local(body, shape(len(values) * rows, width), tuple(values), "stack", ties=ties, flops=flops)
+
+
+def input_grads(near, twins, in_proj, tok):
     features, width = in_proj.shape
-    rows = len(pieces) * tok
-
-    def body(*refs):
-        piece_refs, (proj_ref, out_ref, rows_ref) = refs[: len(pieces)], refs[len(pieces) :]
+    rows = 2 * near.shape[0]
+
+    def body(near_ref, twins_ref, proj_ref, out_ref, rows_ref):
         me = lax.axis_index("expert")
-        for mask, piece_ref in enumerate(piece_refs):
-            rows_ref[block(me ^ mask, tok), :] = piece_ref[:tok, :]
+        for mask in range(rows // tok):
+            src = (near_ref, twins_ref)[mask % 2]
+            rows_ref[block(me ^ mask, tok), :] = src[pl.ds(mask // 2 * tok, tok), :]
         out_ref[...] = mxu(rows_ref[...], proj_ref[...], NT).astype(BF16)
 
     return local(
         body,
         shape(rows, features),
-        tuple(pieces) + (in_proj,),
+        (near, twins, in_proj),
         "input_grads",
         scratch=[pltpu.VMEM((rows, width), BF16)],
         limit=16,
@@ -307,6 +380,54 @@
 
     out = tuple(shape(2 * count * tok, features) for _ in range(chips))
     return local(body, out, sources, "arrange", ties=(tie,))
+
+
+def proj_round(x_rows, near, far, chip, tok, before, last):
+    rows, features = x_rows.shape
+    width = near[0].shape[1]
+    given = [x_rows, *near, *far] + ([] if before is None else [before])
+    steps = 4 if features % 512 == 0 else 1
+    tile = features // steps
+
+    def body(*refs):
+        x_ref = refs[0]
+        out_ref, rows_ref = refs[len(given)], refs[len(given) + 1]
+        for twin in range(2):
+            start = twin * (rows // 2)
+            rows_ref[pl.ds(start, tok), :] = refs[1 + twin][pl.ds(chip * tok, tok), :]
+            if far:
+                rows_ref[pl.ds(start + tok, rows // 2 - tok), :] = refs[3 + twin][...]
+        copies = []
+        for i in range(steps):
+            part = pl.ds(i * tile, tile)
+            total = mxu(x_ref[:, part], rows_ref[...], TN)
+            if before is not None:
+                total = total + refs[len(given) - 1][part, :]
+            if last:
+                whole_ref, sems = refs[len(given) + 2], refs[len(given) + 3]
+                whole_ref[part, :] = total
+                copies.append(pltpu.make_async_copy(whole_ref.at[part], out_ref.at[part], sems.at[i]))
+                copies[-1].start()
+            else:
+                out_ref[part, :] = total
+        for copy in copies:
+            copy.wait()
+
+    scratch = [pltpu.VMEM((rows, width), BF16)]
+    if last:
+        scratch += [pltpu.VMEM((features, width), F32), pltpu.SemaphoreType.DMA((steps,))]
+    return pl.pallas_call(
+        body,
+        out_shape=shape(features, width, F32),
+        in_specs=[VMEM] * len(given),
+        out_specs=ANY if last else VMEM,
+        scratch_shapes=scratch,
+        compiler_params=pltpu.CompilerParams(vmem_limit_bytes=16 * MIB),
+        cost_estimate=pl.CostEstimate(
+            flops=2 * rows * features * width, bytes_accessed=4 * MIB, transcendentals=0
+        ),
+        name="proj_round",
+    )(*given)
 
 
 def per_device(tokens_x, in_proj, up_weight, down_weight, expert_ids, route_probs, out_grad):
@@ -321,42 +442,55 @@
     bits = [1 << b for b in range(1, owners.bit_length() - 1)]
     gather_groups = groups == 4 and groups * owners * tok * width <= 1 << 22
 
-    chosen = expert_ids[None, :, :] == jnp.arange(all_experts, dtype=jnp.int32)[:, None, None]
-    routing = jnp.sum(jnp.where(chosen, route_probs[None, :, :], 0.0), axis=2).astype(BF16)
-    routing = lax.dynamic_update_slice(
-        jnp.zeros((all_experts, width), BF16), routing, (0, chip * tok)
-    )
-
-    part_other, part_mine = project(tokens_x, in_proj, tok)
-    got = xor_permute(part_other, "expert", 1)
-    sent = streams(part_mine, got, out_grad, routing)
+    part_other, *sent = project(tokens_x, in_proj, out_grad, expert_ids, route_probs, all_experts)
     sums = (half // 2 + all_experts, half // 2)
     hops = line_gather(tokens_x, "dp") if gather_groups else []
+    last = [lax.ppermute(hops[1][0], "dp", OUTER)] if hops else []
+    up, down = load(up_weight), load(down_weight)
+    sent = streams(sent, xor_permute(part_other, "expert", 1))
     for step, stream_bits in enumerate(zip(bits, bits[::-1])):
         got = [xor_permute(value, "expert", bit) for value, bit in zip(sent, stream_bits)]
         if step + 1 < len(bits):
-            sent = merge(sent, got, sums, ties=hop(hops, 0))
-    mine = settle(sent, got, (order_of(bits), order_of(bits[::-1])), tok, all_experts, ties=hop(hops, 1))
+            sent = merge(sent, got, sums)
+    mine = settle(sent, got, (order_of(bits), order_of(bits[::-1])), tok, all_experts, ties=(up, down, *hop(hops, 0)))
     other = xor_permute(mine, "expert", 1)
-    act, lat_mine, lat_other = experts(mine, other, up_weight, down_weight, half)
-    latent_grad = scatter_sum(pieces_of(lat_mine, xor_permute(lat_other, "expert", 1), chips, hop(hops, 2)))
-    out_mine, out_other = outputs(act, down_weight, half)
-    combined = scatter_sum(pieces_of(out_mine, xor_permute(out_other, "expert", 1), chips))
-
-    held = [latent_grad]
+
+    act, lat_mine, lat_other = experts(mine, other, up, down, half)
+    out_mine, out_other = outputs(act, down, half)
+    out_pieces = pieces_of(out_mine, xor_permute(out_other, "expert", 1), chips)
+    lat_pieces = pieces_of(lat_mine, xor_permute(lat_other, "expert", 1), chips)
+    got = scatter(lat_pieces)
+    latent_grad = add_pieces((lat_pieces[0], *got), ties=hop(hops, 1))
+
+    own = ()
     if gather_groups:
-        held += [xor_permute(latent_grad, "dp", m) for m in range(1, groups)]
-    own = jnp.concatenate(held, axis=0)
-    x_all = arrange(tokens_x, hops, chips, tok, own)
-    all_pieces = []
-    proj_grad = None
-    for k in range(chips):
-        piece = own if k == 0 else xor_permute(own, "expert", 2 * k)
-        twin = xor_permute(piece, "expert", 1)
-        all_pieces += [piece, twin]
-        term = mxu(x_all[k], jnp.concatenate([piece, twin], axis=0), TN)
-        proj_grad = term if proj_grad is None else proj_grad + term
-    input_grad = input_grads(all_pieces, in_proj, tok)
+        across = [xor_permute(latent_grad, "dp", m) for m in range(1, groups)]
+        own = stack(across, tok, ties=last)
+        hops.append(tuple(last))
+    after = (own,) if gather_groups else ()
+    sent = head(latent_grad, out_pieces[1:])
+    got = scatter([None, *sent])
+    combined = add_pieces((out_pieces[0], *got), tok, ties=after)
+    near = stack([latent_grad, *got], tok, ties=after)
+    split = near.shape[0] // 2
+    twins = [xor_permute(v, "expert", 1) for v in (near[:split], near[split:])]
+    twins = jnp.concatenate(twins, axis=0)
+    input_grad = input_grads(near, twins, in_proj, tok)
+    far = [() for _ in range(chips)]
+    x_all = arrange(tokens_x, hops, chips, tok, latent_grad)
+    order = [0] + list(range(chips - 1, 0, -1))
+    if gather_groups:
+        far[0] = (own, xor_permute(own, "expert", 1))
+    proj_grad = proj_round(x_all[0], (near, twins), far[0], 0, tok, None, False)
+    if gather_groups:
+        ties = (proj_grad, input_grad, combined)
+        for k in order[1:]:
+            piece = xor_permute(own, "expert", 2 * k)
+            relay = stack([piece], piece.shape[0], ties)
+            far[k] = (relay, xor_permute(relay, "expert", 1))
+            ties = ()
+    for k in order[1:]:
+        proj_grad = proj_round(x_all[k], (near, twins), far[k], k, tok, proj_grad, k == order[-1])
     if not gather_groups:
         proj_grad = lax.psum(proj_grad, "dp")
     return (combined, input_grad, proj_grad)

time: 73.1 us -> 69.9 us (0.956)
  local copies, waits for them, and re-layouts: 6.03 us -> 0.06 us
  Pallas kernels: 9.94 us -> 15.6 us
  matrix products: 3.16 us -> 0 us
  starting transfers between devices: 29.7 us -> 31.5 us
  other arithmetic: 1.46 us -> 0 us
    unnamed x17 -> x9, local copies, waits for them, and re-layouts: 5.83 us -> 0.03 us
    pallas_call x10 -> x24, Pallas kernels: 9.94 us -> 15.6 us  [the longest x20 12.6 us: local(): pl.pallas_call(kernel, out_shape=outs, in_specs=[spec] * len(args) + [ANY...]
    dot_general x4 -> x0, matrix products: 3.16 us -> none  [mxu(): return lax.dot_general(first, second, dims, preferred_element_type=F32)]
    ppermute x25 -> x27, waiting for transfers between devices: 14 us -> 16.5 us  [xor_permute(): return lax.ppermute(value, axis, [(i, i ^ mask) for i in range(size)])]
    ppermute x25 -> x27, starting transfers between devices: 25.1 us -> 27.6 us  [xor_permute(): return lax.ppermute(value, axis, [(i, i ^ mask) for i in range(size)])]
    ppermute x4, waiting for transfers between devices: 7.52 us -> 5.16 us  [the longest x1 5.15 us: line_gather(): edge = lax.ppermute(middle, axis, OUTER)]
    reduce_sum x1 -> x0, other arithmetic: 0.73 us -> none  [per_device(): jnp.sum(jnp.where(chosen, route_probs[None, :, :], 0.0), axis=2)]
  transfers between devices with their start and end apart: 29 -> 31, of which waited for: 9 -> 10; matrix products, arithmetic and copies ran while one was open for 4% -> 0% of each run, Pallas kernels for 9% -> 17%
where the time goes in v3:
time: 69.9 us; the launch traced here: 69.7 us
  starting transfers between devices  31.5 us (45%)
  waiting for transfers between devices  21.7 us (31%)
  Pallas kernels  15.6 us (22%)
  between operations  0.94 us (1%)
    ppermute x27, starting transfers between devices, xor_permute(): return lax.ppermute(value, axis, [(i, i ^ mask) for i in range(size)])  27.6 us
    ppermute x27, waiting for transfers between devices, xor_permute(): return lax.ppermute(value, axis, [(i, i ^ mask) for i in range(size)])  16.5 us
    pallas_call x20, Pallas kernels, local(): pl.pallas_call(kernel, out_shape=outs, in_specs=[spec] * len(args) + [ANY...  12.6 us
    ppermute x1, waiting for transfers between devices, line_gather(): edge = lax.ppermute(middle, axis, OUTER)  5.15 us
    pallas_call x4, Pallas kernels, proj_round(): pl.pallas_call(body, out_shape=shape(features, width, F32), in_specs=[VME...  3 us
  transfers between devices with their start and end apart: 31, of which 10 were waited for; matrix products, arithmetic and copies ran while one was open for 0% of the time, Pallas kernels for 17%

profile of v3, /device:TPU:0, one launch (start us, length us, event | category | flops | bytes accessed | tf_op | source)
XLA Modules:
  0.0 69.7 jit_solution(7397878424579536640)
XLA Ops:
  0.6 2.0 %project.1 = (bf16[128,1024]{1,0:T(8,128)(2,1)S(1)}, bf16[96,1024]{1,0:T(8,128)(2,1)S(1)}, bf16[80,1024]{1,0:T(8,128)(2,1)S(1)}) custom-call(bf16[256,512]{1,0:T(8,128)(2,1)} %refs_0_.7, bf16[512,1024]{1,0:T(8,128)(2,1)} %refs_2_.3, bf16[32,1024]{1,0:T(8,128)(2,1)} %refs_2_.2, s32[8,32]{1,0:T(8,128)} %bitcast.2, f32[8,32]{1,0:T(8,128)} %bitcast.3), custom_call_target="tpu_custom_call" | custom-call | flops 268435456 | bytes 1048576 | tf_op jit(solution)/shard_map/project/pallas_call | solution.py:39
  2.6 0.5 collective-permute-start
  3.1 1.2 %collective-permute-done.refs_2_ = bf16[128,1024]{1,0:T(8,128)(2,1)S(1)} collective-permute-done((bf16[128,1024]{1,0:T(8,128)(2,1)S(1)}, bf16[128,1024]{1,0:T(8,128)(2,1)S(1)}, u32[]{:S(2)}, u32[]{:S(2)}) %collective-permute-start) | collective-permute-done | bytes 262176 | tf_op jit(solution)/shard_map/ppermute | solution.py:73
  4.3 0.1 streams.1
  4.3 2.9 %collective-permute-start.1 = (bf16[96,1024]{1,0:T(8,128)(2,1)S(1)}, bf16[96,1024]{1,0:T(8,128)(2,1)S(1)}, u32[]{:S(2)}, u32[]{:S(2)}) collective-permute-start(bf16[96,1024]{1,0:T(8,128)(2,1)S(1)} %get-tuple-element.33.refs_0_), channel_id=1, source_target_pairs={{0,2},{1,3},{2,0},{3,1},{4,6},{5,7},{6,4},{7,5},{8,10},{9,11},{10,... | collective-permute-start | bytes 589832 | tf_op jit(solution)/shard_map/ppermute | solution.py:73
  7.3 1.5 %collective-permute-start.2 = (bf16[80,1024]{1,0:T(8,128)(2,1)S(1)}, bf16[80,1024]{1,0:T(8,128)(2,1)S(1)}, u32[]{:S(2)}, u32[]{:S(2)}) collective-permute-start(bf16[80,1024]{1,0:T(8,128)(2,1)S(1)} %get-tuple-element.34.refs_1_), channel_id=1, source_target_pairs={{0,4},{1,5},{2,6},{3,7},{4,0},{5,1},{6,2},{7,3},{8,12},{9,13},{10,... | collective-permute-start | bytes 491528 | tf_op jit(solution)/shard_map/ppermute | solution.py:73
  8.8 1.6 %collective-permute-start.5 = (bf16[256,512]{1,0:T(8,128)(2,1)}, bf16[256,512]{1,0:T(8,128)(2,1)S(1)}, u32[]{:S(2)}, u32[]{:S(2)}) collective-permute-start(bf16[256,512]{1,0:T(8,128)(2,1)} %refs_0_.7), channel_id=1, source_target_pairs={{0,8},{8,0},{16,24},{24,16},{1,9},{9,1},{17,25},{25,17},{2,10},{10... | collective-permute-start | bytes 786440 | tf_op jit(solution)/shard_map/ppermute | solution.py:73
  10.4 0.7 collective-permute-start.6
  11.0 2.2 %collective-permute-done.2.refs_3_ = bf16[80,1024]{1,0:T(8,128)(2,1)S(1)} collective-permute-done((bf16[80,1024]{1,0:T(8,128)(2,1)S(1)}, bf16[80,1024]{1,0:T(8,128)(2,1)S(1)}, u32[]{:S(2)}, u32[]{:S(2)}) %collective-permute-start.2) | collective-permute-done | bytes 163872 | tf_op jit(solution)/shard_map/ppermute | solution.py:73
  13.2 0.0 collective-permute-done.1.refs_2_
  13.2 0.1 merge.1
  13.3 1.6 %collective-permute-start.3 = (bf16[112,1024]{1,0:T(8,128)(2,1)S(1)}, bf16[112,1024]{1,0:T(8,128)(2,1)S(1)}, u32[]{:S(2)}, u32[]{:S(2)}) collective-permute-start(bf16[112,1024]{1,0:T(8,128)(2,1)S(1)} %get-tuple-element.35.refs_0_), channel_id=1, source_target_pairs={{0,4},{1,5},{2,6},{3,7},{4,0},{5,1},{6,2},{7,3},{8,12},{9,13},{10,... | collective-permute-start | bytes 688136 | tf_op jit(solution)/shard_map/ppermute | solution.py:73
  14.9 1.0 %collective-permute-start.4 = (bf16[96,1024]{1,0:T(8,128)(2,1)S(1)}, bf16[96,1024]{1,0:T(8,128)(2,1)S(1)}, u32[]{:S(2)}, u32[]{:S(2)}) collective-permute-start(bf16[96,1024]{1,0:T(8,128)(2,1)S(1)} %get-tuple-element.36.refs_1_), channel_id=1, source_target_pairs={{0,2},{1,3},{2,0},{3,1},{4,6},{5,7},{6,4},{7,5},{8,10},{9,11},{10,... | collective-permute-start | bytes 589832 | tf_op jit(solution)/shard_map/ppermute | solution.py:73
  15.9 1.9 %load.3.refs_5_.refs_3_.refs_1_ = bf16[2,768,1024]{2,1,0:T(8,128)(2,1)S(1)} custom-call(bf16[2,768,1024]{2,1,0:T(8,128)(2,1)} %refs_0_.6), custom_call_target="tpu_custom_call" | custom-call | bytes 1048576 | tf_op jit(solution)/shard_map/load/pallas_call | solution.py:39
  17.8 1.9 %load.2.refs_4_.refs_2_ = bf16[2,1024,768]{2,1,0:T(8,128)(2,1)S(1)} custom-call(bf16[2,1024,768]{2,1,0:T(8,128)(2,1)} %refs_0_.5), custom_call_target="tpu_custom_call" | custom-call | bytes 1048576 | tf_op jit(solution)/shard_map/load/pallas_call | solution.py:39
  19.7 0.0 collective-permute-done.5.refs_6_.refs_1_
  19.7 0.0 collective-permute-done.6.refs_7_.refs_2_
  19.7 0.9 %collective-permute-done.4.refs_3_ = bf16[96,1024]{1,0:T(8,128)(2,1)S(1)} collective-permute-done((bf16[96,1024]{1,0:T(8,128)(2,1)S(1)}, bf16[96,1024]{1,0:T(8,128)(2,1)S(1)}, u32[]{:S(2)}, u32[]{:S(2)}) %collective-permute-start.4) | collective-permute-done | bytes 196640 | tf_op jit(solution)/shard_map/ppermute | solution.py:73
  20.6 0.0 collective-permute-done.3.refs_2_
  20.6 0.1 settle.1.refs_0_
  20.7 0.1 collective-permute-start.7
  20.7 0.7 collective-permute-start.13
  21.4 1.3 %collective-permute-done.7.refs_1_ = bf16[272,1024]{1,0:T(8,128)(2,1)S(1)} collective-permute-done((bf16[272,1024]{1,0:T(8,128)(2,1)S(1)}, bf16[272,1024]{1,0:T(8,128)(2,1)S(1)}, u32[]{:S(2)}, u32[]{:S(2)}) %collective-permute-start.7) | collective-permute-done | bytes 557088 | tf_op jit(solution)/shard_map/ppermute | solution.py:73
  22.7 3.4 %experts.1 = (bf16[256,1536]{1,0:T(8,128)(2,1)S(1)}, bf16[128,1024]{1,0:T(8,128)(2,1)S(1)}, bf16[128,1024]{1,0:T(8,128)(2,1)S(1)}) custom-call(bf16[272,1024]{1,0:T(8,128)(2,1)S(1)} %settle.1.refs_0_, bf16[272,1024]{1,0:T(8,128)(2,1)S(1)} %collective-permute-done.7.refs_1_, bf16[2,1024,768]{2,1,0:T(8,128)(2,1)S(1)} %load.2.refs_4_.refs_2_, ...), custom_call_target="tpu_custom_call" | custom-call | flops 2415919104 | bytes 1048576 | tf_op jit(solution)/shard_map/experts/pallas_call | solution.py:39
  26.1 0.2 collective-permute-start.9
  26.3 1.0 %outputs.1 = (bf16[128,1024]{1,0:T(8,128)(2,1)S(1)}, bf16[128,1024]{1,0:T(8,128)(2,1)S(1)}) custom-call(bf16[256,1536]{1,0:T(8,128)(2,1)S(1)} %get-tuple-element.37.refs_0_, bf16[2,768,1024]{2,1,0:T(8,128)(2,1)S(1)} %load.3.refs_5_.refs_3_.refs_1_), custom_call_target="tpu_custom_call" | custom-call | flops 805306368 | bytes 1048576 | tf_op jit(solution)/shard_map/outputs/pallas_call | solution.py:39
  27.3 0.4 collective-permute-start.8
  27.7 1.3 %collective-permute-start.14 = (bf16[256,512]{1,0:T(8,128)(2,1)S(1)}, bf16[256,512]{1,0:T(8,128)(2,1)S(1)}, u32[]{:S(2)}, u32[]{:S(2)}) collective-permute-start(bf16[256,512]{1,0:T(8,128)(2,1)S(1)} %collective-permute-done.6.refs_7_.refs_2_), channel_id=1, source_target_pairs={{8,0},{16,24},{9,1},{17,25},{10,2},{18,26},{11,3},{19,27},{12,4},{... | collective-permute-start | bytes 786440 | tf_op jit(solution)/shard_map/ppermute | solution.py:83
  29.0 0.0 collective-permute-done.13.refs_4_.refs_3_
  29.0 1.3 %collective-permute-start.21 = (bf16[256,512]{1,0:T(8,128)(2,1)S(1)}, bf16[256,512]{1,0:T(8,128)(2,1)S(1)}, u32[]{:S(2)}, u32[]{:S(2)}) collective-permute-start(bf16[256,512]{1,0:T(8,128)(2,1)S(1)} %collective-permute-done.13.refs_4_.refs_3_), channel_id=1, source_target_pairs={{8,0},{16,24},{9,1},{17,25},{10,2},{18,26},{11,3},{19,27},{12,4},{... | collective-permute-start | bytes 786440 | tf_op jit(solution)/shard_map/ppermute | solution.py:448
  30.3 0.1 pieces.3
  30.4 1.2 %collective-permute-start.10 = (bf16[32,1024]{1,0:T(8,128)(2,1)S(1)}, bf16[32,1024]{1,0:T(8,128)(2,1)S(1)}, u32[]{:S(2)}, u32[]{:S(2)}) collective-permute-start(bf16[32,1024]{1,0:T(8,128)(2,1)S(1)} %get-tuple-element.44), channel_id=1, source_target_pairs={{0,2},{1,3},{2,0},{3,1},{4,6},{5,7},{6,4},{7,5},{8,10},{9,11},{10,... | collective-permute-start | bytes 196616 | tf_op jit(solution)/shard_map/ppermute | solution.py:73
  31.6 1.0 %collective-permute-start.11 = (bf16[32,1024]{1,0:T(8,128)(2,1)S(1)}, bf16[32,1024]{1,0:T(8,128)(2,1)S(1)}, u32[]{:S(2)}, u32[]{:S(2)}) collective-permute-start(bf16[32,1024]{1,0:T(8,128)(2,1)S(1)} %get-tuple-element.45), channel_id=1, source_target_pairs={{0,4},{1,5},{2,6},{3,7},{4,0},{5,1},{6,2},{7,3},{8,12},{9,13},{10,... | collective-permute-start | bytes 196616 | tf_op jit(solution)/shard_map/ppermute | solution.py:73
  32.6 1.4 %collective-permute-start.12 = (bf16[32,1024]{1,0:T(8,128)(2,1)S(1)}, bf16[32,1024]{1,0:T(8,128)(2,1)S(1)}, u32[]{:S(2)}, u32[]{:S(2)}) collective-permute-start(bf16[32,1024]{1,0:T(8,128)(2,1)S(1)} %get-tuple-element.46), channel_id=1, source_target_pairs={{0,6},{1,7},{2,4},{3,5},{4,2},{5,3},{6,0},{7,1},{8,14},{9,15},{10,... | collective-permute-start | bytes 196616 | tf_op jit(solution)/shard_map/ppermute | solution.py:73
  34.0 0.1 pieces.2
  34.1 0.0 copy-start
  34.1 5.2 %collective-permute-done.14.refs_5_.refs_4_ = bf16[256,512]{1,0:T(8,128)(2,1)S(1)} collective-permute-done((bf16[256,512]{1,0:T(8,128)(2,1)S(1)}, bf16[256,512]{1,0:T(8,128)(2,1)S(1)}, u32[]{:S(2)}, u32[]{:S(2)}) %collective-permute-start.14) | collective-permute-done | bytes 262176 | tf_op jit(solution)/shard_map/ppermute | solution.py:83
  39.3 2.5 %collective-permute-start.18 = (bf16[32,1024]{1,0:T(8,128)(2,1)S(1)}, bf16[32,1024]{1,0:T(8,128)(2,1)S(1)}, u32[]{:S(2)}, u32[]{:S(2)}) collective-permute-start(bf16[32,1024]{1,0:T(8,128)(2,1)S(1)} %add_pieces.2.refs_0_.refs_6_), channel_id=1, source_target_pairs={{0,8},{8,0},{16,24},{24,16},{1,9},{9,1},{17,25},{25,17},{2,10},{10... | collective-permute-start | bytes 196616 | tf_op jit(solution)/shard_map/ppermute | solution.py:73
  41.8 1.1 %collective-permute-start.15 = (bf16[64,1024]{1,0:T(8,128)(2,1)S(1)}, bf16[64,1024]{1,0:T(8,128)(2,1)S(1)}, u32[]{:S(2)}, u32[]{:S(2)}) collective-permute-start(bf16[64,1024]{1,0:T(8,128)(2,1)S(1)} %get-tuple-element.50), channel_id=1, source_target_pairs={{0,2},{1,3},{2,0},{3,1},{4,6},{5,7},{6,4},{7,5},{8,10},{9,11},{10,... | collective-permute-start | bytes 393224 | tf_op jit(solution)/shard_map/ppermute | solution.py:73
  42.9 0.9 %collective-permute-start.16 = (bf16[64,1024]{1,0:T(8,128)(2,1)S(1)}, bf16[64,1024]{1,0:T(8,128)(2,1)S(1)}, u32[]{:S(2)}, u32[]{:S(2)}) collective-permute-start(bf16[64,1024]{1,0:T(8,128)(2,1)S(1)} %get-tuple-element.51), channel_id=1, source_target_pairs={{0,4},{1,5},{2,6},{3,7},{4,0},{5,1},{6,2},{7,3},{8,12},{9,13},{10,... | collective-permute-start | bytes 393224 | tf_op jit(solution)/shard_map/ppermute | solution.py:73
  43.8 1.6 %collective-permute-start.17 = (bf16[64,1024]{1,0:T(8,128)(2,1)S(1)}, bf16[64,1024]{1,0:T(8,128)(2,1)S(1)}, u32[]{:S(2)}, u32[]{:S(2)}) collective-permute-start(bf16[64,1024]{1,0:T(8,128)(2,1)S(1)} %get-tuple-element.52), channel_id=1, source_target_pairs={{0,6},{1,7},{2,4},{3,5},{4,2},{5,3},{6,0},{7,1},{8,14},{9,15},{10,... | collective-permute-start | bytes 393224 | tf_op jit(solution)/shard_map/ppermute | solution.py:73
  45.3 1.3 %collective-permute-start.19 = (bf16[32,1024]{1,0:T(8,128)(2,1)S(1)}, bf16[32,1024]{1,0:T(8,128)(2,1)S(1)}, u32[]{:S(2)}, u32[]{:S(2)}) collective-permute-start(bf16[32,1024]{1,0:T(8,128)(2,1)S(1)} %add_pieces.2.refs_0_.refs_6_), channel_id=1, source_target_pairs={{0,16},{8,24},{16,0},{24,8},{1,17},{9,25},{17,1},{25,9},{2,18},{10... | collective-permute-start | bytes 196616 | tf_op jit(solution)/shard_map/ppermute | solution.py:73
  46.7 1.9 %collective-permute-start.20 = (bf16[32,1024]{1,0:T(8,128)(2,1)S(1)}, bf16[32,1024]{1,0:T(8,128)(2,1)S(1)}, u32[]{:S(2)}, u32[]{:S(2)}) collective-permute-start(bf16[32,1024]{1,0:T(8,128)(2,1)S(1)} %add_pieces.2.refs_0_.refs_6_), channel_id=1, source_target_pairs={{0,24},{8,16},{16,8},{24,0},{1,25},{9,17},{17,9},{25,1},{2,26},{10... | collective-permute-start | bytes 196616 | tf_op jit(solution)/shard_map/ppermute | solution.py:73
  48.6 3.0 %collective-permute-done.19.refs_1_ = bf16[32,1024]{1,0:T(8,128)(2,1)S(1)} collective-permute-done((bf16[32,1024]{1,0:T(8,128)(2,1)S(1)}, bf16[32,1024]{1,0:T(8,128)(2,1)S(1)}, u32[]{:S(2)}, u32[]{:S(2)}) %collective-permute-start.19) | collective-permute-done | bytes 65568 | tf_op jit(solution)/shard_map/ppermute | solution.py:73
  51.6 1.2 %collective-permute-done.20.refs_2_ = bf16[32,1024]{1,0:T(8,128)(2,1)S(1)} collective-permute-done((bf16[32,1024]{1,0:T(8,128)(2,1)S(1)}, bf16[32,1024]{1,0:T(8,128)(2,1)S(1)}, u32[]{:S(2)}, u32[]{:S(2)}) %collective-permute-start.20) | collective-permute-done | bytes 65568 | tf_op jit(solution)/shard_map/ppermute | solution.py:73
  52.9 0.1 collective-permute-start.22
  53.0 0.5 collective-permute-start.23
  53.5 0.1 arrange.1
  53.6 0.1 collective-permute-start.29
  53.7 1.6 %collective-permute-start.28 = (bf16[96,1024]{1,0:T(8,128)(2,1)S(1)}, bf16[96,1024]{1,0:T(8,128)(2,1)S(1)}, u32[]{:S(2)}, u32[]{:S(2)}) collective-permute-start(bf16[96,1024]{1,0:T(8,128)(2,1)S(1)} %stack.5.refs_4_.refs_3_), channel_id=1, source_target_pairs={{0,6},{1,7},{2,4},{3,5},{4,2},{5,3},{6,0},{7,1},{8,14},{9,15},{10,... | collective-permute-start | bytes 589832 | tf_op jit(solution)/shard_map/ppermute | solution.py:73
  55.3 1.0 %collective-permute-start.26 = (bf16[96,1024]{1,0:T(8,128)(2,1)S(1)}, bf16[96,1024]{1,0:T(8,128)(2,1)S(1)}, u32[]{:S(2)}, u32[]{:S(2)}) collective-permute-start(bf16[96,1024]{1,0:T(8,128)(2,1)S(1)} %stack.5.refs_4_.refs_3_), channel_id=1, source_target_pairs={{0,4},{1,5},{2,6},{3,7},{4,0},{5,1},{6,2},{7,3},{8,12},{9,13},{10,... | collective-permute-start | bytes 589832 | tf_op jit(solution)/shard_map/ppermute | solution.py:73
  56.3 0.7 add_pieces.3.refs_3_
  57.0 0.9 %collective-permute-start.24 = (bf16[96,1024]{1,0:T(8,128)(2,1)S(1)}, bf16[96,1024]{1,0:T(8,128)(2,1)S(1)}, u32[]{:S(2)}, u32[]{:S(2)}) collective-permute-start(bf16[96,1024]{1,0:T(8,128)(2,1)S(1)} %stack.5.refs_4_.refs_3_), channel_id=1, source_target_pairs={{0,2},{1,3},{2,0},{3,1},{4,6},{5,7},{6,4},{7,5},{8,10},{9,11},{10,... | collective-permute-start | bytes 589832 | tf_op jit(solution)/shard_map/ppermute | solution.py:73
  57.9 1.2 %input_grads.1.refs_2_ = bf16[256,512]{1,0:T(8,128)(2,1)} custom-call(bf16[128,1024]{1,0:T(8,128)(2,1)S(1)} %stack.6.refs_0_.refs_1_, bf16[128,1024]{1,0:T(8,128)(2,1)S(1)} %constant_dynamic-update-slice_fusion.refs_1_.refs_2_, bf16[512,1024]{1,0:T(8,128)(2,1)S(1)} %copy-done), custom_call_target="tpu_custom_call" | custom-call | flops 268435456 | bytes 1048576 | tf_op jit(solution)/shard_map/input_grads/pallas_call | solution.py:39
  59.1 0.5 proj_round.4.refs_1_.refs_5_
  59.6 2.8 %collective-permute-done.28.refs_0_ = bf16[96,1024]{1,0:T(8,128)(2,1)S(1)} collective-permute-done((bf16[96,1024]{1,0:T(8,128)(2,1)S(1)}, bf16[96,1024]{1,0:T(8,128)(2,1)S(1)}, u32[]{:S(2)}, u32[]{:S(2)}) %collective-permute-start.28) | collective-permute-done | bytes 196640 | tf_op jit(solution)/shard_map/ppermute | solution.py:73
  62.4 0.1 collective-permute-start.30
  62.5 3.6 %collective-permute-done.26.refs_0_ = bf16[96,1024]{1,0:T(8,128)(2,1)S(1)} collective-permute-done((bf16[96,1024]{1,0:T(8,128)(2,1)S(1)}, bf16[96,1024]{1,0:T(8,128)(2,1)S(1)}, u32[]{:S(2)}, u32[]{:S(2)}) %collective-permute-start.26) | collective-permute-done | bytes 196640 | tf_op jit(solution)/shard_map/ppermute | solution.py:73
  66.1 0.1 collective-permute-start.27
  66.2 0.5 collective-permute-start.25
  66.8 0.5 proj_round.5.refs_5_
  67.2 0.4 collective-permute-done.27.refs_4_
  67.6 0.5 proj_round.6.refs_5_
  68.1 1.6 %proj_round.7 = f32[512,1024]{1,0:T(8,128)} custom-call(bf16[256,512]{1,0:T(8,128)(2,1)S(1)} %get-tuple-element.53.refs_0_, bf16[128,1024]{1,0:T(8,128)(2,1)S(1)} %stack.6.refs_0_.refs_1_, bf16[128,1024]{1,0:T(8,128)(2,1)S(1)} %constant_dynamic-update-slice_fusion.refs_1_.refs_2_, bf16[96,1024]{1,0:T(8,128)(2,1)S(1)} %stack.7.refs_3_, ...), custom_call_target="tpu_custom_call" | custom-call | flops 268435456 | bytes 4194304 | tf_op jit(solution)/shard_map/proj_round/pallas_call | solution.py:419
  (33 shorter events, 0.2 us)
Async XLA Ops:
  2.6 1.7 %collective-permute-start = (bf16[128,1024]{1,0:T(8,128)(2,1)S(1)}, bf16[128,1024]{1,0:T(8,128)(2,1)S(1)}, u32[]{:S(2)}, u32[]{:S(2)}) collective-permute-start(bf16[128,1024]{1,0:T(8,128)(2,1)S(1)} %get-tuple-element.32), channel_id=1, source_target_pairs={{0,1},{1,0},{2,3},{3,2},{4,5},{5,4},{6,7},{7,6},{8,9},{9,8},{10,11... | collective-permute-start | bytes 786440 | tf_op jit(solution)/shard_map/ppermute | solution.py:73
  4.3 8.9 %collective-permute-start.1 = (bf16[96,1024]{1,0:T(8,128)(2,1)S(1)}, bf16[96,1024]{1,0:T(8,128)(2,1)S(1)}, u32[]{:S(2)}, u32[]{:S(2)}) collective-permute-start(bf16[96,1024]{1,0:T(8,128)(2,1)S(1)} %get-tuple-element.33.refs_0_), channel_id=1, source_target_pairs={{0,2},{1,3},{2,0},{3,1},{4,6},{5,7},{6,4},{7,5},{8,10},{9,11},{10,... | collective-permute-start | bytes 589832 | tf_op jit(solution)/shard_map/ppermute | solution.py:73
  7.3 6.0 %collective-permute-start.2 = (bf16[80,1024]{1,0:T(8,128)(2,1)S(1)}, bf16[80,1024]{1,0:T(8,128)(2,1)S(1)}, u32[]{:S(2)}, u32[]{:S(2)}) collective-permute-start(bf16[80,1024]{1,0:T(8,128)(2,1)S(1)} %get-tuple-element.34.refs_1_), channel_id=1, source_target_pairs={{0,4},{1,5},{2,6},{3,7},{4,0},{5,1},{6,2},{7,3},{8,12},{9,13},{10,... | collective-permute-start | bytes 491528 | tf_op jit(solution)/shard_map/ppermute | solution.py:73
  8.8 10.9 %collective-permute-start.5 = (bf16[256,512]{1,0:T(8,128)(2,1)}, bf16[256,512]{1,0:T(8,128)(2,1)S(1)}, u32[]{:S(2)}, u32[]{:S(2)}) collective-permute-start(bf16[256,512]{1,0:T(8,128)(2,1)} %refs_0_.7), channel_id=1, source_target_pairs={{0,8},{8,0},{16,24},{24,16},{1,9},{9,1},{17,25},{25,17},{2,10},{10... | collective-permute-start | bytes 786440 | tf_op jit(solution)/shard_map/ppermute | solution.py:73
  10.4 9.3 %collective-permute-start.6 = (bf16[256,512]{1,0:T(8,128)(2,1)}, bf16[256,512]{1,0:T(8,128)(2,1)S(1)}, u32[]{:S(2)}, u32[]{:S(2)}) collective-permute-start(bf16[256,512]{1,0:T(8,128)(2,1)} %refs_0_.7), channel_id=1, source_target_pairs={{8,16},{16,8},{9,17},{17,9},{10,18},{18,10},{11,19},{19,11},{12,20... | collective-permute-start | bytes 786440 | tf_op jit(solution)/shard_map/ppermute | solution.py:81
  13.3 7.3 %collective-permute-start.3 = (bf16[112,1024]{1,0:T(8,128)(2,1)S(1)}, bf16[112,1024]{1,0:T(8,128)(2,1)S(1)}, u32[]{:S(2)}, u32[]{:S(2)}) collective-permute-start(bf16[112,1024]{1,0:T(8,128)(2,1)S(1)} %get-tuple-element.35.refs_0_), channel_id=1, source_target_pairs={{0,4},{1,5},{2,6},{3,7},{4,0},{5,1},{6,2},{7,3},{8,12},{9,13},{10,... | collective-permute-start | bytes 688136 | tf_op jit(solution)/shard_map/ppermute | solution.py:73
  14.9 5.7 %collective-permute-start.4 = (bf16[96,1024]{1,0:T(8,128)(2,1)S(1)}, bf16[96,1024]{1,0:T(8,128)(2,1)S(1)}, u32[]{:S(2)}, u32[]{:S(2)}) collective-permute-start(bf16[96,1024]{1,0:T(8,128)(2,1)S(1)} %get-tuple-element.36.refs_1_), channel_id=1, source_target_pairs={{0,2},{1,3},{2,0},{3,1},{4,6},{5,7},{6,4},{7,5},{8,10},{9,11},{10,... | collective-permute-start | bytes 589832 | tf_op jit(solution)/shard_map/ppermute | solution.py:73
  20.7 2.0 %collective-permute-start.7 = (bf16[272,1024]{1,0:T(8,128)(2,1)S(1)}, bf16[272,1024]{1,0:T(8,128)(2,1)S(1)}, u32[]{:S(2)}, u32[]{:S(2)}) collective-permute-start(bf16[272,1024]{1,0:T(8,128)(2,1)S(1)} %settle.1.refs_0_), channel_id=1, source_target_pairs={{0,1},{1,0},{2,3},{3,2},{4,5},{5,4},{6,7},{7,6},{8,9},{9,8},{10,11... | collective-permute-start | bytes 1671176 | tf_op jit(solution)/shard_map/ppermute | solution.py:73
  20.7 8.3 %collective-permute-start.13 = (bf16[256,512]{1,0:T(8,128)(2,1)S(1)}, bf16[256,512]{1,0:T(8,128)(2,1)S(1)}, u32[]{:S(2)}, u32[]{:S(2)}) collective-permute-start(bf16[256,512]{1,0:T(8,128)(2,1)S(1)} %collective-permute-done.5.refs_6_.refs_1_), channel_id=1, source_target_pairs={{8,16},{16,8},{9,17},{17,9},{10,18},{18,10},{11,19},{19,11},{12,20... | collective-permute-start | bytes 786440 | tf_op jit(solution)/shard_map/ppermute | solution.py:82
  26.1 4.2 %collective-permute-start.9 = (bf16[128,1024]{1,0:T(8,128)(2,1)S(1)}, bf16[128,1024]{1,0:T(8,128)(2,1)S(1)}, u32[]{:S(2)}, u32[]{:S(2)}) collective-permute-start(bf16[128,1024]{1,0:T(8,128)(2,1)S(1)} %get-tuple-element.42), channel_id=1, source_target_pairs={{0,1},{1,0},{2,3},{3,2},{4,5},{5,4},{6,7},{7,6},{8,9},{9,8},{10,11... | collective-permute-start | bytes 786440 | tf_op jit(solution)/shard_map/ppermute | solution.py:73
  26.3 27.2 %copy-start.1 = (bf16[256,512]{1,0:T(8,128)(2,1)S(1)}, bf16[256,512]{1,0:T(8,128)(2,1)}, u32[]{:S(2)}) copy-start(bf16[256,512]{1,0:T(8,128)(2,1)} %refs_0_.7) | copy-start | bytes 786436
  27.3 5.3 %collective-permute-start.8 = (bf16[128,1024]{1,0:T(8,128)(2,1)S(1)}, bf16[128,1024]{1,0:T(8,128)(2,1)S(1)}, u32[]{:S(2)}, u32[]{:S(2)}) collective-permute-start(bf16[128,1024]{1,0:T(8,128)(2,1)S(1)} %get-tuple-element.39), channel_id=1, source_target_pairs={{0,1},{1,0},{2,3},{3,2},{4,5},{5,4},{6,7},{7,6},{8,9},{9,8},{10,11... | collective-permute-start | bytes 786440 | tf_op jit(solution)/shard_map/ppermute | solution.py:73
  27.7 11.5 %collective-permute-start.14 = (bf16[256,512]{1,0:T(8,128)(2,1)S(1)}, bf16[256,512]{1,0:T(8,128)(2,1)S(1)}, u32[]{:S(2)}, u32[]{:S(2)}) collective-permute-start(bf16[256,512]{1,0:T(8,128)(2,1)S(1)} %collective-permute-done.6.refs_7_.refs_2_), channel_id=1, source_target_pairs={{8,0},{16,24},{9,1},{17,25},{10,2},{18,26},{11,3},{19,27},{12,4},{... | collective-permute-start | bytes 786440 | tf_op jit(solution)/shard_map/ppermute | solution.py:83
  29.0 16.3 %collective-permute-start.21 = (bf16[256,512]{1,0:T(8,128)(2,1)S(1)}, bf16[256,512]{1,0:T(8,128)(2,1)S(1)}, u32[]{:S(2)}, u32[]{:S(2)}) collective-permute-start(bf16[256,512]{1,0:T(8,128)(2,1)S(1)} %collective-permute-done.13.refs_4_.refs_3_), channel_id=1, source_target_pairs={{8,0},{16,24},{9,1},{17,25},{10,2},{18,26},{11,3},{19,27},{12,4},{... | collective-permute-start | bytes 786440 | tf_op jit(solution)/shard_map/ppermute | solution.py:448
  30.4 8.8 %collective-permute-start.10 = (bf16[32,1024]{1,0:T(8,128)(2,1)S(1)}, bf16[32,1024]{1,0:T(8,128)(2,1)S(1)}, u32[]{:S(2)}, u32[]{:S(2)}) collective-permute-start(bf16[32,1024]{1,0:T(8,128)(2,1)S(1)} %get-tuple-element.44), channel_id=1, source_target_pairs={{0,2},{1,3},{2,0},{3,1},{4,6},{5,7},{6,4},{7,5},{8,10},{9,11},{10,... | collective-permute-start | bytes 196616 | tf_op jit(solution)/shard_map/ppermute | solution.py:73
  31.6 7.6 %collective-permute-start.11 = (bf16[32,1024]{1,0:T(8,128)(2,1)S(1)}, bf16[32,1024]{1,0:T(8,128)(2,1)S(1)}, u32[]{:S(2)}, u32[]{:S(2)}) collective-permute-start(bf16[32,1024]{1,0:T(8,128)(2,1)S(1)} %get-tuple-element.45), channel_id=1, source_target_pairs={{0,4},{1,5},{2,6},{3,7},{4,0},{5,1},{6,2},{7,3},{8,12},{9,13},{10,... | collective-permute-start | bytes 196616 | tf_op jit(solution)/shard_map/ppermute | solution.py:73
  32.6 6.6 %collective-permute-start.12 = (bf16[32,1024]{1,0:T(8,128)(2,1)S(1)}, bf16[32,1024]{1,0:T(8,128)(2,1)S(1)}, u32[]{:S(2)}, u32[]{:S(2)}) collective-permute-start(bf16[32,1024]{1,0:T(8,128)(2,1)S(1)} %get-tuple-element.46), channel_id=1, source_target_pairs={{0,6},{1,7},{2,4},{3,5},{4,2},{5,3},{6,0},{7,1},{8,14},{9,15},{10,... | collective-permute-start | bytes 196616 | tf_op jit(solution)/shard_map/ppermute | solution.py:73
  34.1 23.9 %copy-start = (bf16[512,1024]{1,0:T(8,128)(2,1)S(1)}, bf16[512,1024]{1,0:T(8,128)(2,1)}, u32[]{:S(2)}) copy-start(bf16[512,1024]{1,0:T(8,128)(2,1)} %refs_2_.3) | copy-start | bytes 3145732
  39.3 7.4 %collective-permute-start.18 = (bf16[32,1024]{1,0:T(8,128)(2,1)S(1)}, bf16[32,1024]{1,0:T(8,128)(2,1)S(1)}, u32[]{:S(2)}, u32[]{:S(2)}) collective-permute-start(bf16[32,1024]{1,0:T(8,128)(2,1)S(1)} %add_pieces.2.refs_0_.refs_6_), channel_id=1, source_target_pairs={{0,8},{8,0},{16,24},{24,16},{1,9},{9,1},{17,25},{25,17},{2,10},{10... | collective-permute-start | bytes 196616 | tf_op jit(solution)/shard_map/ppermute | solution.py:73
  41.8 11.1 %collective-permute-start.15 = (bf16[64,1024]{1,0:T(8,128)(2,1)S(1)}, bf16[64,1024]{1,0:T(8,128)(2,1)S(1)}, u32[]{:S(2)}, u32[]{:S(2)}) collective-permute-start(bf16[64,1024]{1,0:T(8,128)(2,1)S(1)} %get-tuple-element.50), channel_id=1, source_target_pairs={{0,2},{1,3},{2,0},{3,1},{4,6},{5,7},{6,4},{7,5},{8,10},{9,11},{10,... | collective-permute-start | bytes 393224 | tf_op jit(solution)/shard_map/ppermute | solution.py:73
  42.9 9.9 %collective-permute-start.16 = (bf16[64,1024]{1,0:T(8,128)(2,1)S(1)}, bf16[64,1024]{1,0:T(8,128)(2,1)S(1)}, u32[]{:S(2)}, u32[]{:S(2)}) collective-permute-start(bf16[64,1024]{1,0:T(8,128)(2,1)S(1)} %get-tuple-element.51), channel_id=1, source_target_pairs={{0,4},{1,5},{2,6},{3,7},{4,0},{5,1},{6,2},{7,3},{8,12},{9,13},{10,... | collective-permute-start | bytes 393224 | tf_op jit(solution)/shard_map/ppermute | solution.py:73
  43.8 9.1 %collective-permute-start.17 = (bf16[64,1024]{1,0:T(8,128)(2,1)S(1)}, bf16[64,1024]{1,0:T(8,128)(2,1)S(1)}, u32[]{:S(2)}, u32[]{:S(2)}) collective-permute-start(bf16[64,1024]{1,0:T(8,128)(2,1)S(1)} %get-tuple-element.52), channel_id=1, source_target_pairs={{0,6},{1,7},{2,4},{3,5},{4,2},{5,3},{6,0},{7,1},{8,14},{9,15},{10,... | collective-permute-start | bytes 393224 | tf_op jit(solution)/shard_map/ppermute | solution.py:73
  45.3 6.3 %collective-permute-start.19 = (bf16[32,1024]{1,0:T(8,128)(2,1)S(1)}, bf16[32,1024]{1,0:T(8,128)(2,1)S(1)}, u32[]{:S(2)}, u32[]{:S(2)}) collective-permute-start(bf16[32,1024]{1,0:T(8,128)(2,1)S(1)} %add_pieces.2.refs_0_.refs_6_), channel_id=1, source_target_pairs={{0,16},{8,24},{16,0},{24,8},{1,17},{9,25},{17,1},{25,9},{2,18},{10... | collective-permute-start | bytes 196616 | tf_op jit(solution)/shard_map/ppermute | solution.py:73
  46.7 6.2 %collective-permute-start.20 = (bf16[32,1024]{1,0:T(8,128)(2,1)S(1)}, bf16[32,1024]{1,0:T(8,128)(2,1)S(1)}, u32[]{:S(2)}, u32[]{:S(2)}) collective-permute-start(bf16[32,1024]{1,0:T(8,128)(2,1)S(1)} %add_pieces.2.refs_0_.refs_6_), channel_id=1, source_target_pairs={{0,24},{8,16},{16,8},{24,0},{1,25},{9,17},{17,9},{25,1},{2,26},{10... | collective-permute-start | bytes 196616 | tf_op jit(solution)/shard_map/ppermute | solution.py:73
  52.9 4.1 %collective-permute-start.22 = (bf16[64,1024]{1,0:T(8,128)(2,1)S(1)}, bf16[64,1024]{1,0:T(8,128)(2,1)S(1)}, u32[]{:S(2)}, u32[]{:S(2)}) collective-permute-start(bf16[64,1024]{1,0:T(8,128)(2,1)S(1)} %get-tuple-element.58), channel_id=1, source_target_pairs={{0,1},{1,0},{2,3},{3,2},{4,5},{5,4},{6,7},{7,6},{8,9},{9,8},{10,11... | collective-permute-start | bytes 393224 | tf_op jit(solution)/shard_map/ppermute | solution.py:73
  53.0 4.9 %collective-permute-start.23 = (bf16[64,1024]{1,0:T(8,128)(2,1)S(1)}, bf16[64,1024]{1,0:T(8,128)(2,1)S(1)}, u32[]{:S(2)}, u32[]{:S(2)}) collective-permute-start(bf16[64,1024]{1,0:T(8,128)(2,1)S(1)} %get-tuple-element.57), channel_id=1, source_target_pairs={{0,1},{1,0},{2,3},{3,2},{4,5},{5,4},{6,7},{7,6},{8,9},{9,8},{10,11... | collective-permute-start | bytes 393224 | tf_op jit(solution)/shard_map/ppermute | solution.py:73
  53.6 5.5 %collective-permute-start.29 = (bf16[96,1024]{1,0:T(8,128)(2,1)S(1)}, bf16[96,1024]{1,0:T(8,128)(2,1)S(1)}, u32[]{:S(2)}, u32[]{:S(2)}) collective-permute-start(bf16[96,1024]{1,0:T(8,128)(2,1)S(1)} %stack.5.refs_4_.refs_3_), channel_id=1, source_target_pairs={{0,1},{1,0},{2,3},{3,2},{4,5},{5,4},{6,7},{7,6},{8,9},{9,8},{10,11... | collective-permute-start | bytes 589832 | tf_op jit(solution)/shard_map/ppermute | solution.py:73
  53.7 8.6 %collective-permute-start.28 = (bf16[96,1024]{1,0:T(8,128)(2,1)S(1)}, bf16[96,1024]{1,0:T(8,128)(2,1)S(1)}, u32[]{:S(2)}, u32[]{:S(2)}) collective-permute-start(bf16[96,1024]{1,0:T(8,128)(2,1)S(1)} %stack.5.refs_4_.refs_3_), channel_id=1, source_target_pairs={{0,6},{1,7},{2,4},{3,5},{4,2},{5,3},{6,0},{7,1},{8,14},{9,15},{10,... | collective-permute-start | bytes 589832 | tf_op jit(solution)/shard_map/ppermute | solution.py:73
  55.3 10.8 %collective-permute-start.26 = (bf16[96,1024]{1,0:T(8,128)(2,1)S(1)}, bf16[96,1024]{1,0:T(8,128)(2,1)S(1)}, u32[]{:S(2)}, u32[]{:S(2)}) collective-permute-start(bf16[96,1024]{1,0:T(8,128)(2,1)S(1)} %stack.5.refs_4_.refs_3_), channel_id=1, source_target_pairs={{0,4},{1,5},{2,6},{3,7},{4,0},{5,1},{6,2},{7,3},{8,12},{9,13},{10,... | collective-permute-start | bytes 589832 | tf_op jit(solution)/shard_map/ppermute | solution.py:73
  57.0 5.4 %copy-start.3 = (bf16[32,1024]{1,0:T(8,128)(2,1)S(1)}, bf16[32,1024]{1,0:T(8,128)(2,1)}, u32[]{:S(2)}) copy-start(bf16[32,1024]{1,0:T(8,128)(2,1)} %add_pieces.3.refs_3_) | copy-start | bytes 196612
  57.0 9.2 %collective-permute-start.24 = (bf16[96,1024]{1,0:T(8,128)(2,1)S(1)}, bf16[96,1024]{1,0:T(8,128)(2,1)S(1)}, u32[]{:S(2)}, u32[]{:S(2)}) collective-permute-start(bf16[96,1024]{1,0:T(8,128)(2,1)S(1)} %stack.5.refs_4_.refs_3_), channel_id=1, source_target_pairs={{0,2},{1,3},{2,0},{3,1},{4,6},{5,7},{6,4},{7,5},{8,10},{9,11},{10,... | collective-permute-start | bytes 589832 | tf_op jit(solution)/shard_map/ppermute | solution.py:73
  59.1 3.3 %copy-start.2 = (bf16[256,512]{1,0:T(8,128)(2,1)S(1)}, bf16[256,512]{1,0:T(8,128)(2,1)}, u32[]{:S(2)}) copy-start(bf16[256,512]{1,0:T(8,128)(2,1)} %input_grads.1.refs_2_) | copy-start | bytes 786436
  62.4 4.4 %collective-permute-start.30 = (bf16[96,1024]{1,0:T(8,128)(2,1)S(1)}, bf16[96,1024]{1,0:T(8,128)(2,1)S(1)}, u32[]{:S(2)}, u32[]{:S(2)}) collective-permute-start(bf16[96,1024]{1,0:T(8,128)(2,1)S(1)} %stack.9.refs_3_), channel_id=1, source_target_pairs={{0,1},{1,0},{2,3},{3,2},{4,5},{5,4},{6,7},{7,6},{8,9},{9,8},{10,11... | collective-permute-start | bytes 589832 | tf_op jit(solution)/shard_map/ppermute | solution.py:73
  66.1 1.5 %collective-permute-start.27 = (bf16[96,1024]{1,0:T(8,128)(2,1)S(1)}, bf16[96,1024]{1,0:T(8,128)(2,1)S(1)}, u32[]{:S(2)}, u32[]{:S(2)}) collective-permute-start(bf16[96,1024]{1,0:T(8,128)(2,1)S(1)} %stack.8.refs_3_), channel_id=1, source_target_pairs={{0,1},{1,0},{2,3},{3,2},{4,5},{5,4},{6,7},{7,6},{8,9},{9,8},{10,11... | collective-permute-start | bytes 589832 | tf_op jit(solution)/shard_map/ppermute | solution.py:73
  66.2 1.9 %collective-permute-start.25 = (bf16[96,1024]{1,0:T(8,128)(2,1)S(1)}, bf16[96,1024]{1,0:T(8,128)(2,1)S(1)}, u32[]{:S(2)}, u32[]{:S(2)}) collective-permute-start(bf16[96,1024]{1,0:T(8,128)(2,1)S(1)} %stack.7.refs_3_), channel_id=1, source_target_pairs={{0,1},{1,0},{2,3},{3,2},{4,5},{5,4},{6,7},{7,6},{8,9},{9,8},{10,11... | collective-permute-start | bytes 589832 | tf_op jit(solution)/shard_map/ppermute | solution.py:73

commit v4 on v3

--- a/solution.py
+++ b/solution.py
@@ -48,10 +48,14 @@
     )(*args, *ties)
 
 
-def load(value):
-    def body(src, dst, sems):
+def load(*values):
+    count = len(values)
+    parts = [(j, i) for i in range(values[0].shape[0]) for j in range(count)]
+
+    def body(*refs):
         copies = [
-            pltpu.make_async_copy(src.at[i], dst.at[i], sems.at[i]) for i in range(value.shape[0])
+            pltpu.make_async_copy(refs[j].at[i], refs[count + j].at[i], refs[2 * count].at[place])
+            for place, (j, i) in enumerate(parts)
         ]
         for copy in copies:
             copy.start()
@@ -60,10 +64,10 @@
 
     return local(
         body,
-        pltpu.VMEM(value.shape, value.dtype),
-        (value,),
+        tuple(pltpu.VMEM(value.shape, value.dtype) for value in values),
+        values,
         "load",
-        scratch=[pltpu.SemaphoreType.DMA((value.shape[0],))],
+        scratch=[pltpu.SemaphoreType.DMA((len(parts),))],
         pin=pltpu.HBM,
     )
 
@@ -82,6 +86,14 @@
     middle_far = lax.ppermute(near, axis, INNER)
     edge = lax.ppermute(middle, axis, OUTER)
     return [(near, middle), (middle_far, edge)]
+
+
+def hops_last(hops):
+    if not hops:
+        return ()
+    value = hops[1][0]
+    rows = value.shape[0] // 2
+    return tuple(lax.ppermute(value[i * rows : (i + 1) * rows], "dp", OUTER) for i in range(2))
 
 
 def hop(hops, index):
@@ -208,27 +220,44 @@
     return local(body, shape(2 * half + experts, width), tuple(sent) + tuple(got), "settle", ties=ties)
 
 
-def experts(mine, other, up_weight, down_weight, half, ties=()):
+def preacts(latent, up_weight, rows):
     local_experts, width, hidden = up_weight.shape
+
+    def body(latent_ref, up, out_ref):
+        for i in range(local_experts):
+            out_ref[:, pl.ds(i * hidden, hidden)] = jnp.maximum(mxu(latent_ref[:rows, :], up[i]), 0.0)
+
+    return local(
+        body,
+        shape(rows, local_experts * hidden, F32),
+        (latent, up_weight),
+        "preacts",
+        limit=16,
+        flops=2 * rows * width * hidden * local_experts,
+    )
+
+
+def experts(positive, mine, other, up_weight, down_weight):
+    local_experts, width, hidden = up_weight.shape
+    half = positive.shape[0]
     rows = 2 * half
 
-    def body(mine_ref, other_ref, up, down, act_ref, lat_mine_ref, lat_other_ref, cot):
+    def body(positive_ref, mine_ref, other_ref, up, down, act_ref, lat_mine_ref, lat_other_ref, cot):
         me = lax.axis_index("expert")
         all_experts = mine_ref.shape[0] - rows
         ids = lax.broadcasted_iota(jnp.int32, (all_experts, 128), 0)
         slots = lax.broadcasted_iota(jnp.int32, (all_experts, 128), 1)
         pick = jnp.where(ids == slots + me * local_experts, 1.0, 0.0).astype(BF16)
-        sources = ((mine_ref, 0), (other_ref, half))
         probs = []
-        for src, place in sources:
+        for src, place in ((mine_ref, 0), (other_ref, half)):
             cot[pl.ds(place, half), :] = src[half:rows, :]
             probs.append(mxu(src[rows:, :half], pick, TN))
         probs = jnp.concatenate(probs, axis=0)
         total = None
         for i in range(local_experts):
             columns = pl.ds(i * hidden, hidden)
-            pre = [mxu(src[:half, :], up[i]) for src, _ in sources]
-            positive = jnp.maximum(jnp.concatenate(pre, axis=0), 0.0)
+            other = jnp.maximum(mxu(other_ref[:half, :], up[i]), 0.0)
+            positive = jnp.concatenate([positive_ref[:, columns], other], axis=0)
             weighted = positive * probs[:, i : i + 1]
             act_ref[:, columns] = (positive * weighted).astype(BF16)
             grad_act = mxu(cot[...], down[i], NT)
@@ -241,12 +270,11 @@
     return local(
         body,
         (shape(rows, local_experts * hidden), shape(half, width), shape(half, width)),
-        (mine, other, up_weight, down_weight),
+        (positive, mine, other, up_weight, down_weight),
         "experts",
-        ties=ties,
         scratch=[pltpu.VMEM((rows, width), BF16)],
         limit=24,
-        flops=2 * 3 * rows * width * hidden * local_experts,
+        flops=2 * 5 * half * width * hidden * local_experts,
     )
 
 
@@ -445,8 +473,8 @@
     part_other, *sent = project(tokens_x, in_proj, out_grad, expert_ids, route_probs, all_experts)
     sums = (half // 2 + all_experts, half // 2)
     hops = line_gather(tokens_x, "dp") if gather_groups else []
-    last = [lax.ppermute(hops[1][0], "dp", OUTER)] if hops else []
-    up, down = load(up_weight), load(down_weight)
+    last = hops_last(hops)
+    up, down = load(up_weight, down_weight)
     sent = streams(sent, xor_permute(part_other, "expert", 1))
     for step, stream_bits in enumerate(zip(bits, bits[::-1])):
         got = [xor_permute(value, "expert", bit) for value, bit in zip(sent, stream_bits)]
@@ -455,7 +483,8 @@
     mine = settle(sent, got, (order_of(bits), order_of(bits[::-1])), tok, all_experts, ties=(up, down, *hop(hops, 0)))
     other = xor_permute(mine, "expert", 1)
 
-    act, lat_mine, lat_other = experts(mine, other, up, down, half)
+    positive = preacts(mine, up, half)
+    act, lat_mine, lat_other = experts(positive, mine, other, up, down)
     out_mine, out_other = outputs(act, down, half)
     out_pieces = pieces_of(out_mine, xor_permute(out_other, "expert", 1), chips)
     lat_pieces = pieces_of(lat_mine, xor_permute(lat_other, "expert", 1), chips)
@@ -466,7 +495,7 @@
     if gather_groups:
         across = [xor_permute(latent_grad, "dp", m) for m in range(1, groups)]
         own = stack(across, tok, ties=last)
-        hops.append(tuple(last))
+        hops.append((jnp.concatenate(last, axis=0),))
     after = (own,) if gather_groups else ()
     sent = head(latent_grad, out_pieces[1:])
     got = scatter([None, *sent])
@@ -483,12 +512,14 @@
         far[0] = (own, xor_permute(own, "expert", 1))
     proj_grad = proj_round(x_all[0], (near, twins), far[0], 0, tok, None, False)
     if gather_groups:
-        ties = (proj_grad, input_grad, combined)
+        pieces = {k: xor_permute(own, "expert", 2 * k) for k in order[1:]}
         for k in order[1:]:
-            piece = xor_permute(own, "expert", 2 * k)
-            relay = stack([piece], piece.shape[0], ties)
+            if k == order[-1]:
+                ties = (proj_grad, input_grad, combined)
+            else:
+                ties = (pieces[order[-1]],) if k == order[-2] else ()
+            relay = stack([pieces[k]], pieces[k].shape[0], ties)
             far[k] = (relay, xor_permute(relay, "expert", 1))
-            ties = ()
     for k in order[1:]:
         proj_grad = proj_round(x_all[k], (near, twins), far[k], k, tok, proj_grad, k == order[-1])
     if not gather_groups:

time: 69.9 us -> 67.1 us (0.960)
  waiting for transfers between devices: 21.7 us -> 18 us
  starting transfers between devices: 31.5 us -> 32.5 us
  Pallas kernels: 15.6 us -> 14.9 us
    ppermute x1, waiting for transfers between devices: 5.15 us -> 2.11 us  [line_gather(): edge = lax.ppermute(middle, axis, OUTER)]
    ppermute x1 -> x2, starting transfers between devices: 1.29 us -> 2.57 us  [hops_last(): lax.ppermute(value[i * rows:(i + 1) * rows], 'dp', OUTER)]
  transfers between devices with their start and end apart: 31 -> 32, of which waited for: 10 -> 11; matrix products, arithmetic and copies ran while one was open for 0% -> 0% of each run, Pallas kernels for 17% -> 17%
where the time goes in v4:
time: 67.1 us; the launch traced here: 66.9 us
  starting transfers between devices  32.5 us (48%)
  waiting for transfers between devices  18 us (27%)
  Pallas kernels  14.9 us (22%)
  between operations  0.96 us (1%)
    ppermute x27, starting transfers between devices, xor_permute(): return lax.ppermute(value, axis, [(i, i ^ mask) for i in range(size)])  27.2 us
    ppermute x27, waiting for transfers between devices, xor_permute(): return lax.ppermute(value, axis, [(i, i ^ mask) for i in range(size)])  15.9 us
    pallas_call x20, Pallas kernels, local(): pl.pallas_call(kernel, out_shape=outs, in_specs=[spec] * len(args) + [ANY...  11.9 us
    pallas_call x4, Pallas kernels, proj_round(): pl.pallas_call(body, out_shape=shape(features, width, F32), in_specs=[VME...  3.01 us
    ppermute x2, starting transfers between devices, hops_last(): lax.ppermute(value[i * rows:(i + 1) * rows], 'dp', OUTER)  2.57 us
    ppermute x1, waiting for transfers between devices, line_gather(): edge = lax.ppermute(middle, axis, OUTER)  2.11 us
  transfers between devices with their start and end apart: 32, of which 11 were waited for; matrix products, arithmetic and copies ran while one was open for 0% of the time, Pallas kernels for 17%

profile of v4, /device:TPU:0, one launch (start us, length us, event | category | flops | bytes accessed | tf_op | source)
XLA Modules:
  0.0 66.9 jit_solution(15398028624337624526)
XLA Ops:
  0.6 2.0 %project.1 = (bf16[128,1024]{1,0:T(8,128)(2,1)S(1)}, bf16[96,1024]{1,0:T(8,128)(2,1)S(1)}, bf16[80,1024]{1,0:T(8,128)(2,1)S(1)}) custom-call(bf16[256,512]{1,0:T(8,128)(2,1)} %refs_0_.5, bf16[512,1024]{1,0:T(8,128)(2,1)} %refs_2_.3, bf16[32,1024]{1,0:T(8,128)(2,1)} %refs_2_.2, s32[8,32]{1,0:T(8,128)} %bitcast.2, f32[8,32]{1,0:T(8,128)} %bitcast.3), custom_call_target="tpu_custom_call" | custom-call | flops 268435456 | bytes 1048576 | tf_op jit(solution)/shard_map/project/pallas_call | solution.py:39
  2.6 0.5 collective-permute-start
  3.1 1.2 %collective-permute-done.refs_2_ = bf16[128,1024]{1,0:T(8,128)(2,1)S(1)} collective-permute-done((bf16[128,1024]{1,0:T(8,128)(2,1)S(1)}, bf16[128,1024]{1,0:T(8,128)(2,1)S(1)}, u32[]{:S(2)}, u32[]{:S(2)}) %collective-permute-start) | collective-permute-done | bytes 262176 | tf_op jit(solution)/shard_map/ppermute | solution.py:77
  4.3 0.1 streams.1
  4.3 2.9 %collective-permute-start.1 = (bf16[96,1024]{1,0:T(8,128)(2,1)S(1)}, bf16[96,1024]{1,0:T(8,128)(2,1)S(1)}, u32[]{:S(2)}, u32[]{:S(2)}) collective-permute-start(bf16[96,1024]{1,0:T(8,128)(2,1)S(1)} %get-tuple-element.35.refs_0_), channel_id=1, source_target_pairs={{0,2},{1,3},{2,0},{3,1},{4,6},{5,7},{6,4},{7,5},{8,10},{9,11},{10,... | collective-permute-start | bytes 589832 | tf_op jit(solution)/shard_map/ppermute | solution.py:77
  7.3 1.5 %collective-permute-start.2 = (bf16[80,1024]{1,0:T(8,128)(2,1)S(1)}, bf16[80,1024]{1,0:T(8,128)(2,1)S(1)}, u32[]{:S(2)}, u32[]{:S(2)}) collective-permute-start(bf16[80,1024]{1,0:T(8,128)(2,1)S(1)} %get-tuple-element.36.refs_1_), channel_id=1, source_target_pairs={{0,4},{1,5},{2,6},{3,7},{4,0},{5,1},{6,2},{7,3},{8,12},{9,13},{10,... | collective-permute-start | bytes 491528 | tf_op jit(solution)/shard_map/ppermute | solution.py:77
  8.8 1.6 %collective-permute-start.5 = (bf16[256,512]{1,0:T(8,128)(2,1)}, bf16[256,512]{1,0:T(8,128)(2,1)S(1)}, u32[]{:S(2)}, u32[]{:S(2)}) collective-permute-start(bf16[256,512]{1,0:T(8,128)(2,1)} %refs_0_.5), channel_id=1, source_target_pairs={{0,8},{8,0},{16,24},{24,16},{1,9},{9,1},{17,25},{25,17},{2,10},{10... | collective-permute-start | bytes 786440 | tf_op jit(solution)/shard_map/ppermute | solution.py:77
  10.4 0.7 collective-permute-start.6
  11.0 2.2 %collective-permute-done.2.refs_3_ = bf16[80,1024]{1,0:T(8,128)(2,1)S(1)} collective-permute-done((bf16[80,1024]{1,0:T(8,128)(2,1)S(1)}, bf16[80,1024]{1,0:T(8,128)(2,1)S(1)}, u32[]{:S(2)}, u32[]{:S(2)}) %collective-permute-start.2) | collective-permute-done | bytes 163872 | tf_op jit(solution)/shard_map/ppermute | solution.py:77
  13.2 0.1 merge.1
  13.3 1.6 %collective-permute-start.3 = (bf16[112,1024]{1,0:T(8,128)(2,1)S(1)}, bf16[112,1024]{1,0:T(8,128)(2,1)S(1)}, u32[]{:S(2)}, u32[]{:S(2)}) collective-permute-start(bf16[112,1024]{1,0:T(8,128)(2,1)S(1)} %get-tuple-element.37.refs_0_), channel_id=1, source_target_pairs={{0,4},{1,5},{2,6},{3,7},{4,0},{5,1},{6,2},{7,3},{8,12},{9,13},{10,... | collective-permute-start | bytes 688136 | tf_op jit(solution)/shard_map/ppermute | solution.py:77
  14.9 1.0 %collective-permute-start.4 = (bf16[96,1024]{1,0:T(8,128)(2,1)S(1)}, bf16[96,1024]{1,0:T(8,128)(2,1)S(1)}, u32[]{:S(2)}, u32[]{:S(2)}) collective-permute-start(bf16[96,1024]{1,0:T(8,128)(2,1)S(1)} %get-tuple-element.38.refs_1_), channel_id=1, source_target_pairs={{0,2},{1,3},{2,0},{3,1},{4,6},{5,7},{6,4},{7,5},{8,10},{9,11},{10,... | collective-permute-start | bytes 589832 | tf_op jit(solution)/shard_map/ppermute | solution.py:77
  15.9 2.9 %load.1 = (bf16[2,1024,768]{2,1,0:T(8,128)(2,1)S(1)}, bf16[2,768,1024]{2,1,0:T(8,128)(2,1)S(1)}) custom-call(bf16[2,1024,768]{2,1,0:T(8,128)(2,1)} %refs_0_.4, bf16[2,768,1024]{2,1,0:T(8,128)(2,1)} %refs_1_.3), custom_call_target="tpu_custom_call" | custom-call | bytes 1048576 | tf_op jit(solution)/shard_map/load/pallas_call | solution.py:39
  18.7 0.0 collective-permute-done.5.refs_6_.refs_1_
  18.8 0.0 collective-permute-done.6.refs_7_.refs_2_
  18.8 1.8 %collective-permute-done.4.refs_3_ = bf16[96,1024]{1,0:T(8,128)(2,1)S(1)} collective-permute-done((bf16[96,1024]{1,0:T(8,128)(2,1)S(1)}, bf16[96,1024]{1,0:T(8,128)(2,1)S(1)}, u32[]{:S(2)}, u32[]{:S(2)}) %collective-permute-start.4) | collective-permute-done | bytes 196640 | tf_op jit(solution)/shard_map/ppermute | solution.py:77
  20.6 0.1 settle.1.refs_0_.refs_1_
  20.7 0.1 collective-permute-start.7
  20.7 0.7 %collective-permute-start.13 = (bf16[256,512]{1,0:T(8,128)(2,1)S(1)}, bf16[256,512]{1,0:T(8,128)(2,1)S(1)}, u32[]{:S(2)}, u32[]{:S(2)}) collective-permute-start(bf16[256,512]{1,0:T(8,128)(2,1)S(1)} %collective-permute-done.5.refs_6_.refs_1_), channel_id=1, source_target_pairs={{8,16},{16,8},{9,17},{17,9},{10,18},{18,10},{11,19},{19,11},{12,20... | collective-permute-start | bytes 786440 | tf_op jit(solution)/shard_map/ppermute | solution.py:86
  21.4 1.3 %collective-permute-start.14 = (bf16[256,512]{1,0:T(8,128)(2,1)S(1)}, bf16[256,512]{1,0:T(8,128)(2,1)S(1)}, u32[]{:S(2)}, u32[]{:S(2)}) collective-permute-start(bf16[256,512]{1,0:T(8,128)(2,1)S(1)} %collective-permute-done.6.refs_7_.refs_2_), channel_id=1, source_target_pairs={{8,0},{16,24},{9,1},{17,25},{10,2},{18,26},{11,3},{19,27},{12,4},{... | collective-permute-start | bytes 786440 | tf_op jit(solution)/shard_map/ppermute | solution.py:87
  22.7 0.6 preacts.1.refs_0_
  23.3 3.1 %experts.1 = (bf16[256,1536]{1,0:T(8,128)(2,1)S(1)}, bf16[128,1024]{1,0:T(8,128)(2,1)S(1)}, bf16[128,1024]{1,0:T(8,128)(2,1)S(1)}) custom-call(f32[128,1536]{1,0:T(8,128)S(1)} %preacts.1.refs_0_, bf16[272,1024]{1,0:T(8,128)(2,1)S(1)} %settle.1.refs_0_.refs_1_, bf16[272,1024]{1,0:T(8,128)(2,1)S(1)} %collective-permute-done.7.refs_2_, ...), custom_call_target="tpu_custom_call" | custom-call | flops 2013265920 | bytes 1048576 | tf_op jit(solution)/shard_map/experts/pallas_call | solution.py:39
  26.4 0.6 collective-permute-start.9
  27.0 1.0 %outputs.1 = (bf16[128,1024]{1,0:T(8,128)(2,1)S(1)}, bf16[128,1024]{1,0:T(8,128)(2,1)S(1)}) custom-call(bf16[256,1536]{1,0:T(8,128)(2,1)S(1)} %get-tuple-element.41.refs_0_, bf16[2,768,1024]{2,1,0:T(8,128)(2,1)S(1)} %get-tuple-element.40.refs_5_.refs_4_.refs_1_), custom_call_target="tpu_custom_call" | custom-call | flops 805306368 | bytes 1048576 | tf_op jit(solution)/shard_map/outputs/pallas_call | solution.py:39
  27.9 0.0 copy-start.1
  27.9 0.1 collective-permute-start.8
  28.0 0.0 collective-permute-done.13.refs_4_.refs_3_
  28.1 1.3 %collective-permute-start.21 = (bf16[128,512]{1,0:T(8,128)(2,1)S(1)}, bf16[128,512]{1,0:T(8,128)(2,1)S(1)}, u32[]{:S(2)}, u32[]{:S(2)}) collective-permute-start(bf16[128,512]{1,0:T(8,128)(2,1)S(1)} %get-tuple-element.64), channel_id=1, source_target_pairs={{8,0},{16,24},{9,1},{17,25},{10,2},{18,26},{11,3},{19,27},{12,4},{... | collective-permute-start | bytes 393224 | tf_op jit(solution)/shard_map/ppermute | solution.py:96
  29.4 0.1 pieces.3
  29.5 1.2 %collective-permute-start.10 = (bf16[32,1024]{1,0:T(8,128)(2,1)S(1)}, bf16[32,1024]{1,0:T(8,128)(2,1)S(1)}, u32[]{:S(2)}, u32[]{:S(2)}) collective-permute-start(bf16[32,1024]{1,0:T(8,128)(2,1)S(1)} %get-tuple-element.48), channel_id=1, source_target_pairs={{0,2},{1,3},{2,0},{3,1},{4,6},{5,7},{6,4},{7,5},{8,10},{9,11},{10,... | collective-permute-start | bytes 196616 | tf_op jit(solution)/shard_map/ppermute | solution.py:77
  30.7 1.0 %collective-permute-start.11 = (bf16[32,1024]{1,0:T(8,128)(2,1)S(1)}, bf16[32,1024]{1,0:T(8,128)(2,1)S(1)}, u32[]{:S(2)}, u32[]{:S(2)}) collective-permute-start(bf16[32,1024]{1,0:T(8,128)(2,1)S(1)} %get-tuple-element.49), channel_id=1, source_target_pairs={{0,4},{1,5},{2,6},{3,7},{4,0},{5,1},{6,2},{7,3},{8,12},{9,13},{10,... | collective-permute-start | bytes 196616 | tf_op jit(solution)/shard_map/ppermute | solution.py:77
  31.6 2.1 %collective-permute-done.14.refs_5_.refs_4_ = bf16[256,512]{1,0:T(8,128)(2,1)S(1)} collective-permute-done((bf16[256,512]{1,0:T(8,128)(2,1)S(1)}, bf16[256,512]{1,0:T(8,128)(2,1)S(1)}, u32[]{:S(2)}, u32[]{:S(2)}) %collective-permute-start.14) | collective-permute-done | bytes 262176 | tf_op jit(solution)/shard_map/ppermute | solution.py:87
  33.8 1.6 %collective-permute-start.12 = (bf16[32,1024]{1,0:T(8,128)(2,1)S(1)}, bf16[32,1024]{1,0:T(8,128)(2,1)S(1)}, u32[]{:S(2)}, u32[]{:S(2)}) collective-permute-start(bf16[32,1024]{1,0:T(8,128)(2,1)S(1)} %get-tuple-element.50), channel_id=1, source_target_pairs={{0,6},{1,7},{2,4},{3,5},{4,2},{5,3},{6,0},{7,1},{8,14},{9,15},{10,... | collective-permute-start | bytes 196616 | tf_op jit(solution)/shard_map/ppermute | solution.py:77
  35.3 1.3 %collective-permute-start.22 = (bf16[128,512]{1,0:T(8,128)(2,1)S(1)}, bf16[128,512]{1,0:T(8,128)(2,1)S(1)}, u32[]{:S(2)}, u32[]{:S(2)}) collective-permute-start(bf16[128,512]{1,0:T(8,128)(2,1)S(1)} %get-tuple-element.63), channel_id=1, source_target_pairs={{8,0},{16,24},{9,1},{17,25},{10,2},{18,26},{11,3},{19,27},{12,4},{... | collective-permute-start | bytes 393224 | tf_op jit(solution)/shard_map/ppermute | solution.py:96
  36.6 0.1 pieces.2
  36.7 2.2 %collective-permute-done.12.refs_3_ = bf16[32,1024]{1,0:T(8,128)(2,1)S(1)} collective-permute-done((bf16[32,1024]{1,0:T(8,128)(2,1)S(1)}, bf16[32,1024]{1,0:T(8,128)(2,1)S(1)}, u32[]{:S(2)}, u32[]{:S(2)}) %collective-permute-start.12) | collective-permute-done | bytes 65568 | tf_op jit(solution)/shard_map/ppermute | solution.py:77
  39.0 2.8 %collective-permute-start.18 = (bf16[32,1024]{1,0:T(8,128)(2,1)S(1)}, bf16[32,1024]{1,0:T(8,128)(2,1)S(1)}, u32[]{:S(2)}, u32[]{:S(2)}) collective-permute-start(bf16[32,1024]{1,0:T(8,128)(2,1)S(1)} %add_pieces.2.refs_0_.refs_6_), channel_id=1, source_target_pairs={{0,8},{8,0},{16,24},{24,16},{1,9},{9,1},{17,25},{25,17},{2,10},{10... | collective-permute-start | bytes 196616 | tf_op jit(solution)/shard_map/ppermute | solution.py:77
  41.8 1.1 %collective-permute-start.15 = (bf16[64,1024]{1,0:T(8,128)(2,1)S(1)}, bf16[64,1024]{1,0:T(8,128)(2,1)S(1)}, u32[]{:S(2)}, u32[]{:S(2)}) collective-permute-start(bf16[64,1024]{1,0:T(8,128)(2,1)S(1)} %get-tuple-element.54), channel_id=1, source_target_pairs={{0,2},{1,3},{2,0},{3,1},{4,6},{5,7},{6,4},{7,5},{8,10},{9,11},{10,... | collective-permute-start | bytes 393224 | tf_op jit(solution)/shard_map/ppermute | solution.py:77
  42.9 0.9 %collective-permute-start.16 = (bf16[64,1024]{1,0:T(8,128)(2,1)S(1)}, bf16[64,1024]{1,0:T(8,128)(2,1)S(1)}, u32[]{:S(2)}, u32[]{:S(2)}) collective-permute-start(bf16[64,1024]{1,0:T(8,128)(2,1)S(1)} %get-tuple-element.55), channel_id=1, source_target_pairs={{0,4},{1,5},{2,6},{3,7},{4,0},{5,1},{6,2},{7,3},{8,12},{9,13},{10,... | collective-permute-start | bytes 393224 | tf_op jit(solution)/shard_map/ppermute | solution.py:77
  43.8 1.6 %collective-permute-start.17 = (bf16[64,1024]{1,0:T(8,128)(2,1)S(1)}, bf16[64,1024]{1,0:T(8,128)(2,1)S(1)}, u32[]{:S(2)}, u32[]{:S(2)}) collective-permute-start(bf16[64,1024]{1,0:T(8,128)(2,1)S(1)} %get-tuple-element.56), channel_id=1, source_target_pairs={{0,6},{1,7},{2,4},{3,5},{4,2},{5,3},{6,0},{7,1},{8,14},{9,15},{10,... | collective-permute-start | bytes 393224 | tf_op jit(solution)/shard_map/ppermute | solution.py:77
  45.4 1.0 %collective-permute-start.19 = (bf16[32,1024]{1,0:T(8,128)(2,1)S(1)}, bf16[32,1024]{1,0:T(8,128)(2,1)S(1)}, u32[]{:S(2)}, u32[]{:S(2)}) collective-permute-start(bf16[32,1024]{1,0:T(8,128)(2,1)S(1)} %add_pieces.2.refs_0_.refs_6_), channel_id=1, source_target_pairs={{0,16},{8,24},{16,0},{24,8},{1,17},{9,25},{17,1},{25,9},{2,18},{10... | collective-permute-start | bytes 196616 | tf_op jit(solution)/shard_map/ppermute | solution.py:77
  46.4 1.5 %collective-permute-start.20 = (bf16[32,1024]{1,0:T(8,128)(2,1)S(1)}, bf16[32,1024]{1,0:T(8,128)(2,1)S(1)}, u32[]{:S(2)}, u32[]{:S(2)}) collective-permute-start(bf16[32,1024]{1,0:T(8,128)(2,1)S(1)} %add_pieces.2.refs_0_.refs_6_), channel_id=1, source_target_pairs={{0,24},{8,16},{16,8},{24,0},{1,25},{9,17},{17,9},{25,1},{2,26},{10... | collective-permute-start | bytes 196616 | tf_op jit(solution)/shard_map/ppermute | solution.py:77
  47.9 2.9 %collective-permute-done.19.refs_1_ = bf16[32,1024]{1,0:T(8,128)(2,1)S(1)} collective-permute-done((bf16[32,1024]{1,0:T(8,128)(2,1)S(1)}, bf16[32,1024]{1,0:T(8,128)(2,1)S(1)}, u32[]{:S(2)}, u32[]{:S(2)}) %collective-permute-start.19) | collective-permute-done | bytes 65568 | tf_op jit(solution)/shard_map/ppermute | solution.py:77
  50.8 1.8 %collective-permute-done.20.refs_2_ = bf16[32,1024]{1,0:T(8,128)(2,1)S(1)} collective-permute-done((bf16[32,1024]{1,0:T(8,128)(2,1)S(1)}, bf16[32,1024]{1,0:T(8,128)(2,1)S(1)}, u32[]{:S(2)}, u32[]{:S(2)}) %collective-permute-start.20) | collective-permute-done | bytes 65568 | tf_op jit(solution)/shard_map/ppermute | solution.py:77
  52.6 1.4 %collective-permute-start.30 = (bf16[96,1024]{1,0:T(8,128)(2,1)S(1)}, bf16[96,1024]{1,0:T(8,128)(2,1)S(1)}, u32[]{:S(2)}, u32[]{:S(2)}) collective-permute-start(bf16[96,1024]{1,0:T(8,128)(2,1)S(1)} %stack.5.refs_4_.refs_3_), channel_id=1, source_target_pairs={{0,6},{1,7},{2,4},{3,5},{4,2},{5,3},{6,0},{7,1},{8,14},{9,15},{10,... | collective-permute-start | bytes 589832 | tf_op jit(solution)/shard_map/ppermute | solution.py:77
  54.0 1.1 %collective-permute-start.25 = (bf16[96,1024]{1,0:T(8,128)(2,1)S(1)}, bf16[96,1024]{1,0:T(8,128)(2,1)S(1)}, u32[]{:S(2)}, u32[]{:S(2)}) collective-permute-start(bf16[96,1024]{1,0:T(8,128)(2,1)S(1)} %stack.5.refs_4_.refs_3_), channel_id=1, source_target_pairs={{0,2},{1,3},{2,0},{3,1},{4,6},{5,7},{6,4},{7,5},{8,10},{9,11},{10,... | collective-permute-start | bytes 589832 | tf_op jit(solution)/shard_map/ppermute | solution.py:77
  55.2 1.0 %collective-permute-start.28 = (bf16[96,1024]{1,0:T(8,128)(2,1)S(1)}, bf16[96,1024]{1,0:T(8,128)(2,1)S(1)}, u32[]{:S(2)}, u32[]{:S(2)}) collective-permute-start(bf16[96,1024]{1,0:T(8,128)(2,1)S(1)} %stack.5.refs_4_.refs_3_), channel_id=1, source_target_pairs={{0,4},{1,5},{2,6},{3,7},{4,0},{5,1},{6,2},{7,3},{8,12},{9,13},{10,... | collective-permute-start | bytes 589832 | tf_op jit(solution)/shard_map/ppermute | solution.py:77
  56.2 0.1 collective-permute-start.23
  56.3 0.5 collective-permute-start.24
  56.8 0.1 arrange.1
  56.9 0.7 %add_pieces.3.refs_3_ = bf16[32,1024]{1,0:T(8,128)(2,1)} custom-call(bf16[32,1024]{1,0:T(8,128)(2,1)S(1)} %get-tuple-element.44.refs_0_, bf16[64,1024]{1,0:T(8,128)(2,1)S(1)} %collective-permute-done.15.refs_1_, bf16[64,1024]{1,0:T(8,128)(2,1)S(1)} %collective-permute-done.16.refs_2_, bf16[64,1024]{1,0:T(8,128)(2,1)S(1)} %collective-permute-done.17.refs_3_, ...), custom_call_target="tpu_custom_call" | custom-call | bytes 1048576 | tf_op jit(solution)/shard_map/add_pieces/pallas_call | solution.py:39
  57.6 1.7 %collective-permute-done.30.refs_0_ = bf16[96,1024]{1,0:T(8,128)(2,1)S(1)} collective-permute-done((bf16[96,1024]{1,0:T(8,128)(2,1)S(1)}, bf16[96,1024]{1,0:T(8,128)(2,1)S(1)}, u32[]{:S(2)}, u32[]{:S(2)}) %collective-permute-start.30) | collective-permute-done | bytes 196640 | tf_op jit(solution)/shard_map/ppermute | solution.py:77
  59.3 0.0 copy-start.3
  59.3 1.6 %collective-permute-done.25.refs_0_.refs_1_ = bf16[96,1024]{1,0:T(8,128)(2,1)S(1)} collective-permute-done((bf16[96,1024]{1,0:T(8,128)(2,1)S(1)}, bf16[96,1024]{1,0:T(8,128)(2,1)S(1)}, u32[]{:S(2)}, u32[]{:S(2)}) %collective-permute-start.25) | collective-permute-done | bytes 196640 | tf_op jit(solution)/shard_map/ppermute | solution.py:77
  60.9 0.4 collective-permute-done.28.refs_0_
  61.4 0.2 collective-permute-start.29
  61.6 1.2 %input_grads.1.refs_2_ = bf16[256,512]{1,0:T(8,128)(2,1)} custom-call(bf16[128,1024]{1,0:T(8,128)(2,1)S(1)} %stack.6.refs_0_.refs_1_, bf16[128,1024]{1,0:T(8,128)(2,1)S(1)} %constant_dynamic-update-slice_fusion.refs_1_.refs_2_, bf16[512,1024]{1,0:T(8,128)(2,1)S(1)} %copy-done), custom_call_target="tpu_custom_call" | custom-call | flops 268435456 | bytes 1048576 | tf_op jit(solution)/shard_map/input_grads/pallas_call | solution.py:39
  62.8 0.5 proj_round.4.refs_1_.refs_5_
  63.3 0.5 copy-done.2
  63.7 0.5 collective-permute-start.27
  64.2 0.5 proj_round.5.refs_5_
  64.7 0.5 proj_round.6.refs_5_
  65.2 0.1 collective-permute-done.27.refs_4_
  65.3 1.6 %proj_round.7 = f32[512,1024]{1,0:T(8,128)} custom-call(bf16[256,512]{1,0:T(8,128)(2,1)S(1)} %get-tuple-element.57.refs_0_, bf16[128,1024]{1,0:T(8,128)(2,1)S(1)} %stack.6.refs_0_.refs_1_, bf16[128,1024]{1,0:T(8,128)(2,1)S(1)} %constant_dynamic-update-slice_fusion.refs_1_.refs_2_, bf16[96,1024]{1,0:T(8,128)(2,1)S(1)} %stack.7.refs_3_, ...), custom_call_target="tpu_custom_call" | custom-call | flops 268435456 | bytes 4194304 | tf_op jit(solution)/shard_map/proj_round/pallas_call | solution.py:447
  (37 shorter events, 0.3 us)
Async XLA Ops:
  2.6 1.7 %collective-permute-start = (bf16[128,1024]{1,0:T(8,128)(2,1)S(1)}, bf16[128,1024]{1,0:T(8,128)(2,1)S(1)}, u32[]{:S(2)}, u32[]{:S(2)}) collective-permute-start(bf16[128,1024]{1,0:T(8,128)(2,1)S(1)} %get-tuple-element.34), channel_id=1, source_target_pairs={{0,1},{1,0},{2,3},{3,2},{4,5},{5,4},{6,7},{7,6},{8,9},{9,8},{10,11... | collective-permute-start | bytes 786440 | tf_op jit(solution)/shard_map/ppermute | solution.py:77
  4.3 8.9 %collective-permute-start.1 = (bf16[96,1024]{1,0:T(8,128)(2,1)S(1)}, bf16[96,1024]{1,0:T(8,128)(2,1)S(1)}, u32[]{:S(2)}, u32[]{:S(2)}) collective-permute-start(bf16[96,1024]{1,0:T(8,128)(2,1)S(1)} %get-tuple-element.35.refs_0_), channel_id=1, source_target_pairs={{0,2},{1,3},{2,0},{3,1},{4,6},{5,7},{6,4},{7,5},{8,10},{9,11},{10,... | collective-permute-start | bytes 589832 | tf_op jit(solution)/shard_map/ppermute | solution.py:77
  7.3 6.0 %collective-permute-start.2 = (bf16[80,1024]{1,0:T(8,128)(2,1)S(1)}, bf16[80,1024]{1,0:T(8,128)(2,1)S(1)}, u32[]{:S(2)}, u32[]{:S(2)}) collective-permute-start(bf16[80,1024]{1,0:T(8,128)(2,1)S(1)} %get-tuple-element.36.refs_1_), channel_id=1, source_target_pairs={{0,4},{1,5},{2,6},{3,7},{4,0},{5,1},{6,2},{7,3},{8,12},{9,13},{10,... | collective-permute-start | bytes 491528 | tf_op jit(solution)/shard_map/ppermute | solution.py:77
  8.8 10.0 %collective-permute-start.5 = (bf16[256,512]{1,0:T(8,128)(2,1)}, bf16[256,512]{1,0:T(8,128)(2,1)S(1)}, u32[]{:S(2)}, u32[]{:S(2)}) collective-permute-start(bf16[256,512]{1,0:T(8,128)(2,1)} %refs_0_.5), channel_id=1, source_target_pairs={{0,8},{8,0},{16,24},{24,16},{1,9},{9,1},{17,25},{25,17},{2,10},{10... | collective-permute-start | bytes 786440 | tf_op jit(solution)/shard_map/ppermute | solution.py:77
  10.4 8.4 %collective-permute-start.6 = (bf16[256,512]{1,0:T(8,128)(2,1)}, bf16[256,512]{1,0:T(8,128)(2,1)S(1)}, u32[]{:S(2)}, u32[]{:S(2)}) collective-permute-start(bf16[256,512]{1,0:T(8,128)(2,1)} %refs_0_.5), channel_id=1, source_target_pairs={{8,16},{16,8},{9,17},{17,9},{10,18},{18,10},{11,19},{19,11},{12,20... | collective-permute-start | bytes 786440 | tf_op jit(solution)/shard_map/ppermute | solution.py:85
  13.3 7.3 %collective-permute-start.3 = (bf16[112,1024]{1,0:T(8,128)(2,1)S(1)}, bf16[112,1024]{1,0:T(8,128)(2,1)S(1)}, u32[]{:S(2)}, u32[]{:S(2)}) collective-permute-start(bf16[112,1024]{1,0:T(8,128)(2,1)S(1)} %get-tuple-element.37.refs_0_), channel_id=1, source_target_pairs={{0,4},{1,5},{2,6},{3,7},{4,0},{5,1},{6,2},{7,3},{8,12},{9,13},{10,... | collective-permute-start | bytes 688136 | tf_op jit(solution)/shard_map/ppermute | solution.py:77
  14.9 5.7 %collective-permute-start.4 = (bf16[96,1024]{1,0:T(8,128)(2,1)S(1)}, bf16[96,1024]{1,0:T(8,128)(2,1)S(1)}, u32[]{:S(2)}, u32[]{:S(2)}) collective-permute-start(bf16[96,1024]{1,0:T(8,128)(2,1)S(1)} %get-tuple-element.38.refs_1_), channel_id=1, source_target_pairs={{0,2},{1,3},{2,0},{3,1},{4,6},{5,7},{6,4},{7,5},{8,10},{9,11},{10,... | collective-permute-start | bytes 589832 | tf_op jit(solution)/shard_map/ppermute | solution.py:77
  20.7 2.7 %collective-permute-start.7 = (bf16[272,1024]{1,0:T(8,128)(2,1)S(1)}, bf16[272,1024]{1,0:T(8,128)(2,1)S(1)}, u32[]{:S(2)}, u32[]{:S(2)}) collective-permute-start(bf16[272,1024]{1,0:T(8,128)(2,1)S(1)} %settle.1.refs_0_.refs_1_), channel_id=1, source_target_pairs={{0,1},{1,0},{2,3},{3,2},{4,5},{5,4},{6,7},{7,6},{8,9},{9,8},{10,11... | collective-permute-start | bytes 1671176 | tf_op jit(solution)/shard_map/ppermute | solution.py:77
  20.7 7.3 %collective-permute-start.13 = (bf16[256,512]{1,0:T(8,128)(2,1)S(1)}, bf16[256,512]{1,0:T(8,128)(2,1)S(1)}, u32[]{:S(2)}, u32[]{:S(2)}) collective-permute-start(bf16[256,512]{1,0:T(8,128)(2,1)S(1)} %collective-permute-done.5.refs_6_.refs_1_), channel_id=1, source_target_pairs={{8,16},{16,8},{9,17},{17,9},{10,18},{18,10},{11,19},{19,11},{12,20... | collective-permute-start | bytes 786440 | tf_op jit(solution)/shard_map/ppermute | solution.py:86
  21.4 12.3 %collective-permute-start.14 = (bf16[256,512]{1,0:T(8,128)(2,1)S(1)}, bf16[256,512]{1,0:T(8,128)(2,1)S(1)}, u32[]{:S(2)}, u32[]{:S(2)}) collective-permute-start(bf16[256,512]{1,0:T(8,128)(2,1)S(1)} %collective-permute-done.6.refs_7_.refs_2_), channel_id=1, source_target_pairs={{8,0},{16,24},{9,1},{17,25},{10,2},{18,26},{11,3},{19,27},{12,4},{... | collective-permute-start | bytes 786440 | tf_op jit(solution)/shard_map/ppermute | solution.py:87
  26.4 3.0 %collective-permute-start.9 = (bf16[128,1024]{1,0:T(8,128)(2,1)S(1)}, bf16[128,1024]{1,0:T(8,128)(2,1)S(1)}, u32[]{:S(2)}, u32[]{:S(2)}) collective-permute-start(bf16[128,1024]{1,0:T(8,128)(2,1)S(1)} %get-tuple-element.46), channel_id=1, source_target_pairs={{0,1},{1,0},{2,3},{3,2},{4,5},{5,4},{6,7},{7,6},{8,9},{9,8},{10,11... | collective-permute-start | bytes 786440 | tf_op jit(solution)/shard_map/ppermute | solution.py:77
  27.9 28.9 %copy-start.1 = (bf16[256,512]{1,0:T(8,128)(2,1)S(1)}, bf16[256,512]{1,0:T(8,128)(2,1)}, u32[]{:S(2)}) copy-start(bf16[256,512]{1,0:T(8,128)(2,1)} %refs_0_.5) | copy-start | bytes 786436
  27.9 7.4 %collective-permute-start.8 = (bf16[128,1024]{1,0:T(8,128)(2,1)S(1)}, bf16[128,1024]{1,0:T(8,128)(2,1)S(1)}, u32[]{:S(2)}, u32[]{:S(2)}) collective-permute-start(bf16[128,1024]{1,0:T(8,128)(2,1)S(1)} %get-tuple-element.43), channel_id=1, source_target_pairs={{0,1},{1,0},{2,3},{3,2},{4,5},{5,4},{6,7},{7,6},{8,9},{9,8},{10,11... | collective-permute-start | bytes 786440 | tf_op jit(solution)/shard_map/ppermute | solution.py:77
  28.1 15.8 %collective-permute-start.21 = (bf16[128,512]{1,0:T(8,128)(2,1)S(1)}, bf16[128,512]{1,0:T(8,128)(2,1)S(1)}, u32[]{:S(2)}, u32[]{:S(2)}) collective-permute-start(bf16[128,512]{1,0:T(8,128)(2,1)S(1)} %get-tuple-element.64), channel_id=1, source_target_pairs={{8,0},{16,24},{9,1},{17,25},{10,2},{18,26},{11,3},{19,27},{12,4},{... | collective-permute-start | bytes 393224 | tf_op jit(solution)/shard_map/ppermute | solution.py:96
  29.5 7.2 %collective-permute-start.10 = (bf16[32,1024]{1,0:T(8,128)(2,1)S(1)}, bf16[32,1024]{1,0:T(8,128)(2,1)S(1)}, u32[]{:S(2)}, u32[]{:S(2)}) collective-permute-start(bf16[32,1024]{1,0:T(8,128)(2,1)S(1)} %get-tuple-element.48), channel_id=1, source_target_pairs={{0,2},{1,3},{2,0},{3,1},{4,6},{5,7},{6,4},{7,5},{8,10},{9,11},{10,... | collective-permute-start | bytes 196616 | tf_op jit(solution)/shard_map/ppermute | solution.py:77
  30.7 6.0 %collective-permute-start.11 = (bf16[32,1024]{1,0:T(8,128)(2,1)S(1)}, bf16[32,1024]{1,0:T(8,128)(2,1)S(1)}, u32[]{:S(2)}, u32[]{:S(2)}) collective-permute-start(bf16[32,1024]{1,0:T(8,128)(2,1)S(1)} %get-tuple-element.49), channel_id=1, source_target_pairs={{0,4},{1,5},{2,6},{3,7},{4,0},{5,1},{6,2},{7,3},{8,12},{9,13},{10,... | collective-permute-start | bytes 196616 | tf_op jit(solution)/shard_map/ppermute | solution.py:77
  33.8 5.2 %collective-permute-start.12 = (bf16[32,1024]{1,0:T(8,128)(2,1)S(1)}, bf16[32,1024]{1,0:T(8,128)(2,1)S(1)}, u32[]{:S(2)}, u32[]{:S(2)}) collective-permute-start(bf16[32,1024]{1,0:T(8,128)(2,1)S(1)} %get-tuple-element.50), channel_id=1, source_target_pairs={{0,6},{1,7},{2,4},{3,5},{4,2},{5,3},{6,0},{7,1},{8,14},{9,15},{10,... | collective-permute-start | bytes 196616 | tf_op jit(solution)/shard_map/ppermute | solution.py:77
  35.3 10.1 %collective-permute-start.22 = (bf16[128,512]{1,0:T(8,128)(2,1)S(1)}, bf16[128,512]{1,0:T(8,128)(2,1)S(1)}, u32[]{:S(2)}, u32[]{:S(2)}) collective-permute-start(bf16[128,512]{1,0:T(8,128)(2,1)S(1)} %get-tuple-element.63), channel_id=1, source_target_pairs={{8,0},{16,24},{9,1},{17,25},{10,2},{18,26},{11,3},{19,27},{12,4},{... | collective-permute-start | bytes 393224 | tf_op jit(solution)/shard_map/ppermute | solution.py:96
  39.0 7.5 %collective-permute-start.18 = (bf16[32,1024]{1,0:T(8,128)(2,1)S(1)}, bf16[32,1024]{1,0:T(8,128)(2,1)S(1)}, u32[]{:S(2)}, u32[]{:S(2)}) collective-permute-start(bf16[32,1024]{1,0:T(8,128)(2,1)S(1)} %add_pieces.2.refs_0_.refs_6_), channel_id=1, source_target_pairs={{0,8},{8,0},{16,24},{24,16},{1,9},{9,1},{17,25},{25,17},{2,10},{10... | collective-permute-start | bytes 196616 | tf_op jit(solution)/shard_map/ppermute | solution.py:77
  41.8 13.4 %collective-permute-start.15 = (bf16[64,1024]{1,0:T(8,128)(2,1)S(1)}, bf16[64,1024]{1,0:T(8,128)(2,1)S(1)}, u32[]{:S(2)}, u32[]{:S(2)}) collective-permute-start(bf16[64,1024]{1,0:T(8,128)(2,1)S(1)} %get-tuple-element.54), channel_id=1, source_target_pairs={{0,2},{1,3},{2,0},{3,1},{4,6},{5,7},{6,4},{7,5},{8,10},{9,11},{10,... | collective-permute-start | bytes 393224 | tf_op jit(solution)/shard_map/ppermute | solution.py:77
  42.9 13.2 %collective-permute-start.16 = (bf16[64,1024]{1,0:T(8,128)(2,1)S(1)}, bf16[64,1024]{1,0:T(8,128)(2,1)S(1)}, u32[]{:S(2)}, u32[]{:S(2)}) collective-permute-start(bf16[64,1024]{1,0:T(8,128)(2,1)S(1)} %get-tuple-element.55), channel_id=1, source_target_pairs={{0,4},{1,5},{2,6},{3,7},{4,0},{5,1},{6,2},{7,3},{8,12},{9,13},{10,... | collective-permute-start | bytes 393224 | tf_op jit(solution)/shard_map/ppermute | solution.py:77
  43.8 17.8 %copy-start = (bf16[512,1024]{1,0:T(8,128)(2,1)S(1)}, bf16[512,1024]{1,0:T(8,128)(2,1)}, u32[]{:S(2)}) copy-start(bf16[512,1024]{1,0:T(8,128)(2,1)} %refs_2_.3) | copy-start | bytes 3145732
  43.8 12.3 %collective-permute-start.17 = (bf16[64,1024]{1,0:T(8,128)(2,1)S(1)}, bf16[64,1024]{1,0:T(8,128)(2,1)S(1)}, u32[]{:S(2)}, u32[]{:S(2)}) collective-permute-start(bf16[64,1024]{1,0:T(8,128)(2,1)S(1)} %get-tuple-element.56), channel_id=1, source_target_pairs={{0,6},{1,7},{2,4},{3,5},{4,2},{5,3},{6,0},{7,1},{8,14},{9,15},{10,... | collective-permute-start | bytes 393224 | tf_op jit(solution)/shard_map/ppermute | solution.py:77
  45.4 5.4 %collective-permute-start.19 = (bf16[32,1024]{1,0:T(8,128)(2,1)S(1)}, bf16[32,1024]{1,0:T(8,128)(2,1)S(1)}, u32[]{:S(2)}, u32[]{:S(2)}) collective-permute-start(bf16[32,1024]{1,0:T(8,128)(2,1)S(1)} %add_pieces.2.refs_0_.refs_6_), channel_id=1, source_target_pairs={{0,16},{8,24},{16,0},{24,8},{1,17},{9,25},{17,1},{25,9},{2,18},{10... | collective-permute-start | bytes 196616 | tf_op jit(solution)/shard_map/ppermute | solution.py:77
  46.4 6.2 %collective-permute-start.20 = (bf16[32,1024]{1,0:T(8,128)(2,1)S(1)}, bf16[32,1024]{1,0:T(8,128)(2,1)S(1)}, u32[]{:S(2)}, u32[]{:S(2)}) collective-permute-start(bf16[32,1024]{1,0:T(8,128)(2,1)S(1)} %add_pieces.2.refs_0_.refs_6_), channel_id=1, source_target_pairs={{0,24},{8,16},{16,8},{24,0},{1,25},{9,17},{17,9},{25,1},{2,26},{10... | collective-permute-start | bytes 196616 | tf_op jit(solution)/shard_map/ppermute | solution.py:77
  52.6 6.7 %collective-permute-start.30 = (bf16[96,1024]{1,0:T(8,128)(2,1)S(1)}, bf16[96,1024]{1,0:T(8,128)(2,1)S(1)}, u32[]{:S(2)}, u32[]{:S(2)}) collective-permute-start(bf16[96,1024]{1,0:T(8,128)(2,1)S(1)} %stack.5.refs_4_.refs_3_), channel_id=1, source_target_pairs={{0,6},{1,7},{2,4},{3,5},{4,2},{5,3},{6,0},{7,1},{8,14},{9,15},{10,... | collective-permute-start | bytes 589832 | tf_op jit(solution)/shard_map/ppermute | solution.py:77
  54.0 6.9 %collective-permute-start.25 = (bf16[96,1024]{1,0:T(8,128)(2,1)S(1)}, bf16[96,1024]{1,0:T(8,128)(2,1)S(1)}, u32[]{:S(2)}, u32[]{:S(2)}) collective-permute-start(bf16[96,1024]{1,0:T(8,128)(2,1)S(1)} %stack.5.refs_4_.refs_3_), channel_id=1, source_target_pairs={{0,2},{1,3},{2,0},{3,1},{4,6},{5,7},{6,4},{7,5},{8,10},{9,11},{10,... | collective-permute-start | bytes 589832 | tf_op jit(solution)/shard_map/ppermute | solution.py:77
  55.2 6.2 %collective-permute-start.28 = (bf16[96,1024]{1,0:T(8,128)(2,1)S(1)}, bf16[96,1024]{1,0:T(8,128)(2,1)S(1)}, u32[]{:S(2)}, u32[]{:S(2)}) collective-permute-start(bf16[96,1024]{1,0:T(8,128)(2,1)S(1)} %stack.5.refs_4_.refs_3_), channel_id=1, source_target_pairs={{0,4},{1,5},{2,6},{3,7},{4,0},{5,1},{6,2},{7,3},{8,12},{9,13},{10,... | collective-permute-start | bytes 589832 | tf_op jit(solution)/shard_map/ppermute | solution.py:77
  56.2 5.3 %collective-permute-start.23 = (bf16[64,1024]{1,0:T(8,128)(2,1)S(1)}, bf16[64,1024]{1,0:T(8,128)(2,1)S(1)}, u32[]{:S(2)}, u32[]{:S(2)}) collective-permute-start(bf16[64,1024]{1,0:T(8,128)(2,1)S(1)} %get-tuple-element.62), channel_id=1, source_target_pairs={{0,1},{1,0},{2,3},{3,2},{4,5},{5,4},{6,7},{7,6},{8,9},{9,8},{10,11... | collective-permute-start | bytes 393224 | tf_op jit(solution)/shard_map/ppermute | solution.py:77
  56.3 5.2 %collective-permute-start.24 = (bf16[64,1024]{1,0:T(8,128)(2,1)S(1)}, bf16[64,1024]{1,0:T(8,128)(2,1)S(1)}, u32[]{:S(2)}, u32[]{:S(2)}) collective-permute-start(bf16[64,1024]{1,0:T(8,128)(2,1)S(1)} %get-tuple-element.61), channel_id=1, source_target_pairs={{0,1},{1,0},{2,3},{3,2},{4,5},{5,4},{6,7},{7,6},{8,9},{9,8},{10,11... | collective-permute-start | bytes 393224 | tf_op jit(solution)/shard_map/ppermute | solution.py:77
  59.3 3.5 %collective-permute-start.26 = (bf16[96,1024]{1,0:T(8,128)(2,1)S(1)}, bf16[96,1024]{1,0:T(8,128)(2,1)S(1)}, u32[]{:S(2)}, u32[]{:S(2)}) collective-permute-start(bf16[96,1024]{1,0:T(8,128)(2,1)S(1)} %stack.5.refs_4_.refs_3_), channel_id=1, source_target_pairs={{0,1},{1,0},{2,3},{3,2},{4,5},{5,4},{6,7},{7,6},{8,9},{9,8},{10,11... | collective-permute-start | bytes 589832 | tf_op jit(solution)/shard_map/ppermute | solution.py:77
  59.3 3.9 %copy-start.3 = (bf16[32,1024]{1,0:T(8,128)(2,1)S(1)}, bf16[32,1024]{1,0:T(8,128)(2,1)}, u32[]{:S(2)}) copy-start(bf16[32,1024]{1,0:T(8,128)(2,1)} %add_pieces.3.refs_3_) | copy-start | bytes 196612
  60.9 3.3 %collective-permute-start.31 = (bf16[96,1024]{1,0:T(8,128)(2,1)S(1)}, bf16[96,1024]{1,0:T(8,128)(2,1)S(1)}, u32[]{:S(2)}, u32[]{:S(2)}) collective-permute-start(bf16[96,1024]{1,0:T(8,128)(2,1)S(1)} %stack.9.refs_3_), channel_id=1, source_target_pairs={{0,1},{1,0},{2,3},{3,2},{4,5},{5,4},{6,7},{7,6},{8,9},{9,8},{10,11... | collective-permute-start | bytes 589832 | tf_op jit(solution)/shard_map/ppermute | solution.py:77
  61.4 3.3 %collective-permute-start.29 = (bf16[96,1024]{1,0:T(8,128)(2,1)S(1)}, bf16[96,1024]{1,0:T(8,128)(2,1)S(1)}, u32[]{:S(2)}, u32[]{:S(2)}) collective-permute-start(bf16[96,1024]{1,0:T(8,128)(2,1)S(1)} %stack.8.refs_3_), channel_id=1, source_target_pairs={{0,1},{1,0},{2,3},{3,2},{4,5},{5,4},{6,7},{7,6},{8,9},{9,8},{10,11... | collective-permute-start | bytes 589832 | tf_op jit(solution)/shard_map/ppermute | solution.py:77
  62.8 0.9 %copy-start.2 = (bf16[256,512]{1,0:T(8,128)(2,1)S(1)}, bf16[256,512]{1,0:T(8,128)(2,1)}, u32[]{:S(2)}) copy-start(bf16[256,512]{1,0:T(8,128)(2,1)} %input_grads.1.refs_2_) | copy-start | bytes 786436
  63.7 1.5 %collective-permute-start.27 = (bf16[96,1024]{1,0:T(8,128)(2,1)S(1)}, bf16[96,1024]{1,0:T(8,128)(2,1)S(1)}, u32[]{:S(2)}, u32[]{:S(2)}) collective-permute-start(bf16[96,1024]{1,0:T(8,128)(2,1)S(1)} %stack.7.refs_3_), channel_id=1, source_target_pairs={{0,1},{1,0},{2,3},{3,2},{4,5},{5,4},{6,7},{7,6},{8,9},{9,8},{10,11... | collective-permute-start | bytes 589832 | tf_op jit(solution)/shard_map/ppermute | solution.py:77

commit v5 on v4

--- a/solution.py
+++ b/solution.py
@@ -77,29 +77,6 @@
     return lax.ppermute(value, axis, [(i, i ^ mask) for i in range(size)])
 
 
-INNER, OUTER = [(1, 2), (2, 1)], [(1, 0), (2, 3)]
-
-
-def line_gather(value, axis):
-    near = xor_permute(value, axis, 1)
-    middle = lax.ppermute(value, axis, INNER)
-    middle_far = lax.ppermute(near, axis, INNER)
-    edge = lax.ppermute(middle, axis, OUTER)
-    return [(near, middle), (middle_far, edge)]
-
-
-def hops_last(hops):
-    if not hops:
-        return ()
-    value = hops[1][0]
-    rows = value.shape[0] // 2
-    return tuple(lax.ppermute(value[i * rows : (i + 1) * rows], "dp", OUTER) for i in range(2))
-
-
-def hop(hops, index):
-    return hops[index] if index < len(hops) else ()
-
-
 def order_of(bits):
     masks = [0]
     for bit in bits:
@@ -121,10 +98,11 @@
     args = (x, in_proj, out_grad, expert_ids.T, route_probs.T)
 
     def body(*refs):
-        other_ref, first_ref, second_ref, rows_ref = refs[5:9]
-        x_ref, proj_ref, grad_ref, ids_ref, probs_ref = refs[9:14]
+        other_ref, first_ref, second_ref, x_ref, rows_ref = refs[5:10]
+        proj_ref, grad_ref, ids_ref, probs_ref = refs[10:14]
+        held = (x_ref, proj_ref, grad_ref, ids_ref, probs_ref)
         copies = [
-            pltpu.make_async_copy(refs[i], refs[9 + i], refs[14].at[i]) for i in range(len(args))
+            pltpu.make_async_copy(refs[i], held[i], refs[14].at[i]) for i in range(len(args))
         ]
         for copy in copies:
             copy.start()
@@ -154,15 +132,28 @@
 
     return local(
         body,
-        (shape(half, width), shape(mid + all_experts + cot, width), shape(mid + cot, width)),
+        (
+            shape(half, width),
+            shape(mid + all_experts + cot, width),
+            shape(mid + cot, width),
+            pltpu.VMEM(x.shape, x.dtype),
+        ),
         args,
         "project",
         scratch=[pltpu.VMEM((rows, features), BF16)]
-        + [pltpu.VMEM(value.shape, value.dtype) for value in args]
+        + [pltpu.VMEM(value.shape, value.dtype) for value in args[1:]]
         + [pltpu.SemaphoreType.DMA((len(args),))],
         pin=pltpu.HBM,
         flops=2 * rows * features * width,
     )
+
+
+def spread(value, count):
+    def body(src, dst):
+        for i in range(count):
+            dst[i] = src[...]
+
+    return local(body, pltpu.VMEM((count,) + value.shape, value.dtype), (value,), "spread")
 
 
 def streams(sent, got, ties=()):
@@ -373,41 +364,21 @@
     )
 
 
-def arrange(value, hops, chips, tok, tie):
-    rows, features = value.shape
-    count = 4 if hops else 1
-    sources = (value,) + tuple(x for step in hops for x in step)
-
-    def body(*refs):
-        x_refs, out_refs = refs[: len(sources)], refs[len(sources) :]
+def arrange(value, chips, tok, tie):
+    count, rows, features = value.shape
+
+    def body(x_ref, *out_refs):
         me = lax.axis_index("expert")
-
-        def place(x_ref, mask):
+        group = lax.axis_index("dp") if count > 1 else 0
+        for mask in range(count):
             for k in range(chips):
                 for twin in range(2):
                     out_refs[k][pl.ds((twin * count + mask) * tok, tok), :] = x_ref[
-                        block(me ^ (2 * k + twin), tok), :
+                        group ^ mask, block(me ^ (2 * k + twin), tok), :
                     ]
 
-        place(x_refs[0], 0)
-        if hops:
-            near, middle, middle_far, edge, edge_far = x_refs[1:]
-            group = lax.axis_index("dp")
-            at_edge = jnp.logical_or(group == 0, group == 3)
-            place(near, 1)
-
-            @pl.when(at_edge)
-            def _():
-                place(edge, 2)
-                place(edge_far, 3)
-
-            @pl.when(jnp.logical_not(at_edge))
-            def _():
-                place(middle_far, 2)
-                place(middle, 3)
-
     out = tuple(shape(2 * count * tok, features) for _ in range(chips))
-    return local(body, out, sources, "arrange", ties=(tie,))
+    return local(body, out, (value,), "arrange", ties=(tie,))
 
 
 def proj_round(x_rows, near, far, chip, tok, before, last):
@@ -470,17 +441,21 @@
     bits = [1 << b for b in range(1, owners.bit_length() - 1)]
     gather_groups = groups == 4 and groups * owners * tok * width <= 1 << 22
 
-    part_other, *sent = project(tokens_x, in_proj, out_grad, expert_ids, route_probs, all_experts)
+    part_other, *sent, x_own = project(
+        tokens_x, in_proj, out_grad, expert_ids, route_probs, all_experts
+    )
     sums = (half // 2 + all_experts, half // 2)
-    hops = line_gather(tokens_x, "dp") if gather_groups else []
-    last = hops_last(hops)
+    x_groups, x_spread = x_own[None], ()
+    if gather_groups:
+        x_spread = spread(x_own, groups)
+        x_groups = lax.all_to_all(x_spread, "dp", split_axis=0, concat_axis=0, tiled=True)
     up, down = load(up_weight, down_weight)
-    sent = streams(sent, xor_permute(part_other, "expert", 1))
+    sent = streams(sent, xor_permute(part_other, "expert", 1), (x_spread,) if gather_groups else ())
     for step, stream_bits in enumerate(zip(bits, bits[::-1])):
         got = [xor_permute(value, "expert", bit) for value, bit in zip(sent, stream_bits)]
         if step + 1 < len(bits):
             sent = merge(sent, got, sums)
-    mine = settle(sent, got, (order_of(bits), order_of(bits[::-1])), tok, all_experts, ties=(up, down, *hop(hops, 0)))
+    mine = settle(sent, got, (order_of(bits), order_of(bits[::-1])), tok, all_experts, ties=(up, down))
     other = xor_permute(mine, "expert", 1)
 
     positive = preacts(mine, up, half)
@@ -489,24 +464,24 @@
     out_pieces = pieces_of(out_mine, xor_permute(out_other, "expert", 1), chips)
     lat_pieces = pieces_of(lat_mine, xor_permute(lat_other, "expert", 1), chips)
     got = scatter(lat_pieces)
-    latent_grad = add_pieces((lat_pieces[0], *got), ties=hop(hops, 1))
+    latent_grad = add_pieces((lat_pieces[0], *got))
 
     own = ()
     if gather_groups:
         across = [xor_permute(latent_grad, "dp", m) for m in range(1, groups)]
-        own = stack(across, tok, ties=last)
-        hops.append((jnp.concatenate(last, axis=0),))
+        own = stack(across, tok, ties=(x_groups,))
     after = (own,) if gather_groups else ()
     sent = head(latent_grad, out_pieces[1:])
     got = scatter([None, *sent])
     combined = add_pieces((out_pieces[0], *got), tok, ties=after)
     near = stack([latent_grad, *got], tok, ties=after)
-    split = near.shape[0] // 2
-    twins = [xor_permute(v, "expert", 1) for v in (near[:split], near[split:])]
+    parts = 2
+    split = near.shape[0] // parts
+    twins = [xor_permute(near[i * split : (i + 1) * split], "expert", 1) for i in range(parts)]
     twins = jnp.concatenate(twins, axis=0)
     input_grad = input_grads(near, twins, in_proj, tok)
     far = [() for _ in range(chips)]
-    x_all = arrange(tokens_x, hops, chips, tok, latent_grad)
+    x_all = arrange(x_groups, chips, tok, latent_grad)
     order = [0] + list(range(chips - 1, 0, -1))
     if gather_groups:
         far[0] = (own, xor_permute(own, "expert", 1))

time: 67.1 us -> 62.2 us (0.927)
  starting transfers between devices: 32.5 us -> 29 us
  waiting for transfers between devices: 18 us -> 15.7 us
  Pallas kernels: 14.9 us -> 15.9 us
    ppermute x5 -> x0, starting transfers between devices: 5.21 us -> none  [the longest x2 2.57 us: hops_last(): lax.ppermute(value[i * rows:(i + 1) * rows], 'dp', OUTER)]
    all_to_all x0 -> x1, starting transfers between devices: none -> 4.87 us  [per_device(): lax.all_to_all(x_spread, 'dp', split_axis=0, concat_axis=0, tiled=True)]
    ppermute x27 -> x26, starting transfers between devices: 27.2 us -> 24.1 us  [xor_permute(): return lax.ppermute(value, axis, [(i, i ^ mask) for i in range(size)])]
    ppermute x5 -> x0, waiting for transfers between devices: 2.12 us -> none  [the longest x1 2.11 us: line_gather(): edge = lax.ppermute(middle, axis, OUTER)]
    pallas_call x20 -> x21, Pallas kernels: 11.9 us -> 12.9 us  [local(): pl.pallas_call(kernel, out_shape=outs, in_specs=[spec] * len(args) + [ANY...]
    ppermute x27 -> x26, waiting for transfers between devices: 15.9 us -> 15.7 us  [xor_permute(): return lax.ppermute(value, axis, [(i, i ^ mask) for i in range(size)])]
  transfers between devices with their start and end apart: 32 -> 27, of which waited for: 11 -> 11; matrix products, arithmetic and copies ran while one was open for 0% -> 0% of each run, Pallas kernels for 17% -> 20%
where the time goes in v5:
time: 62.2 us; the launch traced here: 61.9 us
  starting transfers between devices  29 us (47%)
  Pallas kernels  15.9 us (26%)
  waiting for transfers between devices  15.7 us (25%)
  between operations  0.85 us (1%)
    ppermute x26, starting transfers between devices, xor_permute(): return lax.ppermute(value, axis, [(i, i ^ mask) for i in range(size)])  24.1 us
    ppermute x26, waiting for transfers between devices, xor_permute(): return lax.ppermute(value, axis, [(i, i ^ mask) for i in range(size)])  15.7 us
    pallas_call x21, Pallas kernels, local(): pl.pallas_call(kernel, out_shape=outs, in_specs=[spec] * len(args) + [ANY...  12.9 us
    all_to_all x1, starting transfers between devices, per_device(): lax.all_to_all(x_spread, 'dp', split_axis=0, concat_axis=0, tiled=True)  4.87 us
    pallas_call x4, Pallas kernels, proj_round(): pl.pallas_call(body, out_shape=shape(features, width, F32), in_specs=[VME...  3 us
  transfers between devices with their start and end apart: 27, of which 11 were waited for; matrix products, arithmetic and copies ran while one was open for 0% of the time, Pallas kernels for 20%

profile of v5, /device:TPU:0, one launch (start us, length us, event | category | flops | bytes accessed | tf_op | source)
XLA Modules:
  0.0 61.9 jit_solution(1559781262558008132)
XLA Ops:
  0.6 2.0 %project.1 = (bf16[128,1024]{1,0:T(8,128)(2,1)S(1)}, bf16[96,1024]{1,0:T(8,128)(2,1)S(1)}, bf16[80,1024]{1,0:T(8,128)(2,1)S(1)}, bf16[256,512]{1,0:T(8,128)(2,1)S(1)}) custom-call(bf16[256,512]{1,0:T(8,128)(2,1)} %refs_0_.2, bf16[512,1024]{1,0:T(8,128)(2,1)} %refs_2_.3, bf16[32,1024]{1,0:T(8,128)(2,1)} %refs_2_.2, s32[8,32]{1,0:T(8,128)} %bitcast.2, ...), custom_call_target="tpu_custom_call" | custom-call | flops 268435456 | bytes 1048576 | tf_op jit(solution)/shard_map/project/pallas_call | solution.py:39
  2.6 0.5 collective-permute-start
  3.1 1.0 %spread.1.refs_3_ = bf16[4,256,512]{2,1,0:T(8,128)(2,1)} custom-call(bf16[256,512]{1,0:T(8,128)(2,1)S(1)} %get-tuple-element.36.refs_0_), custom_call_target="tpu_custom_call" | custom-call | bytes 1048576 | tf_op jit(solution)/shard_map/spread/pallas_call | solution.py:39
  4.2 0.1 collective-permute-done.refs_2_
  4.3 0.1 streams.1
  4.3 2.9 %collective-permute-start.1 = (bf16[96,1024]{1,0:T(8,128)(2,1)S(1)}, bf16[96,1024]{1,0:T(8,128)(2,1)S(1)}, u32[]{:S(2)}, u32[]{:S(2)}) collective-permute-start(bf16[96,1024]{1,0:T(8,128)(2,1)S(1)} %get-tuple-element.37.refs_0_), channel_id=1, source_target_pairs={{0,2},{1,3},{2,0},{3,1},{4,6},{5,7},{6,4},{7,5},{8,10},{9,11},{10,... | collective-permute-start | bytes 589832 | tf_op jit(solution)/shard_map/ppermute | solution.py:77
  7.3 1.5 %collective-permute-start.2 = (bf16[80,1024]{1,0:T(8,128)(2,1)S(1)}, bf16[80,1024]{1,0:T(8,128)(2,1)S(1)}, u32[]{:S(2)}, u32[]{:S(2)}) collective-permute-start(bf16[80,1024]{1,0:T(8,128)(2,1)S(1)} %get-tuple-element.38.refs_1_), channel_id=1, source_target_pairs={{0,4},{1,5},{2,6},{3,7},{4,0},{5,1},{6,2},{7,3},{8,12},{9,13},{10,... | collective-permute-start | bytes 491528 | tf_op jit(solution)/shard_map/ppermute | solution.py:77
  8.8 4.9 %all-to-all-start = ((bf16[4,256,512]{2,1,0:T(8,128)(2,1)}), bf16[4,256,512]{2,1,0:T(8,128)(2,1)S(1)}, u32[]{:S(2)}, u32[]{:S(2)}) async-start(bf16[4,256,512]{2,1,0:T(8,128)(2,1)} %spread.1.refs_3_), calls=%async_computation | async-start | bytes 2097152 | tf_op jit(solution)/shard_map/all_to_all | solution.py:451
  13.7 0.0 collective-permute-done.2.refs_3_
  13.7 0.0 collective-permute-done.1.refs_2_
  13.7 0.1 merge.1
  13.7 1.1 %collective-permute-start.3 = (bf16[112,1024]{1,0:T(8,128)(2,1)S(1)}, bf16[112,1024]{1,0:T(8,128)(2,1)S(1)}, u32[]{:S(2)}, u32[]{:S(2)}) collective-permute-start(bf16[112,1024]{1,0:T(8,128)(2,1)S(1)} %get-tuple-element.39.refs_0_), channel_id=1, source_target_pairs={{0,4},{1,5},{2,6},{3,7},{4,0},{5,1},{6,2},{7,3},{8,12},{9,13},{10,... | collective-permute-start | bytes 688136 | tf_op jit(solution)/shard_map/ppermute | solution.py:77
  14.9 1.0 %collective-permute-start.4 = (bf16[96,1024]{1,0:T(8,128)(2,1)S(1)}, bf16[96,1024]{1,0:T(8,128)(2,1)S(1)}, u32[]{:S(2)}, u32[]{:S(2)}) collective-permute-start(bf16[96,1024]{1,0:T(8,128)(2,1)S(1)} %get-tuple-element.40.refs_1_), channel_id=1, source_target_pairs={{0,2},{1,3},{2,0},{3,1},{4,6},{5,7},{6,4},{7,5},{8,10},{9,11},{10,... | collective-permute-start | bytes 589832 | tf_op jit(solution)/shard_map/ppermute | solution.py:77
  15.9 2.9 %load.1 = (bf16[2,1024,768]{2,1,0:T(8,128)(2,1)S(1)}, bf16[2,768,1024]{2,1,0:T(8,128)(2,1)S(1)}) custom-call(bf16[2,1024,768]{2,1,0:T(8,128)(2,1)} %refs_0_.3, bf16[2,768,1024]{2,1,0:T(8,128)(2,1)} %refs_1_.3), custom_call_target="tpu_custom_call" | custom-call | bytes 1048576 | tf_op jit(solution)/shard_map/load/pallas_call | solution.py:39
  18.7 1.8 %collective-permute-done.4.refs_3_ = bf16[96,1024]{1,0:T(8,128)(2,1)S(1)} collective-permute-done((bf16[96,1024]{1,0:T(8,128)(2,1)S(1)}, bf16[96,1024]{1,0:T(8,128)(2,1)S(1)}, u32[]{:S(2)}, u32[]{:S(2)}) %collective-permute-start.4) | collective-permute-done | bytes 196640 | tf_op jit(solution)/shard_map/ppermute | solution.py:77
  20.6 0.1 collective-permute-done.3.refs_2_
  20.6 0.1 settle.1.refs_0_.refs_1_
  20.7 0.1 collective-permute-start.5
  20.8 0.6 preacts.1.refs_0_
  21.4 1.4 %collective-permute-done.5.refs_2_ = bf16[272,1024]{1,0:T(8,128)(2,1)S(1)} collective-permute-done((bf16[272,1024]{1,0:T(8,128)(2,1)S(1)}, bf16[272,1024]{1,0:T(8,128)(2,1)S(1)}, u32[]{:S(2)}, u32[]{:S(2)}) %collective-permute-start.5) | collective-permute-done | bytes 557088 | tf_op jit(solution)/shard_map/ppermute | solution.py:77
  22.7 3.1 %experts.1 = (bf16[256,1536]{1,0:T(8,128)(2,1)S(1)}, bf16[128,1024]{1,0:T(8,128)(2,1)S(1)}, bf16[128,1024]{1,0:T(8,128)(2,1)S(1)}) custom-call(f32[128,1536]{1,0:T(8,128)S(1)} %preacts.1.refs_0_, bf16[272,1024]{1,0:T(8,128)(2,1)S(1)} %settle.1.refs_0_.refs_1_, bf16[272,1024]{1,0:T(8,128)(2,1)S(1)} %collective-permute-done.5.refs_2_, ...), custom_call_target="tpu_custom_call" | custom-call | flops 2013265920 | bytes 1048576 | tf_op jit(solution)/shard_map/experts/pallas_call | solution.py:39
  25.8 0.2 collective-permute-start.7
  26.0 1.0 %outputs.1 = (bf16[128,1024]{1,0:T(8,128)(2,1)S(1)}, bf16[128,1024]{1,0:T(8,128)(2,1)S(1)}) custom-call(bf16[256,1536]{1,0:T(8,128)(2,1)S(1)} %get-tuple-element.43.refs_0_, bf16[2,768,1024]{2,1,0:T(8,128)(2,1)S(1)} %get-tuple-element.42.refs_5_.refs_4_.refs_1_), custom_call_target="tpu_custom_call" | custom-call | flops 805306368 | bytes 1048576 | tf_op jit(solution)/shard_map/outputs/pallas_call | solution.py:39
  27.0 0.4 collective-permute-start.6
  27.4 0.0 collective-permute-done.7.refs_1_
  27.4 0.1 pieces.3
  27.5 1.2 %collective-permute-start.8 = (bf16[32,1024]{1,0:T(8,128)(2,1)S(1)}, bf16[32,1024]{1,0:T(8,128)(2,1)S(1)}, u32[]{:S(2)}, u32[]{:S(2)}) collective-permute-start(bf16[32,1024]{1,0:T(8,128)(2,1)S(1)} %get-tuple-element.50), channel_id=1, source_target_pairs={{0,2},{1,3},{2,0},{3,1},{4,6},{5,7},{6,4},{7,5},{8,10},{9,11},{10,... | collective-permute-start | bytes 196616 | tf_op jit(solution)/shard_map/ppermute | solution.py:77
  28.7 1.0 %collective-permute-start.9 = (bf16[32,1024]{1,0:T(8,128)(2,1)S(1)}, bf16[32,1024]{1,0:T(8,128)(2,1)S(1)}, u32[]{:S(2)}, u32[]{:S(2)}) collective-permute-start(bf16[32,1024]{1,0:T(8,128)(2,1)S(1)} %get-tuple-element.51), channel_id=1, source_target_pairs={{0,4},{1,5},{2,6},{3,7},{4,0},{5,1},{6,2},{7,3},{8,12},{9,13},{10,... | collective-permute-start | bytes 196616 | tf_op jit(solution)/shard_map/ppermute | solution.py:77
  29.6 1.4 %collective-permute-start.10 = (bf16[32,1024]{1,0:T(8,128)(2,1)S(1)}, bf16[32,1024]{1,0:T(8,128)(2,1)S(1)}, u32[]{:S(2)}, u32[]{:S(2)}) collective-permute-start(bf16[32,1024]{1,0:T(8,128)(2,1)S(1)} %get-tuple-element.52), channel_id=1, source_target_pairs={{0,6},{1,7},{2,4},{3,5},{4,2},{5,3},{6,0},{7,1},{8,14},{9,15},{10,... | collective-permute-start | bytes 196616 | tf_op jit(solution)/shard_map/ppermute | solution.py:77
  31.1 0.1 pieces.2
  31.1 0.7 %collective-permute-done.8.refs_1_ = bf16[32,1024]{1,0:T(8,128)(2,1)S(1)} collective-permute-done((bf16[32,1024]{1,0:T(8,128)(2,1)S(1)}, bf16[32,1024]{1,0:T(8,128)(2,1)S(1)}, u32[]{:S(2)}, u32[]{:S(2)}) %collective-permute-start.8) | collective-permute-done | bytes 65568 | tf_op jit(solution)/shard_map/ppermute | solution.py:77
  31.8 1.8 %collective-permute-done.9.refs_2_ = bf16[32,1024]{1,0:T(8,128)(2,1)S(1)} collective-permute-done((bf16[32,1024]{1,0:T(8,128)(2,1)S(1)}, bf16[32,1024]{1,0:T(8,128)(2,1)S(1)}, u32[]{:S(2)}, u32[]{:S(2)}) %collective-permute-start.9) | collective-permute-done | bytes 65568 | tf_op jit(solution)/shard_map/ppermute | solution.py:77
  33.6 1.2 %collective-permute-done.10.refs_3_ = bf16[32,1024]{1,0:T(8,128)(2,1)S(1)} collective-permute-done((bf16[32,1024]{1,0:T(8,128)(2,1)S(1)}, bf16[32,1024]{1,0:T(8,128)(2,1)S(1)}, u32[]{:S(2)}, u32[]{:S(2)}) %collective-permute-start.10) | collective-permute-done | bytes 65568 | tf_op jit(solution)/shard_map/ppermute | solution.py:77
  34.8 3.7 %collective-permute-start.16 = (bf16[32,1024]{1,0:T(8,128)(2,1)S(1)}, bf16[32,1024]{1,0:T(8,128)(2,1)S(1)}, u32[]{:S(2)}, u32[]{:S(2)}) collective-permute-start(bf16[32,1024]{1,0:T(8,128)(2,1)S(1)} %add_pieces.2.refs_0_.refs_1_), channel_id=1, source_target_pairs={{0,24},{8,16},{16,8},{24,0},{1,25},{9,17},{17,9},{25,1},{2,26},{10... | collective-permute-start | bytes 196616 | tf_op jit(solution)/shard_map/ppermute | solution.py:77
  38.5 0.0 copy-start
  38.6 1.1 %collective-permute-start.11 = (bf16[64,1024]{1,0:T(8,128)(2,1)S(1)}, bf16[64,1024]{1,0:T(8,128)(2,1)S(1)}, u32[]{:S(2)}, u32[]{:S(2)}) collective-permute-start(bf16[64,1024]{1,0:T(8,128)(2,1)S(1)} %get-tuple-element.56), channel_id=1, source_target_pairs={{0,2},{1,3},{2,0},{3,1},{4,6},{5,7},{6,4},{7,5},{8,10},{9,11},{10,... | collective-permute-start | bytes 393224 | tf_op jit(solution)/shard_map/ppermute | solution.py:77
  39.7 0.9 %collective-permute-start.12 = (bf16[64,1024]{1,0:T(8,128)(2,1)S(1)}, bf16[64,1024]{1,0:T(8,128)(2,1)S(1)}, u32[]{:S(2)}, u32[]{:S(2)}) collective-permute-start(bf16[64,1024]{1,0:T(8,128)(2,1)S(1)} %get-tuple-element.57), channel_id=1, source_target_pairs={{0,4},{1,5},{2,6},{3,7},{4,0},{5,1},{6,2},{7,3},{8,12},{9,13},{10,... | collective-permute-start | bytes 393224 | tf_op jit(solution)/shard_map/ppermute | solution.py:77
  40.6 1.6 %collective-permute-start.13 = (bf16[64,1024]{1,0:T(8,128)(2,1)S(1)}, bf16[64,1024]{1,0:T(8,128)(2,1)S(1)}, u32[]{:S(2)}, u32[]{:S(2)}) collective-permute-start(bf16[64,1024]{1,0:T(8,128)(2,1)S(1)} %get-tuple-element.58), channel_id=1, source_target_pairs={{0,6},{1,7},{2,4},{3,5},{4,2},{5,3},{6,0},{7,1},{8,14},{9,15},{10,... | collective-permute-start | bytes 393224 | tf_op jit(solution)/shard_map/ppermute | solution.py:77
  42.1 0.0 collective-permute-start.15
  42.1 0.0 collective-permute-done.16.refs_2_
  42.1 0.8 %collective-permute-start.14 = (bf16[32,1024]{1,0:T(8,128)(2,1)S(1)}, bf16[32,1024]{1,0:T(8,128)(2,1)S(1)}, u32[]{:S(2)}, u32[]{:S(2)}) collective-permute-start(bf16[32,1024]{1,0:T(8,128)(2,1)S(1)} %add_pieces.2.refs_0_.refs_1_), channel_id=1, source_target_pairs={{0,8},{8,0},{16,24},{24,16},{1,9},{9,1},{17,25},{25,17},{2,10},{10... | collective-permute-start | bytes 196616 | tf_op jit(solution)/shard_map/ppermute | solution.py:77
  42.9 0.0 all-to-all-done.refs_3_.refs_0_
  42.9 4.4 %collective-permute-done.15.refs_1_ = bf16[32,1024]{1,0:T(8,128)(2,1)S(1)} collective-permute-done((bf16[32,1024]{1,0:T(8,128)(2,1)S(1)}, bf16[32,1024]{1,0:T(8,128)(2,1)S(1)}, u32[]{:S(2)}, u32[]{:S(2)}) %collective-permute-start.15) | collective-permute-done | bytes 65568 | tf_op jit(solution)/shard_map/ppermute | solution.py:77
  47.3 0.0 collective-permute-done.14.refs_0_
  47.3 1.4 %collective-permute-start.24 = (bf16[96,1024]{1,0:T(8,128)(2,1)S(1)}, bf16[96,1024]{1,0:T(8,128)(2,1)S(1)}, u32[]{:S(2)}, u32[]{:S(2)}) collective-permute-start(bf16[96,1024]{1,0:T(8,128)(2,1)S(1)} %stack.5.refs_4_.refs_3_), channel_id=1, source_target_pairs={{0,6},{1,7},{2,4},{3,5},{4,2},{5,3},{6,0},{7,1},{8,14},{9,15},{10,... | collective-permute-start | bytes 589832 | tf_op jit(solution)/shard_map/ppermute | solution.py:77
  48.7 1.2 %collective-permute-start.22 = (bf16[96,1024]{1,0:T(8,128)(2,1)S(1)}, bf16[96,1024]{1,0:T(8,128)(2,1)S(1)}, u32[]{:S(2)}, u32[]{:S(2)}) collective-permute-start(bf16[96,1024]{1,0:T(8,128)(2,1)S(1)} %stack.5.refs_4_.refs_3_), channel_id=1, source_target_pairs={{0,4},{1,5},{2,6},{3,7},{4,0},{5,1},{6,2},{7,3},{8,12},{9,13},{10,... | collective-permute-start | bytes 589832 | tf_op jit(solution)/shard_map/ppermute | solution.py:77
  49.9 0.0 collective-permute-done.11.refs_1_
  49.9 1.0 %collective-permute-start.19 = (bf16[96,1024]{1,0:T(8,128)(2,1)S(1)}, bf16[96,1024]{1,0:T(8,128)(2,1)S(1)}, u32[]{:S(2)}, u32[]{:S(2)}) collective-permute-start(bf16[96,1024]{1,0:T(8,128)(2,1)S(1)} %stack.5.refs_4_.refs_3_), channel_id=1, source_target_pairs={{0,2},{1,3},{2,0},{3,1},{4,6},{5,7},{6,4},{7,5},{8,10},{9,11},{10,... | collective-permute-start | bytes 589832 | tf_op jit(solution)/shard_map/ppermute | solution.py:77
  50.9 0.1 collective-permute-start.17
  51.0 0.5 collective-permute-start.18
  51.5 0.1 arrange.1
  51.6 0.7 %add_pieces.3.refs_3_ = bf16[32,1024]{1,0:T(8,128)(2,1)} custom-call(bf16[32,1024]{1,0:T(8,128)(2,1)S(1)} %get-tuple-element.46.refs_0_, bf16[64,1024]{1,0:T(8,128)(2,1)S(1)} %collective-permute-done.11.refs_1_, bf16[64,1024]{1,0:T(8,128)(2,1)S(1)} %collective-permute-done.12.refs_2_, bf16[64,1024]{1,0:T(8,128)(2,1)S(1)} %collective-permute-done.13.refs_3_, ...), custom_call_target="tpu_custom_call" | custom-call | bytes 1048576 | tf_op jit(solution)/shard_map/add_pieces/pallas_call | solution.py:39
  52.2 1.8 %collective-permute-done.24.refs_0_ = bf16[96,1024]{1,0:T(8,128)(2,1)S(1)} collective-permute-done((bf16[96,1024]{1,0:T(8,128)(2,1)S(1)}, bf16[96,1024]{1,0:T(8,128)(2,1)S(1)}, u32[]{:S(2)}, u32[]{:S(2)}) %collective-permute-start.24) | collective-permute-done | bytes 196640 | tf_op jit(solution)/shard_map/ppermute | solution.py:77
  54.1 0.0 copy-start.2
  54.1 2.0 %collective-permute-done.22.refs_0_ = bf16[96,1024]{1,0:T(8,128)(2,1)S(1)} collective-permute-done((bf16[96,1024]{1,0:T(8,128)(2,1)S(1)}, bf16[96,1024]{1,0:T(8,128)(2,1)S(1)}, u32[]{:S(2)}, u32[]{:S(2)}) %collective-permute-start.22) | collective-permute-done | bytes 196640 | tf_op jit(solution)/shard_map/ppermute | solution.py:77
  56.1 0.6 collective-permute-start.23
  56.7 1.2 %input_grads.1.refs_2_ = bf16[256,512]{1,0:T(8,128)(2,1)} custom-call(bf16[128,1024]{1,0:T(8,128)(2,1)S(1)} %stack.6.refs_0_.refs_1_, bf16[128,1024]{1,0:T(8,128)(2,1)S(1)} %constant_dynamic-update-slice_fusion.refs_1_.refs_2_, bf16[512,1024]{1,0:T(8,128)(2,1)S(1)} %copy-done), custom_call_target="tpu_custom_call" | custom-call | flops 268435456 | bytes 1048576 | tf_op jit(solution)/shard_map/input_grads/pallas_call | solution.py:39
  57.9 0.5 proj_round.4.refs_1_.refs_5_
  58.4 0.5 copy-done.1
  58.8 0.1 collective-permute-start.21
  58.9 0.5 proj_round.5.refs_5_
  59.4 0.5 proj_round.6.refs_5_
  59.9 0.5 collective-permute-done.21.refs_4_
  60.3 1.6 %proj_round.7 = f32[512,1024]{1,0:T(8,128)} custom-call(bf16[256,512]{1,0:T(8,128)(2,1)S(1)} %get-tuple-element.59.refs_0_, bf16[128,1024]{1,0:T(8,128)(2,1)S(1)} %stack.6.refs_0_.refs_1_, bf16[128,1024]{1,0:T(8,128)(2,1)S(1)} %constant_dynamic-update-slice_fusion.refs_1_.refs_2_, bf16[96,1024]{1,0:T(8,128)(2,1)S(1)} %stack.7.refs_3_, ...), custom_call_target="tpu_custom_call" | custom-call | flops 268435456 | bytes 4194304 | tf_op jit(solution)/shard_map/proj_round/pallas_call | solution.py:418
  (24 shorter events, 0.2 us)
Async XLA Ops:
  2.6 1.7 %collective-permute-start = (bf16[128,1024]{1,0:T(8,128)(2,1)S(1)}, bf16[128,1024]{1,0:T(8,128)(2,1)S(1)}, u32[]{:S(2)}, u32[]{:S(2)}) collective-permute-start(bf16[128,1024]{1,0:T(8,128)(2,1)S(1)} %get-tuple-element.35), channel_id=1, source_target_pairs={{0,1},{1,0},{2,3},{3,2},{4,5},{5,4},{6,7},{7,6},{8,9},{9,8},{10,11... | collective-permute-start | bytes 786440 | tf_op jit(solution)/shard_map/ppermute | solution.py:77
  4.3 9.3 %collective-permute-start.1 = (bf16[96,1024]{1,0:T(8,128)(2,1)S(1)}, bf16[96,1024]{1,0:T(8,128)(2,1)S(1)}, u32[]{:S(2)}, u32[]{:S(2)}) collective-permute-start(bf16[96,1024]{1,0:T(8,128)(2,1)S(1)} %get-tuple-element.37.refs_0_), channel_id=1, source_target_pairs={{0,2},{1,3},{2,0},{3,1},{4,6},{5,7},{6,4},{7,5},{8,10},{9,11},{10,... | collective-permute-start | bytes 589832 | tf_op jit(solution)/shard_map/ppermute | solution.py:77
  7.3 6.4 %collective-permute-start.2 = (bf16[80,1024]{1,0:T(8,128)(2,1)S(1)}, bf16[80,1024]{1,0:T(8,128)(2,1)S(1)}, u32[]{:S(2)}, u32[]{:S(2)}) collective-permute-start(bf16[80,1024]{1,0:T(8,128)(2,1)S(1)} %get-tuple-element.38.refs_1_), channel_id=1, source_target_pairs={{0,4},{1,5},{2,6},{3,7},{4,0},{5,1},{6,2},{7,3},{8,12},{9,13},{10,... | collective-permute-start | bytes 491528 | tf_op jit(solution)/shard_map/ppermute | solution.py:77
  8.8 34.1 %all-to-all-start = ((bf16[4,256,512]{2,1,0:T(8,128)(2,1)}), bf16[4,256,512]{2,1,0:T(8,128)(2,1)S(1)}, u32[]{:S(2)}, u32[]{:S(2)}) async-start(bf16[4,256,512]{2,1,0:T(8,128)(2,1)} %spread.1.refs_3_), calls=%async_computation | async-start | bytes 2097152 | tf_op jit(solution)/shard_map/all_to_all | solution.py:451
  13.7 6.9 %collective-permute-start.3 = (bf16[112,1024]{1,0:T(8,128)(2,1)S(1)}, bf16[112,1024]{1,0:T(8,128)(2,1)S(1)}, u32[]{:S(2)}, u32[]{:S(2)}) collective-permute-start(bf16[112,1024]{1,0:T(8,128)(2,1)S(1)} %get-tuple-element.39.refs_0_), channel_id=1, source_target_pairs={{0,4},{1,5},{2,6},{3,7},{4,0},{5,1},{6,2},{7,3},{8,12},{9,13},{10,... | collective-permute-start | bytes 688136 | tf_op jit(solution)/shard_map/ppermute | solution.py:77
  14.9 5.7 %collective-permute-start.4 = (bf16[96,1024]{1,0:T(8,128)(2,1)S(1)}, bf16[96,1024]{1,0:T(8,128)(2,1)S(1)}, u32[]{:S(2)}, u32[]{:S(2)}) collective-permute-start(bf16[96,1024]{1,0:T(8,128)(2,1)S(1)} %get-tuple-element.40.refs_1_), channel_id=1, source_target_pairs={{0,2},{1,3},{2,0},{3,1},{4,6},{5,7},{6,4},{7,5},{8,10},{9,11},{10,... | collective-permute-start | bytes 589832 | tf_op jit(solution)/shard_map/ppermute | solution.py:77
  20.7 2.0 %collective-permute-start.5 = (bf16[272,1024]{1,0:T(8,128)(2,1)S(1)}, bf16[272,1024]{1,0:T(8,128)(2,1)S(1)}, u32[]{:S(2)}, u32[]{:S(2)}) collective-permute-start(bf16[272,1024]{1,0:T(8,128)(2,1)S(1)} %settle.1.refs_0_.refs_1_), channel_id=1, source_target_pairs={{0,1},{1,0},{2,3},{3,2},{4,5},{5,4},{6,7},{7,6},{8,9},{9,8},{10,11... | collective-permute-start | bytes 1671176 | tf_op jit(solution)/shard_map/ppermute | solution.py:77
  25.8 1.6 %collective-permute-start.7 = (bf16[128,1024]{1,0:T(8,128)(2,1)S(1)}, bf16[128,1024]{1,0:T(8,128)(2,1)S(1)}, u32[]{:S(2)}, u32[]{:S(2)}) collective-permute-start(bf16[128,1024]{1,0:T(8,128)(2,1)S(1)} %get-tuple-element.48), channel_id=1, source_target_pairs={{0,1},{1,0},{2,3},{3,2},{4,5},{5,4},{6,7},{7,6},{8,9},{9,8},{10,11... | collective-permute-start | bytes 786440 | tf_op jit(solution)/shard_map/ppermute | solution.py:77
  27.0 4.1 %collective-permute-start.6 = (bf16[128,1024]{1,0:T(8,128)(2,1)S(1)}, bf16[128,1024]{1,0:T(8,128)(2,1)S(1)}, u32[]{:S(2)}, u32[]{:S(2)}) collective-permute-start(bf16[128,1024]{1,0:T(8,128)(2,1)S(1)} %get-tuple-element.45), channel_id=1, source_target_pairs={{0,1},{1,0},{2,3},{3,2},{4,5},{5,4},{6,7},{7,6},{8,9},{9,8},{10,11... | collective-permute-start | bytes 786440 | tf_op jit(solution)/shard_map/ppermute | solution.py:77
  27.5 4.3 %collective-permute-start.8 = (bf16[32,1024]{1,0:T(8,128)(2,1)S(1)}, bf16[32,1024]{1,0:T(8,128)(2,1)S(1)}, u32[]{:S(2)}, u32[]{:S(2)}) collective-permute-start(bf16[32,1024]{1,0:T(8,128)(2,1)S(1)} %get-tuple-element.50), channel_id=1, source_target_pairs={{0,2},{1,3},{2,0},{3,1},{4,6},{5,7},{6,4},{7,5},{8,10},{9,11},{10,... | collective-permute-start | bytes 196616 | tf_op jit(solution)/shard_map/ppermute | solution.py:77
  28.7 5.0 %collective-permute-start.9 = (bf16[32,1024]{1,0:T(8,128)(2,1)S(1)}, bf16[32,1024]{1,0:T(8,128)(2,1)S(1)}, u32[]{:S(2)}, u32[]{:S(2)}) collective-permute-start(bf16[32,1024]{1,0:T(8,128)(2,1)S(1)} %get-tuple-element.51), channel_id=1, source_target_pairs={{0,4},{1,5},{2,6},{3,7},{4,0},{5,1},{6,2},{7,3},{8,12},{9,13},{10,... | collective-permute-start | bytes 196616 | tf_op jit(solution)/shard_map/ppermute | solution.py:77
  29.6 5.2 %collective-permute-start.10 = (bf16[32,1024]{1,0:T(8,128)(2,1)S(1)}, bf16[32,1024]{1,0:T(8,128)(2,1)S(1)}, u32[]{:S(2)}, u32[]{:S(2)}) collective-permute-start(bf16[32,1024]{1,0:T(8,128)(2,1)S(1)} %get-tuple-element.52), channel_id=1, source_target_pairs={{0,6},{1,7},{2,4},{3,5},{4,2},{5,3},{6,0},{7,1},{8,14},{9,15},{10,... | collective-permute-start | bytes 196616 | tf_op jit(solution)/shard_map/ppermute | solution.py:77
  34.8 7.3 %collective-permute-start.16 = (bf16[32,1024]{1,0:T(8,128)(2,1)S(1)}, bf16[32,1024]{1,0:T(8,128)(2,1)S(1)}, u32[]{:S(2)}, u32[]{:S(2)}) collective-permute-start(bf16[32,1024]{1,0:T(8,128)(2,1)S(1)} %add_pieces.2.refs_0_.refs_1_), channel_id=1, source_target_pairs={{0,24},{8,16},{16,8},{24,0},{1,25},{9,17},{17,9},{25,1},{2,26},{10... | collective-permute-start | bytes 196616 | tf_op jit(solution)/shard_map/ppermute | solution.py:77
  38.5 18.1 %copy-start = (bf16[512,1024]{1,0:T(8,128)(2,1)S(1)}, bf16[512,1024]{1,0:T(8,128)(2,1)}, u32[]{:S(2)}) copy-start(bf16[512,1024]{1,0:T(8,128)(2,1)} %refs_2_.3) | copy-start | bytes 3145732
  38.6 11.3 %collective-permute-start.11 = (bf16[64,1024]{1,0:T(8,128)(2,1)S(1)}, bf16[64,1024]{1,0:T(8,128)(2,1)S(1)}, u32[]{:S(2)}, u32[]{:S(2)}) collective-permute-start(bf16[64,1024]{1,0:T(8,128)(2,1)S(1)} %get-tuple-element.56), channel_id=1, source_target_pairs={{0,2},{1,3},{2,0},{3,1},{4,6},{5,7},{6,4},{7,5},{8,10},{9,11},{10,... | collective-permute-start | bytes 393224 | tf_op jit(solution)/shard_map/ppermute | solution.py:77
  39.7 11.2 %collective-permute-start.12 = (bf16[64,1024]{1,0:T(8,128)(2,1)S(1)}, bf16[64,1024]{1,0:T(8,128)(2,1)S(1)}, u32[]{:S(2)}, u32[]{:S(2)}) collective-permute-start(bf16[64,1024]{1,0:T(8,128)(2,1)S(1)} %get-tuple-element.57), channel_id=1, source_target_pairs={{0,4},{1,5},{2,6},{3,7},{4,0},{5,1},{6,2},{7,3},{8,12},{9,13},{10,... | collective-permute-start | bytes 393224 | tf_op jit(solution)/shard_map/ppermute | solution.py:77
  40.6 10.3 %collective-permute-start.13 = (bf16[64,1024]{1,0:T(8,128)(2,1)S(1)}, bf16[64,1024]{1,0:T(8,128)(2,1)S(1)}, u32[]{:S(2)}, u32[]{:S(2)}) collective-permute-start(bf16[64,1024]{1,0:T(8,128)(2,1)S(1)} %get-tuple-element.58), channel_id=1, source_target_pairs={{0,6},{1,7},{2,4},{3,5},{4,2},{5,3},{6,0},{7,1},{8,14},{9,15},{10,... | collective-permute-start | bytes 393224 | tf_op jit(solution)/shard_map/ppermute | solution.py:77
  42.1 5.2 %collective-permute-start.15 = (bf16[32,1024]{1,0:T(8,128)(2,1)S(1)}, bf16[32,1024]{1,0:T(8,128)(2,1)S(1)}, u32[]{:S(2)}, u32[]{:S(2)}) collective-permute-start(bf16[32,1024]{1,0:T(8,128)(2,1)S(1)} %add_pieces.2.refs_0_.refs_1_), channel_id=1, source_target_pairs={{0,16},{8,24},{16,0},{24,8},{1,17},{9,25},{17,1},{25,9},{2,18},{10... | collective-permute-start | bytes 196616 | tf_op jit(solution)/shard_map/ppermute | solution.py:77
  42.1 5.2 %collective-permute-start.14 = (bf16[32,1024]{1,0:T(8,128)(2,1)S(1)}, bf16[32,1024]{1,0:T(8,128)(2,1)S(1)}, u32[]{:S(2)}, u32[]{:S(2)}) collective-permute-start(bf16[32,1024]{1,0:T(8,128)(2,1)S(1)} %add_pieces.2.refs_0_.refs_1_), channel_id=1, source_target_pairs={{0,8},{8,0},{16,24},{24,16},{1,9},{9,1},{17,25},{25,17},{2,10},{10... | collective-permute-start | bytes 196616 | tf_op jit(solution)/shard_map/ppermute | solution.py:77
  47.3 6.7 %collective-permute-start.24 = (bf16[96,1024]{1,0:T(8,128)(2,1)S(1)}, bf16[96,1024]{1,0:T(8,128)(2,1)S(1)}, u32[]{:S(2)}, u32[]{:S(2)}) collective-permute-start(bf16[96,1024]{1,0:T(8,128)(2,1)S(1)} %stack.5.refs_4_.refs_3_), channel_id=1, source_target_pairs={{0,6},{1,7},{2,4},{3,5},{4,2},{5,3},{6,0},{7,1},{8,14},{9,15},{10,... | collective-permute-start | bytes 589832 | tf_op jit(solution)/shard_map/ppermute | solution.py:77
  48.7 7.3 %collective-permute-start.22 = (bf16[96,1024]{1,0:T(8,128)(2,1)S(1)}, bf16[96,1024]{1,0:T(8,128)(2,1)S(1)}, u32[]{:S(2)}, u32[]{:S(2)}) collective-permute-start(bf16[96,1024]{1,0:T(8,128)(2,1)S(1)} %stack.5.refs_4_.refs_3_), channel_id=1, source_target_pairs={{0,4},{1,5},{2,6},{3,7},{4,0},{5,1},{6,2},{7,3},{8,12},{9,13},{10,... | collective-permute-start | bytes 589832 | tf_op jit(solution)/shard_map/ppermute | solution.py:77
  49.9 6.1 %collective-permute-start.19 = (bf16[96,1024]{1,0:T(8,128)(2,1)S(1)}, bf16[96,1024]{1,0:T(8,128)(2,1)S(1)}, u32[]{:S(2)}, u32[]{:S(2)}) collective-permute-start(bf16[96,1024]{1,0:T(8,128)(2,1)S(1)} %stack.5.refs_4_.refs_3_), channel_id=1, source_target_pairs={{0,2},{1,3},{2,0},{3,1},{4,6},{5,7},{6,4},{7,5},{8,10},{9,11},{10,... | collective-permute-start | bytes 589832 | tf_op jit(solution)/shard_map/ppermute | solution.py:77
  50.9 5.7 %collective-permute-start.17 = (bf16[64,1024]{1,0:T(8,128)(2,1)S(1)}, bf16[64,1024]{1,0:T(8,128)(2,1)S(1)}, u32[]{:S(2)}, u32[]{:S(2)}) collective-permute-start(bf16[64,1024]{1,0:T(8,128)(2,1)S(1)} %get-tuple-element.64), channel_id=1, source_target_pairs={{0,1},{1,0},{2,3},{3,2},{4,5},{5,4},{6,7},{7,6},{8,9},{9,8},{10,11... | collective-permute-start | bytes 393224 | tf_op jit(solution)/shard_map/ppermute | solution.py:77
  51.0 5.7 %collective-permute-start.18 = (bf16[64,1024]{1,0:T(8,128)(2,1)S(1)}, bf16[64,1024]{1,0:T(8,128)(2,1)S(1)}, u32[]{:S(2)}, u32[]{:S(2)}) collective-permute-start(bf16[64,1024]{1,0:T(8,128)(2,1)S(1)} %get-tuple-element.63), channel_id=1, source_target_pairs={{0,1},{1,0},{2,3},{3,2},{4,5},{5,4},{6,7},{7,6},{8,9},{9,8},{10,11... | collective-permute-start | bytes 393224 | tf_op jit(solution)/shard_map/ppermute | solution.py:77
  54.0 3.8 %collective-permute-start.20 = (bf16[96,1024]{1,0:T(8,128)(2,1)S(1)}, bf16[96,1024]{1,0:T(8,128)(2,1)S(1)}, u32[]{:S(2)}, u32[]{:S(2)}) collective-permute-start(bf16[96,1024]{1,0:T(8,128)(2,1)S(1)} %stack.5.refs_4_.refs_3_), channel_id=1, source_target_pairs={{0,1},{1,0},{2,3},{3,2},{4,5},{5,4},{6,7},{7,6},{8,9},{9,8},{10,11... | collective-permute-start | bytes 589832 | tf_op jit(solution)/shard_map/ppermute | solution.py:77
  54.1 4.3 %copy-start.2 = (bf16[32,1024]{1,0:T(8,128)(2,1)S(1)}, bf16[32,1024]{1,0:T(8,128)(2,1)}, u32[]{:S(2)}) copy-start(bf16[32,1024]{1,0:T(8,128)(2,1)} %add_pieces.3.refs_3_) | copy-start | bytes 196612
  56.0 2.9 %collective-permute-start.25 = (bf16[96,1024]{1,0:T(8,128)(2,1)S(1)}, bf16[96,1024]{1,0:T(8,128)(2,1)S(1)}, u32[]{:S(2)}, u32[]{:S(2)}) collective-permute-start(bf16[96,1024]{1,0:T(8,128)(2,1)S(1)} %stack.9.refs_3_), channel_id=1, source_target_pairs={{0,1},{1,0},{2,3},{3,2},{4,5},{5,4},{6,7},{7,6},{8,9},{9,8},{10,11... | collective-permute-start | bytes 589832 | tf_op jit(solution)/shard_map/ppermute | solution.py:77
  56.1 3.3 %collective-permute-start.23 = (bf16[96,1024]{1,0:T(8,128)(2,1)S(1)}, bf16[96,1024]{1,0:T(8,128)(2,1)S(1)}, u32[]{:S(2)}, u32[]{:S(2)}) collective-permute-start(bf16[96,1024]{1,0:T(8,128)(2,1)S(1)} %stack.8.refs_3_), channel_id=1, source_target_pairs={{0,1},{1,0},{2,3},{3,2},{4,5},{5,4},{6,7},{7,6},{8,9},{9,8},{10,11... | collective-permute-start | bytes 589832 | tf_op jit(solution)/shard_map/ppermute | solution.py:77
  57.9 0.9 %copy-start.1 = (bf16[256,512]{1,0:T(8,128)(2,1)S(1)}, bf16[256,512]{1,0:T(8,128)(2,1)}, u32[]{:S(2)}) copy-start(bf16[256,512]{1,0:T(8,128)(2,1)} %input_grads.1.refs_2_) | copy-start | bytes 786436
  58.8 1.5 %collective-permute-start.21 = (bf16[96,1024]{1,0:T(8,128)(2,1)S(1)}, bf16[96,1024]{1,0:T(8,128)(2,1)S(1)}, u32[]{:S(2)}, u32[]{:S(2)}) collective-permute-start(bf16[96,1024]{1,0:T(8,128)(2,1)S(1)} %stack.7.refs_3_), channel_id=1, source_target_pairs={{0,1},{1,0},{2,3},{3,2},{4,5},{5,4},{6,7},{7,6},{8,9},{9,8},{10,11... | collective-permute-start | bytes 589832 | tf_op jit(solution)/shard_map/ppermute | solution.py:77

commit v6 on v5

--- a/solution.py
+++ b/solution.py
@@ -13,6 +13,7 @@
 NT = (((1,), (1,)), ((), ()))
 TN = (((0,), (0,)), ((), ()))
 MIB = 1 << 20
+STEPS = 4
 
 
 def mxu(first, second, dims=NN):
@@ -342,90 +343,73 @@
     return local(body, shape(len(values) * rows, width), tuple(values), "stack", ties=ties, flops=flops)
 
 
-def input_grads(near, twins, in_proj, tok):
-    features, width = in_proj.shape
-    rows = 2 * near.shape[0]
-
-    def body(near_ref, twins_ref, proj_ref, out_ref, rows_ref):
-        me = lax.axis_index("expert")
-        for mask in range(rows // tok):
-            src = (near_ref, twins_ref)[mask % 2]
-            rows_ref[block(me ^ mask, tok), :] = src[pl.ds(mask // 2 * tok, tok), :]
-        out_ref[...] = mxu(rows_ref[...], proj_ref[...], NT).astype(BF16)
-
-    return local(
-        body,
-        shape(rows, features),
-        (near, twins, in_proj),
-        "input_grads",
-        scratch=[pltpu.VMEM((rows, width), BF16)],
-        limit=16,
-        flops=2 * rows * features * width,
-    )
-
-
 def arrange(value, chips, tok, tie):
     count, rows, features = value.shape
 
-    def body(x_ref, *out_refs):
+    def body(x_ref, out_ref):
         me = lax.axis_index("expert")
         group = lax.axis_index("dp") if count > 1 else 0
-        for mask in range(count):
-            for k in range(chips):
-                for twin in range(2):
-                    out_refs[k][pl.ds((twin * count + mask) * tok, tok), :] = x_ref[
-                        group ^ mask, block(me ^ (2 * k + twin), tok), :
-                    ]
-
-    out = tuple(shape(2 * count * tok, features) for _ in range(chips))
-    return local(body, out, (value,), "arrange", ties=(tie,))
-
-
-def proj_round(x_rows, near, far, chip, tok, before, last):
+        for side in range(2 * chips):
+            for mask in range(count):
+                out_ref[pl.ds((side * count + mask) * tok, tok), :] = x_ref[
+                    group ^ mask, block(me ^ side, tok), :
+                ]
+
+    return local(body, shape(count * rows, features), (value,), "arrange", ties=(tie,))
+
+
+def finish(x_rows, near, twins, far, in_proj, tok):
     rows, features = x_rows.shape
-    width = near[0].shape[1]
-    given = [x_rows, *near, *far] + ([] if before is None else [before])
-    steps = 4 if features % 512 == 0 else 1
+    width = near.shape[1]
+    sides = 2 * near.shape[0] // tok
+    count = rows // tok // sides
+    far = [piece for pair in far for piece in pair]
+    given = (x_rows, near, twins, in_proj, *far)
+    steps = STEPS if features % (128 * STEPS) == 0 else 1
     tile = features // steps
 
     def body(*refs):
-        x_ref = refs[0]
-        out_ref, rows_ref = refs[len(given)], refs[len(given) + 1]
-        for twin in range(2):
-            start = twin * (rows // 2)
-            rows_ref[pl.ds(start, tok), :] = refs[1 + twin][pl.ds(chip * tok, tok), :]
-            if far:
-                rows_ref[pl.ds(start + tok, rows // 2 - tok), :] = refs[3 + twin][...]
+        x_ref, near_ref, twins_ref, in_proj_ref = refs[:4]
+        far_refs = refs[4 : len(given)]
+        input_ref, proj_ref, rows_ref, whole_ref, own_ref, result_ref, sems = refs[len(given) :]
+        me = lax.axis_index("expert")
+        for side in range(sides):
+            src = (near_ref, twins_ref)[side % 2]
+            piece = src[pl.ds(side // 2 * tok, tok), :]
+            rows_ref[pl.ds(side * count * tok, tok), :] = piece
+            own_ref[block(me ^ side, tok), :] = piece
+            if far_refs:
+                rows_ref[pl.ds((side * count + 1) * tok, (count - 1) * tok), :] = far_refs[side][...]
         copies = []
         for i in range(steps):
             part = pl.ds(i * tile, tile)
-            total = mxu(x_ref[:, part], rows_ref[...], TN)
-            if before is not None:
-                total = total + refs[len(given) - 1][part, :]
-            if last:
-                whole_ref, sems = refs[len(given) + 2], refs[len(given) + 3]
-                whole_ref[part, :] = total
-                copies.append(pltpu.make_async_copy(whole_ref.at[part], out_ref.at[part], sems.at[i]))
-                copies[-1].start()
-            else:
-                out_ref[part, :] = total
+            whole_ref[part, :] = mxu(x_ref[:, part], rows_ref[...], TN)
+            copies.append(pltpu.make_async_copy(whole_ref.at[part], proj_ref.at[part], sems.at[i]))
+            copies[-1].start()
+        result_ref[...] = mxu(own_ref[...], in_proj_ref[...], NT).astype(BF16)
+        copies.append(pltpu.make_async_copy(result_ref, input_ref, sems.at[steps]))
+        copies[-1].start()
         for copy in copies:
             copy.wait()
 
-    scratch = [pltpu.VMEM((rows, width), BF16)]
-    if last:
-        scratch += [pltpu.VMEM((features, width), F32), pltpu.SemaphoreType.DMA((steps,))]
+    own_rows = sides * tok
     return pl.pallas_call(
         body,
-        out_shape=shape(features, width, F32),
+        out_shape=(shape(own_rows, features), shape(features, width, F32)),
         in_specs=[VMEM] * len(given),
-        out_specs=ANY if last else VMEM,
-        scratch_shapes=scratch,
-        compiler_params=pltpu.CompilerParams(vmem_limit_bytes=16 * MIB),
+        out_specs=(ANY, ANY),
+        scratch_shapes=[
+            pltpu.VMEM((rows, width), BF16),
+            pltpu.VMEM((features, width), F32),
+            pltpu.VMEM((own_rows, width), BF16),
+            pltpu.VMEM((own_rows, features), BF16),
+            pltpu.SemaphoreType.DMA((steps + 1,)),
+        ],
+        compiler_params=pltpu.CompilerParams(vmem_limit_bytes=24 * MIB),
         cost_estimate=pl.CostEstimate(
             flops=2 * rows * features * width, bytes_accessed=4 * MIB, transcendentals=0
         ),
-        name="proj_round",
+        name="finish",
     )(*given)
 
 
@@ -479,24 +463,12 @@
     split = near.shape[0] // parts
     twins = [xor_permute(near[i * split : (i + 1) * split], "expert", 1) for i in range(parts)]
     twins = jnp.concatenate(twins, axis=0)
-    input_grad = input_grads(near, twins, in_proj, tok)
-    far = [() for _ in range(chips)]
-    x_all = arrange(x_groups, chips, tok, latent_grad)
-    order = [0] + list(range(chips - 1, 0, -1))
+    x_rows = arrange(x_groups, chips, tok, latent_grad)
+    far = []
     if gather_groups:
-        far[0] = (own, xor_permute(own, "expert", 1))
-    proj_grad = proj_round(x_all[0], (near, twins), far[0], 0, tok, None, False)
-    if gather_groups:
-        pieces = {k: xor_permute(own, "expert", 2 * k) for k in order[1:]}
-        for k in order[1:]:
-            if k == order[-1]:
-                ties = (proj_grad, input_grad, combined)
-            else:
-                ties = (pieces[order[-1]],) if k == order[-2] else ()
-            relay = stack([pieces[k]], pieces[k].shape[0], ties)
-            far[k] = (relay, xor_permute(relay, "expert", 1))
-    for k in order[1:]:
-        proj_grad = proj_round(x_all[k], (near, twins), far[k], k, tok, proj_grad, k == order[-1])
+        pieces = [own] + [xor_permute(own, "expert", 2 * k) for k in range(1, chips)]
+        far = [(piece, xor_permute(piece, "expert", 1)) for piece in pieces]
+    input_grad, proj_grad = finish(x_rows, near, twins, far, in_proj, tok)
     if not gather_groups:
         proj_grad = lax.psum(proj_grad, "dp")
     return (combined, input_grad, proj_grad)

time: 62.2 us -> 60.6 us (0.974)
  Pallas kernels: 15.9 us -> 14.1 us
  waiting for transfers between devices: 15.7 us -> 16.6 us
    pallas_call x21 -> x17, Pallas kernels: 12.9 us -> 11.7 us  [local(): pl.pallas_call(kernel, out_shape=outs, in_specs=[spec] * len(args) + [ANY...]
    ppermute x26, waiting for transfers between devices: 15.7 us -> 16.6 us  [xor_permute(): return lax.ppermute(value, axis, [(i, i ^ mask) for i in range(size)])]
    pallas_call x4 -> x1, Pallas kernels: 3 us -> 2.39 us  [finish(): pl.pallas_call(body, out_shape=(shape(own_rows, features), shape(features...]
  transfers between devices with their start and end apart: 27 -> 27, of which waited for: 11 -> 13; matrix products, arithmetic and copies ran while one was open for 0% -> 0% of each run, Pallas kernels for 20% -> 16%
where the time goes in v6:
time: 60.6 us; the launch traced here: 60.4 us
  starting transfers between devices  28.9 us (48%)
  waiting for transfers between devices  16.6 us (27%)
  Pallas kernels  14.1 us (23%)
  between operations  0.78 us (1%)
    ppermute x26, starting transfers between devices, xor_permute(): return lax.ppermute(value, axis, [(i, i ^ mask) for i in range(size)])  24.1 us
    ppermute x26, waiting for transfers between devices, xor_permute(): return lax.ppermute(value, axis, [(i, i ^ mask) for i in range(size)])  16.6 us
    pallas_call x17, Pallas kernels, local(): pl.pallas_call(kernel, out_shape=outs, in_specs=[spec] * len(args) + [ANY...  11.7 us
    all_to_all x1, starting transfers between devices, per_device(): lax.all_to_all(x_spread, 'dp', split_axis=0, concat_axis=0, tiled=True)  4.87 us
    pallas_call x1, Pallas kernels, finish(): pl.pallas_call(body, out_shape=(shape(own_rows, features), shape(features...  2.39 us
  transfers between devices with their start and end apart: 27, of which 13 were waited for; matrix products, arithmetic and copies ran while one was open for 0% of the time, Pallas kernels for 16%

profile of v6, /device:TPU:0, one launch (start us, length us, event | category | flops | bytes accessed | tf_op | source)
XLA Modules:
  0.0 60.4 jit_solution(12123134604561093434)
XLA Ops:
  0.6 2.0 %project.1 = (bf16[128,1024]{1,0:T(8,128)(2,1)S(1)}, bf16[96,1024]{1,0:T(8,128)(2,1)S(1)}, bf16[80,1024]{1,0:T(8,128)(2,1)S(1)}, bf16[256,512]{1,0:T(8,128)(2,1)S(1)}) custom-call(bf16[256,512]{1,0:T(8,128)(2,1)} %refs_0_.2, bf16[512,1024]{1,0:T(8,128)(2,1)} %refs_3_.1, bf16[32,1024]{1,0:T(8,128)(2,1)} %refs_2_.1, s32[8,32]{1,0:T(8,128)} %bitcast.2, ...), custom_call_target="tpu_custom_call" | custom-call | flops 268435456 | bytes 1048576 | tf_op jit(solution)/shard_map/project/pallas_call | solution.py:40
  2.6 0.5 collective-permute-start
  3.1 1.0 %spread.1.refs_3_ = bf16[4,256,512]{2,1,0:T(8,128)(2,1)} custom-call(bf16[256,512]{1,0:T(8,128)(2,1)S(1)} %get-tuple-element.34.refs_0_), custom_call_target="tpu_custom_call" | custom-call | bytes 1048576 | tf_op jit(solution)/shard_map/spread/pallas_call | solution.py:40
  4.2 0.1 collective-permute-done.refs_2_
  4.3 0.1 streams.1
  4.3 2.9 %collective-permute-start.1 = (bf16[96,1024]{1,0:T(8,128)(2,1)S(1)}, bf16[96,1024]{1,0:T(8,128)(2,1)S(1)}, u32[]{:S(2)}, u32[]{:S(2)}) collective-permute-start(bf16[96,1024]{1,0:T(8,128)(2,1)S(1)} %get-tuple-element.35.refs_0_), channel_id=1, source_target_pairs={{0,2},{1,3},{2,0},{3,1},{4,6},{5,7},{6,4},{7,5},{8,10},{9,11},{10,... | collective-permute-start | bytes 589832 | tf_op jit(solution)/shard_map/ppermute | solution.py:78
  7.3 1.5 %collective-permute-start.2 = (bf16[80,1024]{1,0:T(8,128)(2,1)S(1)}, bf16[80,1024]{1,0:T(8,128)(2,1)S(1)}, u32[]{:S(2)}, u32[]{:S(2)}) collective-permute-start(bf16[80,1024]{1,0:T(8,128)(2,1)S(1)} %get-tuple-element.36.refs_1_), channel_id=1, source_target_pairs={{0,4},{1,5},{2,6},{3,7},{4,0},{5,1},{6,2},{7,3},{8,12},{9,13},{10,... | collective-permute-start | bytes 491528 | tf_op jit(solution)/shard_map/ppermute | solution.py:78
  8.8 4.9 %all-to-all-start = ((bf16[4,256,512]{2,1,0:T(8,128)(2,1)}), bf16[4,256,512]{2,1,0:T(8,128)(2,1)S(1)}, u32[]{:S(2)}, u32[]{:S(2)}) async-start(bf16[4,256,512]{2,1,0:T(8,128)(2,1)} %spread.1.refs_3_), calls=%async_computation | async-start | bytes 2097152 | tf_op jit(solution)/shard_map/all_to_all | solution.py:435
  13.7 0.0 collective-permute-done.2.refs_3_
  13.7 0.0 collective-permute-done.1.refs_2_
  13.7 0.1 merge.1
  13.7 1.1 %collective-permute-start.3 = (bf16[112,1024]{1,0:T(8,128)(2,1)S(1)}, bf16[112,1024]{1,0:T(8,128)(2,1)S(1)}, u32[]{:S(2)}, u32[]{:S(2)}) collective-permute-start(bf16[112,1024]{1,0:T(8,128)(2,1)S(1)} %get-tuple-element.37.refs_0_), channel_id=1, source_target_pairs={{0,4},{1,5},{2,6},{3,7},{4,0},{5,1},{6,2},{7,3},{8,12},{9,13},{10,... | collective-permute-start | bytes 688136 | tf_op jit(solution)/shard_map/ppermute | solution.py:78
  14.9 1.0 %collective-permute-start.4 = (bf16[96,1024]{1,0:T(8,128)(2,1)S(1)}, bf16[96,1024]{1,0:T(8,128)(2,1)S(1)}, u32[]{:S(2)}, u32[]{:S(2)}) collective-permute-start(bf16[96,1024]{1,0:T(8,128)(2,1)S(1)} %get-tuple-element.38.refs_1_), channel_id=1, source_target_pairs={{0,2},{1,3},{2,0},{3,1},{4,6},{5,7},{6,4},{7,5},{8,10},{9,11},{10,... | collective-permute-start | bytes 589832 | tf_op jit(solution)/shard_map/ppermute | solution.py:78
  15.9 2.9 %load.1 = (bf16[2,1024,768]{2,1,0:T(8,128)(2,1)S(1)}, bf16[2,768,1024]{2,1,0:T(8,128)(2,1)S(1)}) custom-call(bf16[2,1024,768]{2,1,0:T(8,128)(2,1)} %refs_0_.3, bf16[2,768,1024]{2,1,0:T(8,128)(2,1)} %refs_1_.3), custom_call_target="tpu_custom_call" | custom-call | bytes 1048576 | tf_op jit(solution)/shard_map/load/pallas_call | solution.py:40
  18.7 1.8 %collective-permute-done.4.refs_3_ = bf16[96,1024]{1,0:T(8,128)(2,1)S(1)} collective-permute-done((bf16[96,1024]{1,0:T(8,128)(2,1)S(1)}, bf16[96,1024]{1,0:T(8,128)(2,1)S(1)}, u32[]{:S(2)}, u32[]{:S(2)}) %collective-permute-start.4) | collective-permute-done | bytes 196640 | tf_op jit(solution)/shard_map/ppermute | solution.py:78
  20.6 0.1 collective-permute-done.3.refs_2_
  20.6 0.1 settle.1.refs_0_.refs_1_
  20.7 0.1 collective-permute-start.5
  20.8 0.6 preacts.1.refs_0_
  21.4 1.4 %collective-permute-done.5.refs_2_ = bf16[272,1024]{1,0:T(8,128)(2,1)S(1)} collective-permute-done((bf16[272,1024]{1,0:T(8,128)(2,1)S(1)}, bf16[272,1024]{1,0:T(8,128)(2,1)S(1)}, u32[]{:S(2)}, u32[]{:S(2)}) %collective-permute-start.5) | collective-permute-done | bytes 557088 | tf_op jit(solution)/shard_map/ppermute | solution.py:78
  22.7 3.1 %experts.1 = (bf16[256,1536]{1,0:T(8,128)(2,1)S(1)}, bf16[128,1024]{1,0:T(8,128)(2,1)S(1)}, bf16[128,1024]{1,0:T(8,128)(2,1)S(1)}) custom-call(f32[128,1536]{1,0:T(8,128)S(1)} %preacts.1.refs_0_, bf16[272,1024]{1,0:T(8,128)(2,1)S(1)} %settle.1.refs_0_.refs_1_, bf16[272,1024]{1,0:T(8,128)(2,1)S(1)} %collective-permute-done.5.refs_2_, ...), custom_call_target="tpu_custom_call" | custom-call | flops 2013265920 | bytes 1048576 | tf_op jit(solution)/shard_map/experts/pallas_call | solution.py:40
  25.8 0.2 collective-permute-start.7
  26.0 1.0 %outputs.1 = (bf16[128,1024]{1,0:T(8,128)(2,1)S(1)}, bf16[128,1024]{1,0:T(8,128)(2,1)S(1)}) custom-call(bf16[256,1536]{1,0:T(8,128)(2,1)S(1)} %get-tuple-element.41.refs_0_, bf16[2,768,1024]{2,1,0:T(8,128)(2,1)S(1)} %get-tuple-element.40.refs_5_.refs_4_.refs_1_), custom_call_target="tpu_custom_call" | custom-call | flops 805306368 | bytes 1048576 | tf_op jit(solution)/shard_map/outputs/pallas_call | solution.py:40
  27.0 0.4 collective-permute-start.6
  27.4 0.0 collective-permute-done.7.refs_1_
  27.4 0.1 pieces.3
  27.5 1.2 %collective-permute-start.8 = (bf16[32,1024]{1,0:T(8,128)(2,1)S(1)}, bf16[32,1024]{1,0:T(8,128)(2,1)S(1)}, u32[]{:S(2)}, u32[]{:S(2)}) collective-permute-start(bf16[32,1024]{1,0:T(8,128)(2,1)S(1)} %get-tuple-element.48), channel_id=1, source_target_pairs={{0,2},{1,3},{2,0},{3,1},{4,6},{5,7},{6,4},{7,5},{8,10},{9,11},{10,... | collective-permute-start | bytes 196616 | tf_op jit(solution)/shard_map/ppermute | solution.py:78
  28.7 1.0 %collective-permute-start.9 = (bf16[32,1024]{1,0:T(8,128)(2,1)S(1)}, bf16[32,1024]{1,0:T(8,128)(2,1)S(1)}, u32[]{:S(2)}, u32[]{:S(2)}) collective-permute-start(bf16[32,1024]{1,0:T(8,128)(2,1)S(1)} %get-tuple-element.49), channel_id=1, source_target_pairs={{0,4},{1,5},{2,6},{3,7},{4,0},{5,1},{6,2},{7,3},{8,12},{9,13},{10,... | collective-permute-start | bytes 196616 | tf_op jit(solution)/shard_map/ppermute | solution.py:78
  29.6 1.4 %collective-permute-start.10 = (bf16[32,1024]{1,0:T(8,128)(2,1)S(1)}, bf16[32,1024]{1,0:T(8,128)(2,1)S(1)}, u32[]{:S(2)}, u32[]{:S(2)}) collective-permute-start(bf16[32,1024]{1,0:T(8,128)(2,1)S(1)} %get-tuple-element.50), channel_id=1, source_target_pairs={{0,6},{1,7},{2,4},{3,5},{4,2},{5,3},{6,0},{7,1},{8,14},{9,15},{10,... | collective-permute-start | bytes 196616 | tf_op jit(solution)/shard_map/ppermute | solution.py:78
  31.1 0.0 collective-permute-done.6.refs_1_
  31.1 0.1 pieces.2
  31.1 0.7 %collective-permute-done.8.refs_1_ = bf16[32,1024]{1,0:T(8,128)(2,1)S(1)} collective-permute-done((bf16[32,1024]{1,0:T(8,128)(2,1)S(1)}, bf16[32,1024]{1,0:T(8,128)(2,1)S(1)}, u32[]{:S(2)}, u32[]{:S(2)}) %collective-permute-start.8) | collective-permute-done | bytes 65568 | tf_op jit(solution)/shard_map/ppermute | solution.py:78
  31.8 1.8 %collective-permute-done.9.refs_2_ = bf16[32,1024]{1,0:T(8,128)(2,1)S(1)} collective-permute-done((bf16[32,1024]{1,0:T(8,128)(2,1)S(1)}, bf16[32,1024]{1,0:T(8,128)(2,1)S(1)}, u32[]{:S(2)}, u32[]{:S(2)}) %collective-permute-start.9) | collective-permute-done | bytes 65568 | tf_op jit(solution)/shard_map/ppermute | solution.py:78
  33.6 1.2 %collective-permute-done.10.refs_3_ = bf16[32,1024]{1,0:T(8,128)(2,1)S(1)} collective-permute-done((bf16[32,1024]{1,0:T(8,128)(2,1)S(1)}, bf16[32,1024]{1,0:T(8,128)(2,1)S(1)}, u32[]{:S(2)}, u32[]{:S(2)}) %collective-permute-start.10) | collective-permute-done | bytes 65568 | tf_op jit(solution)/shard_map/ppermute | solution.py:78
  34.8 3.7 %collective-permute-start.16 = (bf16[32,1024]{1,0:T(8,128)(2,1)S(1)}, bf16[32,1024]{1,0:T(8,128)(2,1)S(1)}, u32[]{:S(2)}, u32[]{:S(2)}) collective-permute-start(bf16[32,1024]{1,0:T(8,128)(2,1)S(1)} %add_pieces.2.refs_0_.refs_1_), channel_id=1, source_target_pairs={{0,24},{8,16},{16,8},{24,0},{1,25},{9,17},{17,9},{25,1},{2,26},{10... | collective-permute-start | bytes 196616 | tf_op jit(solution)/shard_map/ppermute | solution.py:78
  38.5 1.1 %collective-permute-start.11 = (bf16[64,1024]{1,0:T(8,128)(2,1)S(1)}, bf16[64,1024]{1,0:T(8,128)(2,1)S(1)}, u32[]{:S(2)}, u32[]{:S(2)}) collective-permute-start(bf16[64,1024]{1,0:T(8,128)(2,1)S(1)} %get-tuple-element.54), channel_id=1, source_target_pairs={{0,2},{1,3},{2,0},{3,1},{4,6},{5,7},{6,4},{7,5},{8,10},{9,11},{10,... | collective-permute-start | bytes 393224 | tf_op jit(solution)/shard_map/ppermute | solution.py:78
  39.7 0.9 %collective-permute-start.12 = (bf16[64,1024]{1,0:T(8,128)(2,1)S(1)}, bf16[64,1024]{1,0:T(8,128)(2,1)S(1)}, u32[]{:S(2)}, u32[]{:S(2)}) collective-permute-start(bf16[64,1024]{1,0:T(8,128)(2,1)S(1)} %get-tuple-element.55), channel_id=1, source_target_pairs={{0,4},{1,5},{2,6},{3,7},{4,0},{5,1},{6,2},{7,3},{8,12},{9,13},{10,... | collective-permute-start | bytes 393224 | tf_op jit(solution)/shard_map/ppermute | solution.py:78
  40.5 1.6 %collective-permute-start.13 = (bf16[64,1024]{1,0:T(8,128)(2,1)S(1)}, bf16[64,1024]{1,0:T(8,128)(2,1)S(1)}, u32[]{:S(2)}, u32[]{:S(2)}) collective-permute-start(bf16[64,1024]{1,0:T(8,128)(2,1)S(1)} %get-tuple-element.56), channel_id=1, source_target_pairs={{0,6},{1,7},{2,4},{3,5},{4,2},{5,3},{6,0},{7,1},{8,14},{9,15},{10,... | collective-permute-start | bytes 393224 | tf_op jit(solution)/shard_map/ppermute | solution.py:78
  42.1 0.0 collective-permute-start.15
  42.1 0.0 collective-permute-done.16.refs_2_
  42.1 0.8 %collective-permute-start.14 = (bf16[32,1024]{1,0:T(8,128)(2,1)S(1)}, bf16[32,1024]{1,0:T(8,128)(2,1)S(1)}, u32[]{:S(2)}, u32[]{:S(2)}) collective-permute-start(bf16[32,1024]{1,0:T(8,128)(2,1)S(1)} %add_pieces.2.refs_0_.refs_1_), channel_id=1, source_target_pairs={{0,8},{8,0},{16,24},{24,16},{1,9},{9,1},{17,25},{25,17},{2,10},{10... | collective-permute-start | bytes 196616 | tf_op jit(solution)/shard_map/ppermute | solution.py:78
  42.9 0.0 all-to-all-done.refs_3_.refs_0_
  42.9 4.4 %collective-permute-done.15.refs_1_ = bf16[32,1024]{1,0:T(8,128)(2,1)S(1)} collective-permute-done((bf16[32,1024]{1,0:T(8,128)(2,1)S(1)}, bf16[32,1024]{1,0:T(8,128)(2,1)S(1)}, u32[]{:S(2)}, u32[]{:S(2)}) %collective-permute-start.15) | collective-permute-done | bytes 65568 | tf_op jit(solution)/shard_map/ppermute | solution.py:78
  47.3 0.0 collective-permute-done.14.refs_0_
  47.3 1.4 %collective-permute-start.24 = (bf16[96,1024]{1,0:T(8,128)(2,1)S(1)}, bf16[96,1024]{1,0:T(8,128)(2,1)S(1)}, u32[]{:S(2)}, u32[]{:S(2)}) collective-permute-start(bf16[96,1024]{1,0:T(8,128)(2,1)S(1)} %stack.2.refs_4_), channel_id=1, source_target_pairs={{0,6},{1,7},{2,4},{3,5},{4,2},{5,3},{6,0},{7,1},{8,14},{9,15},{10,... | collective-permute-start | bytes 589832 | tf_op jit(solution)/shard_map/ppermute | solution.py:78
  48.7 1.2 %collective-permute-start.22 = (bf16[96,1024]{1,0:T(8,128)(2,1)S(1)}, bf16[96,1024]{1,0:T(8,128)(2,1)S(1)}, u32[]{:S(2)}, u32[]{:S(2)}) collective-permute-start(bf16[96,1024]{1,0:T(8,128)(2,1)S(1)} %stack.2.refs_4_), channel_id=1, source_target_pairs={{0,4},{1,5},{2,6},{3,7},{4,0},{5,1},{6,2},{7,3},{8,12},{9,13},{10,... | collective-permute-start | bytes 589832 | tf_op jit(solution)/shard_map/ppermute | solution.py:78
  49.9 0.0 collective-permute-done.11.refs_1_
  49.9 1.0 %collective-permute-start.20 = (bf16[96,1024]{1,0:T(8,128)(2,1)S(1)}, bf16[96,1024]{1,0:T(8,128)(2,1)S(1)}, u32[]{:S(2)}, u32[]{:S(2)}) collective-permute-start(bf16[96,1024]{1,0:T(8,128)(2,1)S(1)} %stack.2.refs_4_), channel_id=1, source_target_pairs={{0,2},{1,3},{2,0},{3,1},{4,6},{5,7},{6,4},{7,5},{8,10},{9,11},{10,... | collective-permute-start | bytes 589832 | tf_op jit(solution)/shard_map/ppermute | solution.py:78
  50.8 0.0 collective-permute-done.12.refs_2_
  50.8 0.0 collective-permute-done.13.refs_3_
  50.9 0.1 collective-permute-start.17
  51.0 0.5 collective-permute-start.18
  51.5 2.5 %collective-permute-done.24.refs_10_ = bf16[96,1024]{1,0:T(8,128)(2,1)S(1)} collective-permute-done((bf16[96,1024]{1,0:T(8,128)(2,1)S(1)}, bf16[96,1024]{1,0:T(8,128)(2,1)S(1)}, u32[]{:S(2)}, u32[]{:S(2)}) %collective-permute-start.24) | collective-permute-done | bytes 196640 | tf_op jit(solution)/shard_map/ppermute | solution.py:78
  54.0 0.0 collective-permute-start.19
  54.0 2.0 %collective-permute-done.22.refs_8_ = bf16[96,1024]{1,0:T(8,128)(2,1)S(1)} collective-permute-done((bf16[96,1024]{1,0:T(8,128)(2,1)S(1)}, bf16[96,1024]{1,0:T(8,128)(2,1)S(1)}, u32[]{:S(2)}, u32[]{:S(2)}) %collective-permute-start.22) | collective-permute-done | bytes 196640 | tf_op jit(solution)/shard_map/ppermute | solution.py:78
  56.0 0.5 collective-permute-start.23
  56.5 0.1 collective-permute-start.21
  56.6 0.1 arrange.1.refs_0_
  56.7 0.7 %add_pieces.3 = bf16[32,1024]{1,0:T(8,128)(2,1)} custom-call(bf16[32,1024]{1,0:T(8,128)(2,1)S(1)} %get-tuple-element.44.refs_0_, bf16[64,1024]{1,0:T(8,128)(2,1)S(1)} %collective-permute-done.11.refs_1_, bf16[64,1024]{1,0:T(8,128)(2,1)S(1)} %collective-permute-done.12.refs_2_, bf16[64,1024]{1,0:T(8,128)(2,1)S(1)} %collective-permute-done.13.refs_3_, ...), custom_call_target="tpu_custom_call" | custom-call | bytes 1048576 | tf_op jit(solution)/shard_map/add_pieces/pallas_call | solution.py:40
  57.4 0.0 collective-permute-done.19.refs_5_
  57.4 0.1 collective-permute-done.25.refs_11_
  57.5 0.3 collective-permute-done.23.refs_9_
  57.7 0.3 collective-permute-done.21.refs_7_
  58.0 2.4 %finish.1 = (bf16[256,512]{1,0:T(8,128)(2,1)}, f32[512,1024]{1,0:T(8,128)}) custom-call(bf16[1024,512]{1,0:T(8,128)(2,1)S(1)} %arrange.1.refs_0_, bf16[128,1024]{1,0:T(8,128)(2,1)S(1)} %stack.3.refs_1_, bf16[128,1024]{1,0:T(8,128)(2,1)S(1)} %pad_maximum_fusion.refs_2_, bf16[512,1024]{1,0:T(8,128)(2,1)S(1)} %copy-done, bf16[96,1024]{1,0:T(8,128)(2,1)S(1)} %stack.2.refs_4_, ...), custom_call_target="tpu_custom_call" | custom-call | flops 1073741824 | bytes 4194304 | tf_op jit(solution)/shard_map/finish/pallas_call | solution.py:396
  (12 shorter events, 0.1 us)
Async XLA Ops:
  2.6 1.7 %collective-permute-start = (bf16[128,1024]{1,0:T(8,128)(2,1)S(1)}, bf16[128,1024]{1,0:T(8,128)(2,1)S(1)}, u32[]{:S(2)}, u32[]{:S(2)}) collective-permute-start(bf16[128,1024]{1,0:T(8,128)(2,1)S(1)} %get-tuple-element.33), channel_id=1, source_target_pairs={{0,1},{1,0},{2,3},{3,2},{4,5},{5,4},{6,7},{7,6},{8,9},{9,8},{10,11... | collective-permute-start | bytes 786440 | tf_op jit(solution)/shard_map/ppermute | solution.py:78
  4.3 9.3 %collective-permute-start.1 = (bf16[96,1024]{1,0:T(8,128)(2,1)S(1)}, bf16[96,1024]{1,0:T(8,128)(2,1)S(1)}, u32[]{:S(2)}, u32[]{:S(2)}) collective-permute-start(bf16[96,1024]{1,0:T(8,128)(2,1)S(1)} %get-tuple-element.35.refs_0_), channel_id=1, source_target_pairs={{0,2},{1,3},{2,0},{3,1},{4,6},{5,7},{6,4},{7,5},{8,10},{9,11},{10,... | collective-permute-start | bytes 589832 | tf_op jit(solution)/shard_map/ppermute | solution.py:78
  7.3 6.4 %collective-permute-start.2 = (bf16[80,1024]{1,0:T(8,128)(2,1)S(1)}, bf16[80,1024]{1,0:T(8,128)(2,1)S(1)}, u32[]{:S(2)}, u32[]{:S(2)}) collective-permute-start(bf16[80,1024]{1,0:T(8,128)(2,1)S(1)} %get-tuple-element.36.refs_1_), channel_id=1, source_target_pairs={{0,4},{1,5},{2,6},{3,7},{4,0},{5,1},{6,2},{7,3},{8,12},{9,13},{10,... | collective-permute-start | bytes 491528 | tf_op jit(solution)/shard_map/ppermute | solution.py:78
  8.8 34.1 %all-to-all-start = ((bf16[4,256,512]{2,1,0:T(8,128)(2,1)}), bf16[4,256,512]{2,1,0:T(8,128)(2,1)S(1)}, u32[]{:S(2)}, u32[]{:S(2)}) async-start(bf16[4,256,512]{2,1,0:T(8,128)(2,1)} %spread.1.refs_3_), calls=%async_computation | async-start | bytes 2097152 | tf_op jit(solution)/shard_map/all_to_all | solution.py:435
  13.7 6.9 %collective-permute-start.3 = (bf16[112,1024]{1,0:T(8,128)(2,1)S(1)}, bf16[112,1024]{1,0:T(8,128)(2,1)S(1)}, u32[]{:S(2)}, u32[]{:S(2)}) collective-permute-start(bf16[112,1024]{1,0:T(8,128)(2,1)S(1)} %get-tuple-element.37.refs_0_), channel_id=1, source_target_pairs={{0,4},{1,5},{2,6},{3,7},{4,0},{5,1},{6,2},{7,3},{8,12},{9,13},{10,... | collective-permute-start | bytes 688136 | tf_op jit(solution)/shard_map/ppermute | solution.py:78
  14.9 5.7 %collective-permute-start.4 = (bf16[96,1024]{1,0:T(8,128)(2,1)S(1)}, bf16[96,1024]{1,0:T(8,128)(2,1)S(1)}, u32[]{:S(2)}, u32[]{:S(2)}) collective-permute-start(bf16[96,1024]{1,0:T(8,128)(2,1)S(1)} %get-tuple-element.38.refs_1_), channel_id=1, source_target_pairs={{0,2},{1,3},{2,0},{3,1},{4,6},{5,7},{6,4},{7,5},{8,10},{9,11},{10,... | collective-permute-start | bytes 589832 | tf_op jit(solution)/shard_map/ppermute | solution.py:78
  20.7 2.0 %collective-permute-start.5 = (bf16[272,1024]{1,0:T(8,128)(2,1)S(1)}, bf16[272,1024]{1,0:T(8,128)(2,1)S(1)}, u32[]{:S(2)}, u32[]{:S(2)}) collective-permute-start(bf16[272,1024]{1,0:T(8,128)(2,1)S(1)} %settle.1.refs_0_.refs_1_), channel_id=1, source_target_pairs={{0,1},{1,0},{2,3},{3,2},{4,5},{5,4},{6,7},{7,6},{8,9},{9,8},{10,11... | collective-permute-start | bytes 1671176 | tf_op jit(solution)/shard_map/ppermute | solution.py:78
  25.8 1.6 %collective-permute-start.7 = (bf16[128,1024]{1,0:T(8,128)(2,1)S(1)}, bf16[128,1024]{1,0:T(8,128)(2,1)S(1)}, u32[]{:S(2)}, u32[]{:S(2)}) collective-permute-start(bf16[128,1024]{1,0:T(8,128)(2,1)S(1)} %get-tuple-element.46), channel_id=1, source_target_pairs={{0,1},{1,0},{2,3},{3,2},{4,5},{5,4},{6,7},{7,6},{8,9},{9,8},{10,11... | collective-permute-start | bytes 786440 | tf_op jit(solution)/shard_map/ppermute | solution.py:78
  27.0 4.1 %collective-permute-start.6 = (bf16[128,1024]{1,0:T(8,128)(2,1)S(1)}, bf16[128,1024]{1,0:T(8,128)(2,1)S(1)}, u32[]{:S(2)}, u32[]{:S(2)}) collective-permute-start(bf16[128,1024]{1,0:T(8,128)(2,1)S(1)} %get-tuple-element.43), channel_id=1, source_target_pairs={{0,1},{1,0},{2,3},{3,2},{4,5},{5,4},{6,7},{7,6},{8,9},{9,8},{10,11... | collective-permute-start | bytes 786440 | tf_op jit(solution)/shard_map/ppermute | solution.py:78
  27.5 4.3 %collective-permute-start.8 = (bf16[32,1024]{1,0:T(8,128)(2,1)S(1)}, bf16[32,1024]{1,0:T(8,128)(2,1)S(1)}, u32[]{:S(2)}, u32[]{:S(2)}) collective-permute-start(bf16[32,1024]{1,0:T(8,128)(2,1)S(1)} %get-tuple-element.48), channel_id=1, source_target_pairs={{0,2},{1,3},{2,0},{3,1},{4,6},{5,7},{6,4},{7,5},{8,10},{9,11},{10,... | collective-permute-start | bytes 196616 | tf_op jit(solution)/shard_map/ppermute | solution.py:78
  28.7 5.0 %collective-permute-start.9 = (bf16[32,1024]{1,0:T(8,128)(2,1)S(1)}, bf16[32,1024]{1,0:T(8,128)(2,1)S(1)}, u32[]{:S(2)}, u32[]{:S(2)}) collective-permute-start(bf16[32,1024]{1,0:T(8,128)(2,1)S(1)} %get-tuple-element.49), channel_id=1, source_target_pairs={{0,4},{1,5},{2,6},{3,7},{4,0},{5,1},{6,2},{7,3},{8,12},{9,13},{10,... | collective-permute-start | bytes 196616 | tf_op jit(solution)/shard_map/ppermute | solution.py:78
  29.6 5.2 %collective-permute-start.10 = (bf16[32,1024]{1,0:T(8,128)(2,1)S(1)}, bf16[32,1024]{1,0:T(8,128)(2,1)S(1)}, u32[]{:S(2)}, u32[]{:S(2)}) collective-permute-start(bf16[32,1024]{1,0:T(8,128)(2,1)S(1)} %get-tuple-element.50), channel_id=1, source_target_pairs={{0,6},{1,7},{2,4},{3,5},{4,2},{5,3},{6,0},{7,1},{8,14},{9,15},{10,... | collective-permute-start | bytes 196616 | tf_op jit(solution)/shard_map/ppermute | solution.py:78
  34.8 7.3 %collective-permute-start.16 = (bf16[32,1024]{1,0:T(8,128)(2,1)S(1)}, bf16[32,1024]{1,0:T(8,128)(2,1)S(1)}, u32[]{:S(2)}, u32[]{:S(2)}) collective-permute-start(bf16[32,1024]{1,0:T(8,128)(2,1)S(1)} %add_pieces.2.refs_0_.refs_1_), channel_id=1, source_target_pairs={{0,24},{8,16},{16,8},{24,0},{1,25},{9,17},{17,9},{25,1},{2,26},{10... | collective-permute-start | bytes 196616 | tf_op jit(solution)/shard_map/ppermute | solution.py:78
  38.5 11.3 %collective-permute-start.11 = (bf16[64,1024]{1,0:T(8,128)(2,1)S(1)}, bf16[64,1024]{1,0:T(8,128)(2,1)S(1)}, u32[]{:S(2)}, u32[]{:S(2)}) collective-permute-start(bf16[64,1024]{1,0:T(8,128)(2,1)S(1)} %get-tuple-element.54), channel_id=1, source_target_pairs={{0,2},{1,3},{2,0},{3,1},{4,6},{5,7},{6,4},{7,5},{8,10},{9,11},{10,... | collective-permute-start | bytes 393224 | tf_op jit(solution)/shard_map/ppermute | solution.py:78
  39.7 11.2 %collective-permute-start.12 = (bf16[64,1024]{1,0:T(8,128)(2,1)S(1)}, bf16[64,1024]{1,0:T(8,128)(2,1)S(1)}, u32[]{:S(2)}, u32[]{:S(2)}) collective-permute-start(bf16[64,1024]{1,0:T(8,128)(2,1)S(1)} %get-tuple-element.55), channel_id=1, source_target_pairs={{0,4},{1,5},{2,6},{3,7},{4,0},{5,1},{6,2},{7,3},{8,12},{9,13},{10,... | collective-permute-start | bytes 393224 | tf_op jit(solution)/shard_map/ppermute | solution.py:78
  40.5 17.5 %copy-start = (bf16[512,1024]{1,0:T(8,128)(2,1)S(1)}, bf16[512,1024]{1,0:T(8,128)(2,1)}, u32[]{:S(2)}) copy-start(bf16[512,1024]{1,0:T(8,128)(2,1)} %refs_3_.1) | copy-start | bytes 3145732
  40.5 10.3 %collective-permute-start.13 = (bf16[64,1024]{1,0:T(8,128)(2,1)S(1)}, bf16[64,1024]{1,0:T(8,128)(2,1)S(1)}, u32[]{:S(2)}, u32[]{:S(2)}) collective-permute-start(bf16[64,1024]{1,0:T(8,128)(2,1)S(1)} %get-tuple-element.56), channel_id=1, source_target_pairs={{0,6},{1,7},{2,4},{3,5},{4,2},{5,3},{6,0},{7,1},{8,14},{9,15},{10,... | collective-permute-start | bytes 393224 | tf_op jit(solution)/shard_map/ppermute | solution.py:78
  42.1 5.2 %collective-permute-start.15 = (bf16[32,1024]{1,0:T(8,128)(2,1)S(1)}, bf16[32,1024]{1,0:T(8,128)(2,1)S(1)}, u32[]{:S(2)}, u32[]{:S(2)}) collective-permute-start(bf16[32,1024]{1,0:T(8,128)(2,1)S(1)} %add_pieces.2.refs_0_.refs_1_), channel_id=1, source_target_pairs={{0,16},{8,24},{16,0},{24,8},{1,17},{9,25},{17,1},{25,9},{2,18},{10... | collective-permute-start | bytes 196616 | tf_op jit(solution)/shard_map/ppermute | solution.py:78
  42.1 5.2 %collective-permute-start.14 = (bf16[32,1024]{1,0:T(8,128)(2,1)S(1)}, bf16[32,1024]{1,0:T(8,128)(2,1)S(1)}, u32[]{:S(2)}, u32[]{:S(2)}) collective-permute-start(bf16[32,1024]{1,0:T(8,128)(2,1)S(1)} %add_pieces.2.refs_0_.refs_1_), channel_id=1, source_target_pairs={{0,8},{8,0},{16,24},{24,16},{1,9},{9,1},{17,25},{25,17},{2,10},{10... | collective-permute-start | bytes 196616 | tf_op jit(solution)/shard_map/ppermute | solution.py:78
  47.3 6.7 %collective-permute-start.24 = (bf16[96,1024]{1,0:T(8,128)(2,1)S(1)}, bf16[96,1024]{1,0:T(8,128)(2,1)S(1)}, u32[]{:S(2)}, u32[]{:S(2)}) collective-permute-start(bf16[96,1024]{1,0:T(8,128)(2,1)S(1)} %stack.2.refs_4_), channel_id=1, source_target_pairs={{0,6},{1,7},{2,4},{3,5},{4,2},{5,3},{6,0},{7,1},{8,14},{9,15},{10,... | collective-permute-start | bytes 589832 | tf_op jit(solution)/shard_map/ppermute | solution.py:78
  48.7 7.3 %collective-permute-start.22 = (bf16[96,1024]{1,0:T(8,128)(2,1)S(1)}, bf16[96,1024]{1,0:T(8,128)(2,1)S(1)}, u32[]{:S(2)}, u32[]{:S(2)}) collective-permute-start(bf16[96,1024]{1,0:T(8,128)(2,1)S(1)} %stack.2.refs_4_), channel_id=1, source_target_pairs={{0,4},{1,5},{2,6},{3,7},{4,0},{5,1},{6,2},{7,3},{8,12},{9,13},{10,... | collective-permute-start | bytes 589832 | tf_op jit(solution)/shard_map/ppermute | solution.py:78
  49.9 6.1 %collective-permute-start.20 = (bf16[96,1024]{1,0:T(8,128)(2,1)S(1)}, bf16[96,1024]{1,0:T(8,128)(2,1)S(1)}, u32[]{:S(2)}, u32[]{:S(2)}) collective-permute-start(bf16[96,1024]{1,0:T(8,128)(2,1)S(1)} %stack.2.refs_4_), channel_id=1, source_target_pairs={{0,2},{1,3},{2,0},{3,1},{4,6},{5,7},{6,4},{7,5},{8,10},{9,11},{10,... | collective-permute-start | bytes 589832 | tf_op jit(solution)/shard_map/ppermute | solution.py:78
  50.9 5.6 %collective-permute-start.17 = (bf16[64,1024]{1,0:T(8,128)(2,1)S(1)}, bf16[64,1024]{1,0:T(8,128)(2,1)S(1)}, u32[]{:S(2)}, u32[]{:S(2)}) collective-permute-start(bf16[64,1024]{1,0:T(8,128)(2,1)S(1)} %get-tuple-element.59), channel_id=1, source_target_pairs={{0,1},{1,0},{2,3},{3,2},{4,5},{5,4},{6,7},{7,6},{8,9},{9,8},{10,11... | collective-permute-start | bytes 393224 | tf_op jit(solution)/shard_map/ppermute | solution.py:78
  51.0 6.4 %collective-permute-start.18 = (bf16[64,1024]{1,0:T(8,128)(2,1)S(1)}, bf16[64,1024]{1,0:T(8,128)(2,1)S(1)}, u32[]{:S(2)}, u32[]{:S(2)}) collective-permute-start(bf16[64,1024]{1,0:T(8,128)(2,1)S(1)} %get-tuple-element.60), channel_id=1, source_target_pairs={{0,1},{1,0},{2,3},{3,2},{4,5},{5,4},{6,7},{7,6},{8,9},{9,8},{10,11... | collective-permute-start | bytes 393224 | tf_op jit(solution)/shard_map/ppermute | solution.py:78
  54.0 3.4 %collective-permute-start.19 = (bf16[96,1024]{1,0:T(8,128)(2,1)S(1)}, bf16[96,1024]{1,0:T(8,128)(2,1)S(1)}, u32[]{:S(2)}, u32[]{:S(2)}) collective-permute-start(bf16[96,1024]{1,0:T(8,128)(2,1)S(1)} %stack.2.refs_4_), channel_id=1, source_target_pairs={{0,1},{1,0},{2,3},{3,2},{4,5},{5,4},{6,7},{7,6},{8,9},{9,8},{10,11... | collective-permute-start | bytes 589832 | tf_op jit(solution)/shard_map/ppermute | solution.py:78
  56.0 1.4 %collective-permute-start.25 = (bf16[96,1024]{1,0:T(8,128)(2,1)S(1)}, bf16[96,1024]{1,0:T(8,128)(2,1)S(1)}, u32[]{:S(2)}, u32[]{:S(2)}) collective-permute-start(bf16[96,1024]{1,0:T(8,128)(2,1)S(1)} %collective-permute-done.24.refs_10_), channel_id=1, source_target_pairs={{0,1},{1,0},{2,3},{3,2},{4,5},{5,4},{6,7},{7,6},{8,9},{9,8},{10,11... | collective-permute-start | bytes 589832 | tf_op jit(solution)/shard_map/ppermute | solution.py:78
  56.0 1.7 %collective-permute-start.23 = (bf16[96,1024]{1,0:T(8,128)(2,1)S(1)}, bf16[96,1024]{1,0:T(8,128)(2,1)S(1)}, u32[]{:S(2)}, u32[]{:S(2)}) collective-permute-start(bf16[96,1024]{1,0:T(8,128)(2,1)S(1)} %collective-permute-done.22.refs_8_), channel_id=1, source_target_pairs={{0,1},{1,0},{2,3},{3,2},{4,5},{5,4},{6,7},{7,6},{8,9},{9,8},{10,11... | collective-permute-start | bytes 589832 | tf_op jit(solution)/shard_map/ppermute | solution.py:78
  56.5 1.5 %collective-permute-start.21 = (bf16[96,1024]{1,0:T(8,128)(2,1)S(1)}, bf16[96,1024]{1,0:T(8,128)(2,1)S(1)}, u32[]{:S(2)}, u32[]{:S(2)}) collective-permute-start(bf16[96,1024]{1,0:T(8,128)(2,1)S(1)} %collective-permute-done.20.refs_6_), channel_id=1, source_target_pairs={{0,1},{1,0},{2,3},{3,2},{4,5},{5,4},{6,7},{7,6},{8,9},{9,8},{10,11... | collective-permute-start | bytes 589832 | tf_op jit(solution)/shard_map/ppermute | solution.py:78

commit v7 on v6

--- a/solution.py
+++ b/solution.py
@@ -320,19 +320,6 @@
     return local(body, shape(rows, width), tuple(pieces), "add_pieces", ties=ties)
 
 
-def head(value, tails, ties=()):
-    rows, width = value.shape
-    count = len(tails)
-
-    def body(*refs):
-        for tail, out in zip(refs[1 : 1 + count], refs[1 + count :]):
-            out[pl.ds(0, rows), :] = refs[0][...]
-            out[pl.ds(rows, tail.shape[0]), :] = tail[...]
-
-    outs = tuple(shape(rows + tail.shape[0], width) for tail in tails)
-    return local(body, outs, (value, *tails), "head", ties=ties)
-
-
 def stack(values, rows, ties=(), flops=0):
     width = values[0].shape[1]
 
@@ -451,13 +438,13 @@
     latent_grad = add_pieces((lat_pieces[0], *got))
 
     own = ()
+    out_got = scatter(out_pieces)
     if gather_groups:
         across = [xor_permute(latent_grad, "dp", m) for m in range(1, groups)]
-        own = stack(across, tok, ties=(x_groups,))
+        own = stack(across, tok, ties=(x_groups, *out_got))
     after = (own,) if gather_groups else ()
-    sent = head(latent_grad, out_pieces[1:])
-    got = scatter([None, *sent])
-    combined = add_pieces((out_pieces[0], *got), tok, ties=after)
+    got = scatter([latent_grad] * chips)
+    combined = add_pieces((out_pieces[0], *out_got))
     near = stack([latent_grad, *got], tok, ties=after)
     parts = 2
     split = near.shape[0] // parts

time: 60.6 us -> 59.5 us (0.982)
  waiting for transfers between devices: 16.6 us -> 11.9 us
  starting transfers between devices: 28.9 us -> 32.5 us
    ppermute x26 -> x29, waiting for transfers between devices: 16.6 us -> 11.9 us  [xor_permute(): return lax.ppermute(value, axis, [(i, i ^ mask) for i in range(size)])]
    ppermute x26 -> x29, starting transfers between devices: 24.1 us -> 27.6 us  [xor_permute(): return lax.ppermute(value, axis, [(i, i ^ mask) for i in range(size)])]
    pallas_call x17 -> x16, Pallas kernels: 11.7 us -> 11.6 us  [local(): pl.pallas_call(kernel, out_shape=outs, in_specs=[spec] * len(args) + [ANY...]
  transfers between devices with their start and end apart: 27 -> 30, of which waited for: 13 -> 11; matrix products, arithmetic and copies ran while one was open for 0% -> 0% of each run, Pallas kernels for 16% -> 16%
where the time goes in v7:
time: 59.5 us; the launch traced here: 59.3 us
  starting transfers between devices  32.5 us (55%)
  Pallas kernels  14 us (24%)
  waiting for transfers between devices  11.9 us (20%)
  between operations  0.79 us (1%)
    ppermute x29, starting transfers between devices, xor_permute(): return lax.ppermute(value, axis, [(i, i ^ mask) for i in range(size)])  27.6 us
    ppermute x29, waiting for transfers between devices, xor_permute(): return lax.ppermute(value, axis, [(i, i ^ mask) for i in range(size)])  11.9 us
    pallas_call x16, Pallas kernels, local(): pl.pallas_call(kernel, out_shape=outs, in_specs=[spec] * len(args) + [ANY...  11.6 us
    all_to_all x1, starting transfers between devices, per_device(): lax.all_to_all(x_spread, 'dp', split_axis=0, concat_axis=0, tiled=True)  4.87 us
    pallas_call x1, Pallas kernels, finish(): pl.pallas_call(body, out_shape=(shape(own_rows, features), shape(features...  2.39 us
  transfers between devices with their start and end apart: 30, of which 11 were waited for; matrix products, arithmetic and copies ran while one was open for 0% of the time, Pallas kernels for 16%

profile of v7, /device:TPU:0, one launch (start us, length us, event | category | flops | bytes accessed | tf_op | source)
XLA Modules:
  0.0 59.3 jit_solution(14873136285574009910)
XLA Ops:
  0.6 2.0 %project.1 = (bf16[128,1024]{1,0:T(8,128)(2,1)S(1)}, bf16[96,1024]{1,0:T(8,128)(2,1)S(1)}, bf16[80,1024]{1,0:T(8,128)(2,1)S(1)}, bf16[256,512]{1,0:T(8,128)(2,1)S(1)}) custom-call(bf16[256,512]{1,0:T(8,128)(2,1)} %refs_0_.2, bf16[512,1024]{1,0:T(8,128)(2,1)} %refs_3_.1, bf16[32,1024]{1,0:T(8,128)(2,1)} %refs_2_.1, s32[8,32]{1,0:T(8,128)} %bitcast.2, ...), custom_call_target="tpu_custom_call" | custom-call | flops 268435456 | bytes 1048576 | tf_op jit(solution)/shard_map/project/pallas_call | solution.py:40
  2.6 0.5 collective-permute-start
  3.1 1.0 %spread.1.refs_3_ = bf16[4,256,512]{2,1,0:T(8,128)(2,1)} custom-call(bf16[256,512]{1,0:T(8,128)(2,1)S(1)} %get-tuple-element.31.refs_0_), custom_call_target="tpu_custom_call" | custom-call | bytes 1048576 | tf_op jit(solution)/shard_map/spread/pallas_call | solution.py:40
  4.2 0.1 collective-permute-done.refs_2_
  4.3 0.1 streams.1
  4.3 2.9 %collective-permute-start.1 = (bf16[96,1024]{1,0:T(8,128)(2,1)S(1)}, bf16[96,1024]{1,0:T(8,128)(2,1)S(1)}, u32[]{:S(2)}, u32[]{:S(2)}) collective-permute-start(bf16[96,1024]{1,0:T(8,128)(2,1)S(1)} %get-tuple-element.32.refs_0_), channel_id=1, source_target_pairs={{0,2},{1,3},{2,0},{3,1},{4,6},{5,7},{6,4},{7,5},{8,10},{9,11},{10,... | collective-permute-start | bytes 589832 | tf_op jit(solution)/shard_map/ppermute | solution.py:78
  7.3 1.5 %collective-permute-start.2 = (bf16[80,1024]{1,0:T(8,128)(2,1)S(1)}, bf16[80,1024]{1,0:T(8,128)(2,1)S(1)}, u32[]{:S(2)}, u32[]{:S(2)}) collective-permute-start(bf16[80,1024]{1,0:T(8,128)(2,1)S(1)} %get-tuple-element.33.refs_1_), channel_id=1, source_target_pairs={{0,4},{1,5},{2,6},{3,7},{4,0},{5,1},{6,2},{7,3},{8,12},{9,13},{10,... | collective-permute-start | bytes 491528 | tf_op jit(solution)/shard_map/ppermute | solution.py:78
  8.8 4.9 %all-to-all-start = ((bf16[4,256,512]{2,1,0:T(8,128)(2,1)}), bf16[4,256,512]{2,1,0:T(8,128)(2,1)S(1)}, u32[]{:S(2)}, u32[]{:S(2)}) async-start(bf16[4,256,512]{2,1,0:T(8,128)(2,1)} %spread.1.refs_3_), calls=%async_computation | async-start | bytes 2097152 | tf_op jit(solution)/shard_map/all_to_all | solution.py:422
  13.7 0.0 collective-permute-done.1.refs_2_
  13.7 0.1 merge.1
  13.7 1.1 %collective-permute-start.3 = (bf16[112,1024]{1,0:T(8,128)(2,1)S(1)}, bf16[112,1024]{1,0:T(8,128)(2,1)S(1)}, u32[]{:S(2)}, u32[]{:S(2)}) collective-permute-start(bf16[112,1024]{1,0:T(8,128)(2,1)S(1)} %get-tuple-element.34.refs_0_), channel_id=1, source_target_pairs={{0,4},{1,5},{2,6},{3,7},{4,0},{5,1},{6,2},{7,3},{8,12},{9,13},{10,... | collective-permute-start | bytes 688136 | tf_op jit(solution)/shard_map/ppermute | solution.py:78
  14.9 1.0 %collective-permute-start.4 = (bf16[96,1024]{1,0:T(8,128)(2,1)S(1)}, bf16[96,1024]{1,0:T(8,128)(2,1)S(1)}, u32[]{:S(2)}, u32[]{:S(2)}) collective-permute-start(bf16[96,1024]{1,0:T(8,128)(2,1)S(1)} %get-tuple-element.35.refs_1_), channel_id=1, source_target_pairs={{0,2},{1,3},{2,0},{3,1},{4,6},{5,7},{6,4},{7,5},{8,10},{9,11},{10,... | collective-permute-start | bytes 589832 | tf_op jit(solution)/shard_map/ppermute | solution.py:78
  15.9 2.9 %load.1 = (bf16[2,1024,768]{2,1,0:T(8,128)(2,1)S(1)}, bf16[2,768,1024]{2,1,0:T(8,128)(2,1)S(1)}) custom-call(bf16[2,1024,768]{2,1,0:T(8,128)(2,1)} %refs_0_.3, bf16[2,768,1024]{2,1,0:T(8,128)(2,1)} %refs_1_.3), custom_call_target="tpu_custom_call" | custom-call | bytes 1048576 | tf_op jit(solution)/shard_map/load/pallas_call | solution.py:40
  18.7 1.8 %collective-permute-done.4.refs_3_ = bf16[96,1024]{1,0:T(8,128)(2,1)S(1)} collective-permute-done((bf16[96,1024]{1,0:T(8,128)(2,1)S(1)}, bf16[96,1024]{1,0:T(8,128)(2,1)S(1)}, u32[]{:S(2)}, u32[]{:S(2)}) %collective-permute-start.4) | collective-permute-done | bytes 196640 | tf_op jit(solution)/shard_map/ppermute | solution.py:78
  20.6 0.1 collective-permute-done.3.refs_2_
  20.6 0.1 settle.1.refs_0_.refs_1_
  20.7 0.1 collective-permute-start.5
  20.8 0.6 preacts.1.refs_0_
  21.4 1.4 %collective-permute-done.5.refs_2_ = bf16[272,1024]{1,0:T(8,128)(2,1)S(1)} collective-permute-done((bf16[272,1024]{1,0:T(8,128)(2,1)S(1)}, bf16[272,1024]{1,0:T(8,128)(2,1)S(1)}, u32[]{:S(2)}, u32[]{:S(2)}) %collective-permute-start.5) | collective-permute-done | bytes 557088 | tf_op jit(solution)/shard_map/ppermute | solution.py:78
  22.7 3.1 %experts.1 = (bf16[256,1536]{1,0:T(8,128)(2,1)S(1)}, bf16[128,1024]{1,0:T(8,128)(2,1)S(1)}, bf16[128,1024]{1,0:T(8,128)(2,1)S(1)}) custom-call(f32[128,1536]{1,0:T(8,128)S(1)} %preacts.1.refs_0_, bf16[272,1024]{1,0:T(8,128)(2,1)S(1)} %settle.1.refs_0_.refs_1_, bf16[272,1024]{1,0:T(8,128)(2,1)S(1)} %collective-permute-done.5.refs_2_, ...), custom_call_target="tpu_custom_call" | custom-call | flops 2013265920 | bytes 1048576 | tf_op jit(solution)/shard_map/experts/pallas_call | solution.py:40
  25.8 0.2 collective-permute-start.10
  26.0 1.0 %outputs.1 = (bf16[128,1024]{1,0:T(8,128)(2,1)S(1)}, bf16[128,1024]{1,0:T(8,128)(2,1)S(1)}) custom-call(bf16[256,1536]{1,0:T(8,128)(2,1)S(1)} %get-tuple-element.38.refs_0_, bf16[2,768,1024]{2,1,0:T(8,128)(2,1)S(1)} %get-tuple-element.37.refs_5_.refs_4_.refs_1_), custom_call_target="tpu_custom_call" | custom-call | flops 805306368 | bytes 1048576 | tf_op jit(solution)/shard_map/outputs/pallas_call | solution.py:40
  27.0 0.4 collective-permute-start.6
  27.4 0.1 pieces.3
  27.5 1.2 %collective-permute-start.11 = (bf16[32,1024]{1,0:T(8,128)(2,1)S(1)}, bf16[32,1024]{1,0:T(8,128)(2,1)S(1)}, u32[]{:S(2)}, u32[]{:S(2)}) collective-permute-start(bf16[32,1024]{1,0:T(8,128)(2,1)S(1)} %get-tuple-element.48), channel_id=1, source_target_pairs={{0,2},{1,3},{2,0},{3,1},{4,6},{5,7},{6,4},{7,5},{8,10},{9,11},{10,... | collective-permute-start | bytes 196616 | tf_op jit(solution)/shard_map/ppermute | solution.py:78
  28.7 1.0 %collective-permute-start.12 = (bf16[32,1024]{1,0:T(8,128)(2,1)S(1)}, bf16[32,1024]{1,0:T(8,128)(2,1)S(1)}, u32[]{:S(2)}, u32[]{:S(2)}) collective-permute-start(bf16[32,1024]{1,0:T(8,128)(2,1)S(1)} %get-tuple-element.49), channel_id=1, source_target_pairs={{0,4},{1,5},{2,6},{3,7},{4,0},{5,1},{6,2},{7,3},{8,12},{9,13},{10,... | collective-permute-start | bytes 196616 | tf_op jit(solution)/shard_map/ppermute | solution.py:78
  29.6 1.4 %collective-permute-start.13 = (bf16[32,1024]{1,0:T(8,128)(2,1)S(1)}, bf16[32,1024]{1,0:T(8,128)(2,1)S(1)}, u32[]{:S(2)}, u32[]{:S(2)}) collective-permute-start(bf16[32,1024]{1,0:T(8,128)(2,1)S(1)} %get-tuple-element.50), channel_id=1, source_target_pairs={{0,6},{1,7},{2,4},{3,5},{4,2},{5,3},{6,0},{7,1},{8,14},{9,15},{10,... | collective-permute-start | bytes 196616 | tf_op jit(solution)/shard_map/ppermute | solution.py:78
  31.1 0.0 collective-permute-done.6.refs_1_
  31.1 0.1 pieces.2
  31.1 0.0 copy-start
  31.1 1.2 %collective-permute-start.7 = (bf16[32,1024]{1,0:T(8,128)(2,1)S(1)}, bf16[32,1024]{1,0:T(8,128)(2,1)S(1)}, u32[]{:S(2)}, u32[]{:S(2)}) collective-permute-start(bf16[32,1024]{1,0:T(8,128)(2,1)S(1)} %get-tuple-element.42), channel_id=1, source_target_pairs={{0,2},{1,3},{2,0},{3,1},{4,6},{5,7},{6,4},{7,5},{8,10},{9,11},{10,... | collective-permute-start | bytes 196616 | tf_op jit(solution)/shard_map/ppermute | solution.py:78
  32.3 1.0 %collective-permute-start.8 = (bf16[32,1024]{1,0:T(8,128)(2,1)S(1)}, bf16[32,1024]{1,0:T(8,128)(2,1)S(1)}, u32[]{:S(2)}, u32[]{:S(2)}) collective-permute-start(bf16[32,1024]{1,0:T(8,128)(2,1)S(1)} %get-tuple-element.43), channel_id=1, source_target_pairs={{0,4},{1,5},{2,6},{3,7},{4,0},{5,1},{6,2},{7,3},{8,12},{9,13},{10,... | collective-permute-start | bytes 196616 | tf_op jit(solution)/shard_map/ppermute | solution.py:78
  33.3 0.0 collective-permute-done.11.refs_1_
  33.3 1.4 %collective-permute-start.9 = (bf16[32,1024]{1,0:T(8,128)(2,1)S(1)}, bf16[32,1024]{1,0:T(8,128)(2,1)S(1)}, u32[]{:S(2)}, u32[]{:S(2)}) collective-permute-start(bf16[32,1024]{1,0:T(8,128)(2,1)S(1)} %get-tuple-element.44), channel_id=1, source_target_pairs={{0,6},{1,7},{2,4},{3,5},{4,2},{5,3},{6,0},{7,1},{8,14},{9,15},{10,... | collective-permute-start | bytes 196616 | tf_op jit(solution)/shard_map/ppermute | solution.py:78
  34.7 0.3 collective-permute-done.13.refs_3_
  35.1 3.7 %collective-permute-start.19 = (bf16[32,1024]{1,0:T(8,128)(2,1)S(1)}, bf16[32,1024]{1,0:T(8,128)(2,1)S(1)}, u32[]{:S(2)}, u32[]{:S(2)}) collective-permute-start(bf16[32,1024]{1,0:T(8,128)(2,1)S(1)} %add_pieces.3.refs_1_.refs_0_), channel_id=1, source_target_pairs={{0,24},{8,16},{16,8},{24,0},{1,25},{9,17},{17,9},{25,1},{2,26},{10... | collective-permute-start | bytes 196616 | tf_op jit(solution)/shard_map/ppermute | solution.py:78
  38.8 0.0 collective-permute-done.7.refs_1_.refs_4_
  38.8 0.7 %collective-permute-start.17 = (bf16[32,1024]{1,0:T(8,128)(2,1)S(1)}, bf16[32,1024]{1,0:T(8,128)(2,1)S(1)}, u32[]{:S(2)}, u32[]{:S(2)}) collective-permute-start(bf16[32,1024]{1,0:T(8,128)(2,1)S(1)} %add_pieces.3.refs_1_.refs_0_), channel_id=1, source_target_pairs={{0,8},{8,0},{16,24},{24,16},{1,9},{9,1},{17,25},{25,17},{2,10},{10... | collective-permute-start | bytes 196616 | tf_op jit(solution)/shard_map/ppermute | solution.py:78
  39.5 0.0 collective-permute-done.8.refs_2_.refs_5_
  39.5 1.5 %collective-permute-start.16 = (bf16[32,1024]{1,0:T(8,128)(2,1)S(1)}, bf16[32,1024]{1,0:T(8,128)(2,1)S(1)}, u32[]{:S(2)}, u32[]{:S(2)}) collective-permute-start(bf16[32,1024]{1,0:T(8,128)(2,1)S(1)} %add_pieces.3.refs_1_.refs_0_), channel_id=1, source_target_pairs={{0,6},{1,7},{2,4},{3,5},{4,2},{5,3},{6,0},{7,1},{8,14},{9,15},{10,... | collective-permute-start | bytes 196616 | tf_op jit(solution)/shard_map/ppermute | solution.py:78
  41.0 0.0 collective-permute-done.9.refs_3_.refs_6_
  41.0 1.0 %collective-permute-start.15 = (bf16[32,1024]{1,0:T(8,128)(2,1)S(1)}, bf16[32,1024]{1,0:T(8,128)(2,1)S(1)}, u32[]{:S(2)}, u32[]{:S(2)}) collective-permute-start(bf16[32,1024]{1,0:T(8,128)(2,1)S(1)} %add_pieces.3.refs_1_.refs_0_), channel_id=1, source_target_pairs={{0,4},{1,5},{2,6},{3,7},{4,0},{5,1},{6,2},{7,3},{8,12},{9,13},{10,... | collective-permute-start | bytes 196616 | tf_op jit(solution)/shard_map/ppermute | solution.py:78
  42.0 1.0 %collective-permute-start.14 = (bf16[32,1024]{1,0:T(8,128)(2,1)S(1)}, bf16[32,1024]{1,0:T(8,128)(2,1)S(1)}, u32[]{:S(2)}, u32[]{:S(2)}) collective-permute-start(bf16[32,1024]{1,0:T(8,128)(2,1)S(1)} %add_pieces.3.refs_1_.refs_0_), channel_id=1, source_target_pairs={{0,2},{1,3},{2,0},{3,1},{4,6},{5,7},{6,4},{7,5},{8,10},{9,11},{10,... | collective-permute-start | bytes 196616 | tf_op jit(solution)/shard_map/ppermute | solution.py:78
  43.0 1.7 %collective-permute-done.18.refs_1_ = bf16[32,1024]{1,0:T(8,128)(2,1)S(1)} collective-permute-done((bf16[32,1024]{1,0:T(8,128)(2,1)S(1)}, bf16[32,1024]{1,0:T(8,128)(2,1)S(1)}, u32[]{:S(2)}, u32[]{:S(2)}) %collective-permute-start.18) | collective-permute-done | bytes 65568 | tf_op jit(solution)/shard_map/ppermute | solution.py:78
  44.8 0.7 %collective-permute-start.27 = (bf16[96,1024]{1,0:T(8,128)(2,1)S(1)}, bf16[96,1024]{1,0:T(8,128)(2,1)S(1)}, u32[]{:S(2)}, u32[]{:S(2)}) collective-permute-start(bf16[96,1024]{1,0:T(8,128)(2,1)S(1)} %stack.2.refs_4_), channel_id=1, source_target_pairs={{0,6},{1,7},{2,4},{3,5},{4,2},{5,3},{6,0},{7,1},{8,14},{9,15},{10,... | collective-permute-start | bytes 589832 | tf_op jit(solution)/shard_map/ppermute | solution.py:78
  45.5 1.4 %collective-permute-start.25 = (bf16[96,1024]{1,0:T(8,128)(2,1)S(1)}, bf16[96,1024]{1,0:T(8,128)(2,1)S(1)}, u32[]{:S(2)}, u32[]{:S(2)}) collective-permute-start(bf16[96,1024]{1,0:T(8,128)(2,1)S(1)} %stack.2.refs_4_), channel_id=1, source_target_pairs={{0,4},{1,5},{2,6},{3,7},{4,0},{5,1},{6,2},{7,3},{8,12},{9,13},{10,... | collective-permute-start | bytes 589832 | tf_op jit(solution)/shard_map/ppermute | solution.py:78
  46.9 0.0 collective-permute-done.16.refs_3_
  46.9 1.5 %collective-permute-start.23 = (bf16[96,1024]{1,0:T(8,128)(2,1)S(1)}, bf16[96,1024]{1,0:T(8,128)(2,1)S(1)}, u32[]{:S(2)}, u32[]{:S(2)}) collective-permute-start(bf16[96,1024]{1,0:T(8,128)(2,1)S(1)} %stack.2.refs_4_), channel_id=1, source_target_pairs={{0,2},{1,3},{2,0},{3,1},{4,6},{5,7},{6,4},{7,5},{8,10},{9,11},{10,... | collective-permute-start | bytes 589832 | tf_op jit(solution)/shard_map/ppermute | solution.py:78
  48.3 0.0 collective-permute-done.15.refs_2_
  48.3 0.0 collective-permute-done.14.refs_1_
  48.4 0.1 collective-permute-start.20
  48.5 0.5 collective-permute-start.21
  49.0 0.8 %collective-permute-done.20 = bf16[64,1024]{1,0:T(8,128)(2,1)S(1)} collective-permute-done((bf16[64,1024]{1,0:T(8,128)(2,1)S(1)}, bf16[64,1024]{1,0:T(8,128)(2,1)S(1)}, u32[]{:S(2)}, u32[]{:S(2)}) %collective-permute-start.20) | collective-permute-done | bytes 131104 | tf_op jit(solution)/shard_map/ppermute | solution.py:78
  49.8 0.1 collective-permute-start.22
  49.9 3.5 %collective-permute-done.27.refs_10_ = bf16[96,1024]{1,0:T(8,128)(2,1)S(1)} collective-permute-done((bf16[96,1024]{1,0:T(8,128)(2,1)S(1)}, bf16[96,1024]{1,0:T(8,128)(2,1)S(1)}, u32[]{:S(2)}, u32[]{:S(2)}) %collective-permute-start.27) | collective-permute-done | bytes 196640 | tf_op jit(solution)/shard_map/ppermute | solution.py:78
  53.5 0.0 collective-permute-start.28
  53.5 1.7 %collective-permute-done.25.refs_8_ = bf16[96,1024]{1,0:T(8,128)(2,1)S(1)} collective-permute-done((bf16[96,1024]{1,0:T(8,128)(2,1)S(1)}, bf16[96,1024]{1,0:T(8,128)(2,1)S(1)}, u32[]{:S(2)}, u32[]{:S(2)}) %collective-permute-start.25) | collective-permute-done | bytes 196640 | tf_op jit(solution)/shard_map/ppermute | solution.py:78
  55.2 0.5 collective-permute-start.24
  55.7 0.1 arrange.1.refs_0_
  55.8 0.7 %add_pieces.2 = bf16[32,1024]{1,0:T(8,128)(2,1)} custom-call(bf16[32,1024]{1,0:T(8,128)(2,1)S(1)} %get-tuple-element.41.refs_0_, bf16[32,1024]{1,0:T(8,128)(2,1)S(1)} %collective-permute-done.7.refs_1_.refs_4_, bf16[32,1024]{1,0:T(8,128)(2,1)S(1)} %collective-permute-done.8.refs_2_.refs_5_, bf16[32,1024]{1,0:T(8,128)(2,1)S(1)} %collective-permute-done.9.refs_3_.refs_6_), custom_call_target="tpu_custom_call" | custom-call | bytes 1048576 | tf_op jit(solution)/shard_map/add_pieces/pallas_call | solution.py:40
  56.5 0.0 collective-permute-done.28.refs_11_
  56.5 0.1 collective-permute-done.26.refs_9_
  56.6 0.3 collective-permute-done.24.refs_7_
  56.9 2.4 %finish.1 = (bf16[256,512]{1,0:T(8,128)(2,1)}, f32[512,1024]{1,0:T(8,128)}) custom-call(bf16[1024,512]{1,0:T(8,128)(2,1)S(1)} %arrange.1.refs_0_, bf16[128,1024]{1,0:T(8,128)(2,1)S(1)} %stack.3.refs_1_, bf16[128,1024]{1,0:T(8,128)(2,1)S(1)} %pad_maximum_fusion.refs_2_, bf16[512,1024]{1,0:T(8,128)(2,1)S(1)} %copy-done, bf16[96,1024]{1,0:T(8,128)(2,1)S(1)} %stack.2.refs_4_, ...), custom_call_target="tpu_custom_call" | custom-call | flops 1073741824 | bytes 4194304 | tf_op jit(solution)/shard_map/finish/pallas_call | solution.py:383
  (17 shorter events, 0.1 us)
Async XLA Ops:
  2.6 1.7 %collective-permute-start = (bf16[128,1024]{1,0:T(8,128)(2,1)S(1)}, bf16[128,1024]{1,0:T(8,128)(2,1)S(1)}, u32[]{:S(2)}, u32[]{:S(2)}) collective-permute-start(bf16[128,1024]{1,0:T(8,128)(2,1)S(1)} %get-tuple-element.30), channel_id=1, source_target_pairs={{0,1},{1,0},{2,3},{3,2},{4,5},{5,4},{6,7},{7,6},{8,9},{9,8},{10,11... | collective-permute-start | bytes 786440 | tf_op jit(solution)/shard_map/ppermute | solution.py:78
  4.3 9.3 %collective-permute-start.1 = (bf16[96,1024]{1,0:T(8,128)(2,1)S(1)}, bf16[96,1024]{1,0:T(8,128)(2,1)S(1)}, u32[]{:S(2)}, u32[]{:S(2)}) collective-permute-start(bf16[96,1024]{1,0:T(8,128)(2,1)S(1)} %get-tuple-element.32.refs_0_), channel_id=1, source_target_pairs={{0,2},{1,3},{2,0},{3,1},{4,6},{5,7},{6,4},{7,5},{8,10},{9,11},{10,... | collective-permute-start | bytes 589832 | tf_op jit(solution)/shard_map/ppermute | solution.py:78
  7.3 6.4 %collective-permute-start.2 = (bf16[80,1024]{1,0:T(8,128)(2,1)S(1)}, bf16[80,1024]{1,0:T(8,128)(2,1)S(1)}, u32[]{:S(2)}, u32[]{:S(2)}) collective-permute-start(bf16[80,1024]{1,0:T(8,128)(2,1)S(1)} %get-tuple-element.33.refs_1_), channel_id=1, source_target_pairs={{0,4},{1,5},{2,6},{3,7},{4,0},{5,1},{6,2},{7,3},{8,12},{9,13},{10,... | collective-permute-start | bytes 491528 | tf_op jit(solution)/shard_map/ppermute | solution.py:78
  8.8 34.3 %all-to-all-start = ((bf16[4,256,512]{2,1,0:T(8,128)(2,1)}), bf16[4,256,512]{2,1,0:T(8,128)(2,1)S(1)}, u32[]{:S(2)}, u32[]{:S(2)}) async-start(bf16[4,256,512]{2,1,0:T(8,128)(2,1)} %spread.1.refs_3_), calls=%async_computation | async-start | bytes 2097152 | tf_op jit(solution)/shard_map/all_to_all | solution.py:422
  13.7 6.9 %collective-permute-start.3 = (bf16[112,1024]{1,0:T(8,128)(2,1)S(1)}, bf16[112,1024]{1,0:T(8,128)(2,1)S(1)}, u32[]{:S(2)}, u32[]{:S(2)}) collective-permute-start(bf16[112,1024]{1,0:T(8,128)(2,1)S(1)} %get-tuple-element.34.refs_0_), channel_id=1, source_target_pairs={{0,4},{1,5},{2,6},{3,7},{4,0},{5,1},{6,2},{7,3},{8,12},{9,13},{10,... | collective-permute-start | bytes 688136 | tf_op jit(solution)/shard_map/ppermute | solution.py:78
  14.9 5.7 %collective-permute-start.4 = (bf16[96,1024]{1,0:T(8,128)(2,1)S(1)}, bf16[96,1024]{1,0:T(8,128)(2,1)S(1)}, u32[]{:S(2)}, u32[]{:S(2)}) collective-permute-start(bf16[96,1024]{1,0:T(8,128)(2,1)S(1)} %get-tuple-element.35.refs_1_), channel_id=1, source_target_pairs={{0,2},{1,3},{2,0},{3,1},{4,6},{5,7},{6,4},{7,5},{8,10},{9,11},{10,... | collective-permute-start | bytes 589832 | tf_op jit(solution)/shard_map/ppermute | solution.py:78
  20.7 2.0 %collective-permute-start.5 = (bf16[272,1024]{1,0:T(8,128)(2,1)S(1)}, bf16[272,1024]{1,0:T(8,128)(2,1)S(1)}, u32[]{:S(2)}, u32[]{:S(2)}) collective-permute-start(bf16[272,1024]{1,0:T(8,128)(2,1)S(1)} %settle.1.refs_0_.refs_1_), channel_id=1, source_target_pairs={{0,1},{1,0},{2,3},{3,2},{4,5},{5,4},{6,7},{7,6},{8,9},{9,8},{10,11... | collective-permute-start | bytes 1671176 | tf_op jit(solution)/shard_map/ppermute | solution.py:78
  25.8 1.6 %collective-permute-start.10 = (bf16[128,1024]{1,0:T(8,128)(2,1)S(1)}, bf16[128,1024]{1,0:T(8,128)(2,1)S(1)}, u32[]{:S(2)}, u32[]{:S(2)}) collective-permute-start(bf16[128,1024]{1,0:T(8,128)(2,1)S(1)} %get-tuple-element.46), channel_id=1, source_target_pairs={{0,1},{1,0},{2,3},{3,2},{4,5},{5,4},{6,7},{7,6},{8,9},{9,8},{10,11... | collective-permute-start | bytes 786440 | tf_op jit(solution)/shard_map/ppermute | solution.py:78
  27.0 4.1 %collective-permute-start.6 = (bf16[128,1024]{1,0:T(8,128)(2,1)S(1)}, bf16[128,1024]{1,0:T(8,128)(2,1)S(1)}, u32[]{:S(2)}, u32[]{:S(2)}) collective-permute-start(bf16[128,1024]{1,0:T(8,128)(2,1)S(1)} %get-tuple-element.40), channel_id=1, source_target_pairs={{0,1},{1,0},{2,3},{3,2},{4,5},{5,4},{6,7},{7,6},{8,9},{9,8},{10,11... | collective-permute-start | bytes 786440 | tf_op jit(solution)/shard_map/ppermute | solution.py:78
  27.5 5.8 %collective-permute-start.11 = (bf16[32,1024]{1,0:T(8,128)(2,1)S(1)}, bf16[32,1024]{1,0:T(8,128)(2,1)S(1)}, u32[]{:S(2)}, u32[]{:S(2)}) collective-permute-start(bf16[32,1024]{1,0:T(8,128)(2,1)S(1)} %get-tuple-element.48), channel_id=1, source_target_pairs={{0,2},{1,3},{2,0},{3,1},{4,6},{5,7},{6,4},{7,5},{8,10},{9,11},{10,... | collective-permute-start | bytes 196616 | tf_op jit(solution)/shard_map/ppermute | solution.py:78
  28.7 6.0 %collective-permute-start.12 = (bf16[32,1024]{1,0:T(8,128)(2,1)S(1)}, bf16[32,1024]{1,0:T(8,128)(2,1)S(1)}, u32[]{:S(2)}, u32[]{:S(2)}) collective-permute-start(bf16[32,1024]{1,0:T(8,128)(2,1)S(1)} %get-tuple-element.49), channel_id=1, source_target_pairs={{0,4},{1,5},{2,6},{3,7},{4,0},{5,1},{6,2},{7,3},{8,12},{9,13},{10,... | collective-permute-start | bytes 196616 | tf_op jit(solution)/shard_map/ppermute | solution.py:78
  29.6 5.4 %collective-permute-start.13 = (bf16[32,1024]{1,0:T(8,128)(2,1)S(1)}, bf16[32,1024]{1,0:T(8,128)(2,1)S(1)}, u32[]{:S(2)}, u32[]{:S(2)}) collective-permute-start(bf16[32,1024]{1,0:T(8,128)(2,1)S(1)} %get-tuple-element.50), channel_id=1, source_target_pairs={{0,6},{1,7},{2,4},{3,5},{4,2},{5,3},{6,0},{7,1},{8,14},{9,15},{10,... | collective-permute-start | bytes 196616 | tf_op jit(solution)/shard_map/ppermute | solution.py:78
  31.1 25.8 %copy-start = (bf16[512,1024]{1,0:T(8,128)(2,1)S(1)}, bf16[512,1024]{1,0:T(8,128)(2,1)}, u32[]{:S(2)}) copy-start(bf16[512,1024]{1,0:T(8,128)(2,1)} %refs_3_.1) | copy-start | bytes 3145732
  31.1 7.7 %collective-permute-start.7 = (bf16[32,1024]{1,0:T(8,128)(2,1)S(1)}, bf16[32,1024]{1,0:T(8,128)(2,1)S(1)}, u32[]{:S(2)}, u32[]{:S(2)}) collective-permute-start(bf16[32,1024]{1,0:T(8,128)(2,1)S(1)} %get-tuple-element.42), channel_id=1, source_target_pairs={{0,2},{1,3},{2,0},{3,1},{4,6},{5,7},{6,4},{7,5},{8,10},{9,11},{10,... | collective-permute-start | bytes 196616 | tf_op jit(solution)/shard_map/ppermute | solution.py:78
  32.3 7.2 %collective-permute-start.8 = (bf16[32,1024]{1,0:T(8,128)(2,1)S(1)}, bf16[32,1024]{1,0:T(8,128)(2,1)S(1)}, u32[]{:S(2)}, u32[]{:S(2)}) collective-permute-start(bf16[32,1024]{1,0:T(8,128)(2,1)S(1)} %get-tuple-element.43), channel_id=1, source_target_pairs={{0,4},{1,5},{2,6},{3,7},{4,0},{5,1},{6,2},{7,3},{8,12},{9,13},{10,... | collective-permute-start | bytes 196616 | tf_op jit(solution)/shard_map/ppermute | solution.py:78
  33.3 7.8 %collective-permute-start.9 = (bf16[32,1024]{1,0:T(8,128)(2,1)S(1)}, bf16[32,1024]{1,0:T(8,128)(2,1)S(1)}, u32[]{:S(2)}, u32[]{:S(2)}) collective-permute-start(bf16[32,1024]{1,0:T(8,128)(2,1)S(1)} %get-tuple-element.44), channel_id=1, source_target_pairs={{0,6},{1,7},{2,4},{3,5},{4,2},{5,3},{6,0},{7,1},{8,14},{9,15},{10,... | collective-permute-start | bytes 196616 | tf_op jit(solution)/shard_map/ppermute | solution.py:78
  35.1 6.9 %collective-permute-start.19 = (bf16[32,1024]{1,0:T(8,128)(2,1)S(1)}, bf16[32,1024]{1,0:T(8,128)(2,1)S(1)}, u32[]{:S(2)}, u32[]{:S(2)}) collective-permute-start(bf16[32,1024]{1,0:T(8,128)(2,1)S(1)} %add_pieces.3.refs_1_.refs_0_), channel_id=1, source_target_pairs={{0,24},{8,16},{16,8},{24,0},{1,25},{9,17},{17,9},{25,1},{2,26},{10... | collective-permute-start | bytes 196616 | tf_op jit(solution)/shard_map/ppermute | solution.py:78
  38.8 6.0 %collective-permute-start.18 = (bf16[32,1024]{1,0:T(8,128)(2,1)S(1)}, bf16[32,1024]{1,0:T(8,128)(2,1)S(1)}, u32[]{:S(2)}, u32[]{:S(2)}) collective-permute-start(bf16[32,1024]{1,0:T(8,128)(2,1)S(1)} %add_pieces.3.refs_1_.refs_0_), channel_id=1, source_target_pairs={{0,16},{8,24},{16,0},{24,8},{1,17},{9,25},{17,1},{25,9},{2,18},{10... | collective-permute-start | bytes 196616 | tf_op jit(solution)/shard_map/ppermute | solution.py:78
  38.8 6.0 %collective-permute-start.17 = (bf16[32,1024]{1,0:T(8,128)(2,1)S(1)}, bf16[32,1024]{1,0:T(8,128)(2,1)S(1)}, u32[]{:S(2)}, u32[]{:S(2)}) collective-permute-start(bf16[32,1024]{1,0:T(8,128)(2,1)S(1)} %add_pieces.3.refs_1_.refs_0_), channel_id=1, source_target_pairs={{0,8},{8,0},{16,24},{24,16},{1,9},{9,1},{17,25},{25,17},{2,10},{10... | collective-permute-start | bytes 196616 | tf_op jit(solution)/shard_map/ppermute | solution.py:78
  39.5 7.3 %collective-permute-start.16 = (bf16[32,1024]{1,0:T(8,128)(2,1)S(1)}, bf16[32,1024]{1,0:T(8,128)(2,1)S(1)}, u32[]{:S(2)}, u32[]{:S(2)}) collective-permute-start(bf16[32,1024]{1,0:T(8,128)(2,1)S(1)} %add_pieces.3.refs_1_.refs_0_), channel_id=1, source_target_pairs={{0,6},{1,7},{2,4},{3,5},{4,2},{5,3},{6,0},{7,1},{8,14},{9,15},{10,... | collective-permute-start | bytes 196616 | tf_op jit(solution)/shard_map/ppermute | solution.py:78
  41.0 7.3 %collective-permute-start.15 = (bf16[32,1024]{1,0:T(8,128)(2,1)S(1)}, bf16[32,1024]{1,0:T(8,128)(2,1)S(1)}, u32[]{:S(2)}, u32[]{:S(2)}) collective-permute-start(bf16[32,1024]{1,0:T(8,128)(2,1)S(1)} %add_pieces.3.refs_1_.refs_0_), channel_id=1, source_target_pairs={{0,4},{1,5},{2,6},{3,7},{4,0},{5,1},{6,2},{7,3},{8,12},{9,13},{10,... | collective-permute-start | bytes 196616 | tf_op jit(solution)/shard_map/ppermute | solution.py:78
  42.0 6.3 %collective-permute-start.14 = (bf16[32,1024]{1,0:T(8,128)(2,1)S(1)}, bf16[32,1024]{1,0:T(8,128)(2,1)S(1)}, u32[]{:S(2)}, u32[]{:S(2)}) collective-permute-start(bf16[32,1024]{1,0:T(8,128)(2,1)S(1)} %add_pieces.3.refs_1_.refs_0_), channel_id=1, source_target_pairs={{0,2},{1,3},{2,0},{3,1},{4,6},{5,7},{6,4},{7,5},{8,10},{9,11},{10,... | collective-permute-start | bytes 196616 | tf_op jit(solution)/shard_map/ppermute | solution.py:78
  44.8 8.7 %collective-permute-start.27 = (bf16[96,1024]{1,0:T(8,128)(2,1)S(1)}, bf16[96,1024]{1,0:T(8,128)(2,1)S(1)}, u32[]{:S(2)}, u32[]{:S(2)}) collective-permute-start(bf16[96,1024]{1,0:T(8,128)(2,1)S(1)} %stack.2.refs_4_), channel_id=1, source_target_pairs={{0,6},{1,7},{2,4},{3,5},{4,2},{5,3},{6,0},{7,1},{8,14},{9,15},{10,... | collective-permute-start | bytes 589832 | tf_op jit(solution)/shard_map/ppermute | solution.py:78
  45.5 9.7 %collective-permute-start.25 = (bf16[96,1024]{1,0:T(8,128)(2,1)S(1)}, bf16[96,1024]{1,0:T(8,128)(2,1)S(1)}, u32[]{:S(2)}, u32[]{:S(2)}) collective-permute-start(bf16[96,1024]{1,0:T(8,128)(2,1)S(1)} %stack.2.refs_4_), channel_id=1, source_target_pairs={{0,4},{1,5},{2,6},{3,7},{4,0},{5,1},{6,2},{7,3},{8,12},{9,13},{10,... | collective-permute-start | bytes 589832 | tf_op jit(solution)/shard_map/ppermute | solution.py:78
  46.9 8.3 %collective-permute-start.23 = (bf16[96,1024]{1,0:T(8,128)(2,1)S(1)}, bf16[96,1024]{1,0:T(8,128)(2,1)S(1)}, u32[]{:S(2)}, u32[]{:S(2)}) collective-permute-start(bf16[96,1024]{1,0:T(8,128)(2,1)S(1)} %stack.2.refs_4_), channel_id=1, source_target_pairs={{0,2},{1,3},{2,0},{3,1},{4,6},{5,7},{6,4},{7,5},{8,10},{9,11},{10,... | collective-permute-start | bytes 589832 | tf_op jit(solution)/shard_map/ppermute | solution.py:78
  48.4 1.4 %collective-permute-start.20 = (bf16[64,1024]{1,0:T(8,128)(2,1)S(1)}, bf16[64,1024]{1,0:T(8,128)(2,1)S(1)}, u32[]{:S(2)}, u32[]{:S(2)}) collective-permute-start(bf16[64,1024]{1,0:T(8,128)(2,1)S(1)} %get-tuple-element.53), channel_id=1, source_target_pairs={{0,1},{1,0},{2,3},{3,2},{4,5},{5,4},{6,7},{7,6},{8,9},{9,8},{10,11... | collective-permute-start | bytes 393224 | tf_op jit(solution)/shard_map/ppermute | solution.py:78
  48.5 8.0 %collective-permute-start.21 = (bf16[64,1024]{1,0:T(8,128)(2,1)S(1)}, bf16[64,1024]{1,0:T(8,128)(2,1)S(1)}, u32[]{:S(2)}, u32[]{:S(2)}) collective-permute-start(bf16[64,1024]{1,0:T(8,128)(2,1)S(1)} %get-tuple-element.54), channel_id=1, source_target_pairs={{0,1},{1,0},{2,3},{3,2},{4,5},{5,4},{6,7},{7,6},{8,9},{9,8},{10,11... | collective-permute-start | bytes 393224 | tf_op jit(solution)/shard_map/ppermute | solution.py:78
  49.8 6.7 %collective-permute-start.22 = (bf16[96,1024]{1,0:T(8,128)(2,1)S(1)}, bf16[96,1024]{1,0:T(8,128)(2,1)S(1)}, u32[]{:S(2)}, u32[]{:S(2)}) collective-permute-start(bf16[96,1024]{1,0:T(8,128)(2,1)S(1)} %stack.2.refs_4_), channel_id=1, source_target_pairs={{0,1},{1,0},{2,3},{3,2},{4,5},{5,4},{6,7},{7,6},{8,9},{9,8},{10,11... | collective-permute-start | bytes 589832 | tf_op jit(solution)/shard_map/ppermute | solution.py:78
  53.5 3.0 %collective-permute-start.28 = (bf16[96,1024]{1,0:T(8,128)(2,1)S(1)}, bf16[96,1024]{1,0:T(8,128)(2,1)S(1)}, u32[]{:S(2)}, u32[]{:S(2)}) collective-permute-start(bf16[96,1024]{1,0:T(8,128)(2,1)S(1)} %collective-permute-done.27.refs_10_), channel_id=1, source_target_pairs={{0,1},{1,0},{2,3},{3,2},{4,5},{5,4},{6,7},{7,6},{8,9},{9,8},{10,11... | collective-permute-start | bytes 589832 | tf_op jit(solution)/shard_map/ppermute | solution.py:78
  55.2 1.4 %collective-permute-start.26 = (bf16[96,1024]{1,0:T(8,128)(2,1)S(1)}, bf16[96,1024]{1,0:T(8,128)(2,1)S(1)}, u32[]{:S(2)}, u32[]{:S(2)}) collective-permute-start(bf16[96,1024]{1,0:T(8,128)(2,1)S(1)} %collective-permute-done.25.refs_8_), channel_id=1, source_target_pairs={{0,1},{1,0},{2,3},{3,2},{4,5},{5,4},{6,7},{7,6},{8,9},{9,8},{10,11... | collective-permute-start | bytes 589832 | tf_op jit(solution)/shard_map/ppermute | solution.py:78
  55.2 1.7 %collective-permute-start.24 = (bf16[96,1024]{1,0:T(8,128)(2,1)S(1)}, bf16[96,1024]{1,0:T(8,128)(2,1)S(1)}, u32[]{:S(2)}, u32[]{:S(2)}) collective-permute-start(bf16[96,1024]{1,0:T(8,128)(2,1)S(1)} %collective-permute-done.23.refs_6_), channel_id=1, source_target_pairs={{0,1},{1,0},{2,3},{3,2},{4,5},{5,4},{6,7},{7,6},{8,9},{9,8},{10,11... | collective-permute-start | bytes 589832 | tf_op jit(solution)/shard_map/ppermute | solution.py:78
